TPU v7x, 32 devices: a whole 2x2x4 slice. The times are simulated.
32 devices in a mesh: row: 4 (over z), col: 8 (over y, x, core).
Axes of the slice: x: 2, y: 2, z: 4, core: 2. Of those that a mesh axis runs over, the one named last changes fastest.
Arguments:
- activations: bfloat16 [1024, 5120], P('row', 'col'), may hold values from -6 to 6
- up_weight: bfloat16 [5120, 6912], P('row', 'col'), may hold values from -0.078125 to 0.078125
- hidden_cot: bfloat16 [1024, 6912], P('row', 'col'), may hold values from -6 to 6
Outputs:
- hidden: bfloat16 [1024, 6912], P('row', 'col')
- input_grad: bfloat16 [1024, 5120], P(('row', 'col'))
- weight_grad: float32 [5120, 6912], P('row', 'col')
All inputs are finite; a program needn't handle non-finite values.
Results may differ from a plain program's by a relative error of at most 0.022.
Values may be sent and summed in bfloat16 or wider, within the bound.
No kernel may reach another device: no remote copies, remote signals or barrier semaphores. Data moves between devices by JAX's collectives and lax.ppermute only.
A program may use at most 64 MiB of HBM per device.

v0:
```python
import jax
import jax.numpy as jnp
from jax import lax
from jax.sharding import PartitionSpec as P

grad_scale = 0.015625


def gelu_tanh(value):
    return 0.5 * value * (1.0 + jnp.tanh(0.7978845608 * (value + 0.044715 * value * value * value)))


def on_device(activations, up_weight, hidden_cot):
    tok_rows = activations.shape[0]
    whole_x = lax.all_gather(activations, "col", axis=1, tiled=True)
    panel = lax.all_gather(up_weight, "row", axis=0, tiled=True)
    pre = jnp.dot(whole_x, panel, preferred_element_type=jnp.float32)
    hidden = gelu_tanh(pre).astype(jnp.bfloat16)
    _, pull = jax.vjp(gelu_tanh, pre)
    slope = pull(hidden_cot.astype(jnp.float32))[0].astype(jnp.bfloat16)
    partial_in = lax.dot_general(
        slope, panel, (((1,), (1,)), ((), ())), preferred_element_type=jnp.float32
    )
    summed = lax.psum_scatter(
        partial_in.astype(jnp.bfloat16), "col", scatter_dimension=1, tiled=True
    )
    input_grad = lax.all_to_all(summed, "col", split_axis=0, concat_axis=1, tiled=True)
    x_cols = lax.all_to_all(whole_x, "row", split_axis=1, concat_axis=0, tiled=True)
    piece = lax.all_gather(slope, "row", axis=0, tiled=True)
    count = piece.shape[0] // tok_rows
    terms = jnp.einsum(
        "nta,ntf->naf",
        x_cols.reshape(count, tok_rows, x_cols.shape[1]),
        piece.reshape(count, tok_rows, piece.shape[1]),
        preferred_element_type=jnp.float32,
    )
    rounded = lax.optimization_barrier(terms.astype(jnp.bfloat16))
    weight_total = jnp.sum(rounded.astype(jnp.float32), axis=0)
    return (hidden, input_grad, weight_total * grad_scale)


def solution(mesh):
    in_specs = (P("row", "col"), P("row", "col"), P("row", "col"))
    out_specs = (P("row", "col"), P(("row", "col"), None), P("row", "col"))
    return jax.shard_map(
        on_device, mesh=mesh, in_specs=in_specs, out_specs=out_specs, check_vma=False
    )
```

profile of v0, /device:TPU:0, one launch (start us, length us, event | category | flops | bytes accessed | tf_op | source)
XLA Modules:
  0.0 363.7 jit_solution(6300767487821949958)
XLA Ops:
  7.2 0.0 all-gather.4.cloned.1.call-start
  7.2 1.9 copy.12
  9.1 0.0 all-gather.4.cloned.1.call-update
  9.1 0.0 all-gather.6.cloned.1.call-start
  9.2 0.7 all-gather.6.cloned.1.call-update
  9.9 0.0 all-gather.8.cloned.1.call-start
  9.9 33.4 %all-gather.4.cloned.1.call-done = bf16[256,5120]{0,1:T(8,128)(2,1)} async-done(((bf16[256,640]{0,1:T(8,128)(2,1)}), bf16[256,5120]{0,1:T(8,128)(2,1)}) %all-gather.4.cloned.1.call-update) | async-done | bytes 2621456 | tf_op jit(solution)/shard_map/all_gather | solution.py:15
  43.3 0.0 copy-start
  43.3 158.7 %all-gather.6.cloned.1.call-done = bf16[5120,864]{0,1:T(8,128)(2,1)} async-done(((bf16[1280,864]{0,1:T(8,128)(2,1)}), bf16[5120,864]{0,1:T(8,128)(2,1)}) %all-gather.6.cloned.1.call-update) | async-done | bytes 8847376 | tf_op jit(solution)/shard_map/all_gather | solution.py:16
  202.0 8.4 %fusion.8 = (bf16[256,864]{0,1:T(8,128)(2,1)}, bf16[256,864]{0,1:T(8,128)(2,1)}) fusion(bf16[256,864]{0,1:T(8,128)(2,1)} %param.5, bf16[5120,864]{0,1:T(8,128)(2,1)} %all-gather.6.cloned.1.call-done, bf16[256,5120]{0,1:T(8,128)(2,1)} %all-gather.4.cloned.1.call-done), kind=kOutput, calls=%fused_computation.18 | convolution fusion | flops 2270896128 | bytes 12795904 | tf_op jit(solution)/shard_map/dot_general | solution.py:17
  210.4 0.0 all-gather.8.cloned.1.call-update
  210.4 0.0 copy-done
  210.5 0.0 copy-start.1
  210.5 2.6 copy.14
  213.1 3.7 %all-to-all-start.1 = ((bf16[256,4,1280]{2,0,1:T(8,128)(2,1)}), bf16[256,4,1280]{2,0,1:T(8,128)(2,1)S(1)}, u32[]{:S(2)}, u32[]{:S(2)}) async-start(bf16[256,4,1280]{2,0,1:T(8,128)(2,1)} %copy.14), calls=%async_computation.1 | async-start | bytes 5242880 | tf_op jit(solution)/shard_map/all_to_all | solution.py:28
  216.8 0.0 reduce-scatter.4.cloned.1.call-start
  216.8 0.0 copy-done.1
  216.8 7.9 %convolution_convert_fusion.1 = bf16[256,5120]{1,0:T(8,128)(2,1)} fusion(bf16[256,864]{0,1:T(8,128)(2,1)S(1)} %copy-done.1, bf16[5120,864]{0,1:T(8,128)(2,1)} %all-gather.6.cloned.1.call-done), kind=kOutput, calls=%fused_computation.3 | convolution fusion | flops 2266234880 | bytes 11911168 | tf_op jit(solution)/shard_map/dot_general | solution.py:21
  224.7 4.4 %copy.16 = bf16[256,5120]{0,1:T(8,128)(2,1)} copy(bf16[256,5120]{1,0:T(8,128)(2,1)} %convolution_convert_fusion.1) | data formatting | bytes 5242880
  229.1 0.0 reduce-scatter.4.cloned.1.call-update
  229.1 75.8 %all-to-all-done.1 = bf16[256,4,1280]{2,0,1:T(8,128)(2,1)S(1)} async-done(((bf16[256,4,1280]{2,0,1:T(8,128)(2,1)}), bf16[256,4,1280]{2,0,1:T(8,128)(2,1)S(1)}, u32[]{:S(2)}, u32[]{:S(2)}) %all-to-all-start.1) | async-done | bytes 2621472 | tf_op jit(solution)/shard_map/all_to_all | solution.py:28
  304.9 0.0 all-gather.8.cloned.1.call-done
  304.9 4.0 %fusion = bf16[4,1280,864]{1,2,0:T(8,128)(2,1)S(1)} fusion(bf16[256,4,1280]{2,0,1:T(8,128)(2,1)S(1)} %all-to-all-done.1, bf16[108,4,8,256]{3,2,1,0:T(8,128)(2,1)} %bitcast.21), kind=kOutput, calls=%fused_computation.2 | convolution fusion | flops 2269347840 | bytes 13238272 | tf_op jit(solution)/shard_map/nta,ntf->naf/dot_general | solution.py:31
  308.9 3.3 convert_reduce_fusion
  312.1 31.3 %reduce-scatter.4.cloned.1.call-done = bf16[640,256]{1,0:T(8,128)(2,1)} async-done(((bf16[5120,256]{1,0:T(8,128)(2,1)}), bf16[640,256]{1,0:T(8,128)(2,1)}) %reduce-scatter.4.cloned.1.call-update) | async-done | bytes 327696
  343.5 1.9 copy.17
  345.4 3.4 all-to-all-start
  348.8 4.6 %broadcast_multiply_fusion = f32[1280,864]{0,1:T(8,128)} fusion(f32[1280,864]{0,1:T(8,128)} %convert_reduce_fusion), kind=kLoop, calls=%fused_computation.5 | loop fusion | flops 1105920 | bytes 8847360 | tf_op jit(solution)/shard_map/mul | solution.py:39
  353.4 2.9 all-to-all-done
  356.4 0.8 copy.19
Async XLA Ops:
  7.2 36.1 %all-gather.4.cloned.1.call-start = ((), (), s32[]{:S(2)}) async-start(), calls=%async_computation.3 | async-start | bytes 2949120 | tf_op jit(solution)/shard_map/all_gather | solution.py:15
  9.1 192.9 %all-gather.6.cloned.1.call-start = ((), (), s32[]{:S(2)}) async-start(), calls=%async_computation.4 | async-start | bytes 11059200 | tf_op jit(solution)/shard_map/all_gather | solution.py:16
  9.9 295.0 %all-gather.8.cloned.1.call-start = ((), (), s32[]{:S(2)}) async-start(), calls=%async_computation.5 | async-start | bytes 2211840 | tf_op jit(solution)/shard_map/all_gather | solution.py:29
  43.3 167.1 %copy-start = (bf16[256,5120]{0,1:T(8,128)(2,1)S(1)}, bf16[256,5120]{0,1:T(8,128)(2,1)}, u32[]{:S(2)}) copy-start(bf16[256,5120]{0,1:T(8,128)(2,1)} %all-gather.4.cloned.1.call-done) | copy-start | bytes 7864324
  210.5 6.4 %copy-start.1 = (bf16[256,864]{0,1:T(8,128)(2,1)S(1)}, bf16[256,864]{0,1:T(8,128)(2,1)}, u32[]{:S(2)}) copy-start(bf16[256,864]{0,1:T(8,128)(2,1)} %get-tuple-element.3) | copy-start | bytes 1327108
  213.1 91.8 %all-to-all-start.1 = ((bf16[256,4,1280]{2,0,1:T(8,128)(2,1)}), bf16[256,4,1280]{2,0,1:T(8,128)(2,1)S(1)}, u32[]{:S(2)}, u32[]{:S(2)}) async-start(bf16[256,4,1280]{2,0,1:T(8,128)(2,1)} %copy.14), calls=%async_computation.1 | async-start | bytes 5242880 | tf_op jit(solution)/shard_map/all_to_all | solution.py:28
  216.8 126.7 %reduce-scatter.4.cloned.1.call-start = ((), (), s32[]{:S(2)}) async-start(), calls=%async_computation.6 | async-start | bytes 2949120
  345.4 11.0 %all-to-all-start = ((bf16[8,32,640]{2,1,0:T(8,128)(2,1)}), bf16[8,32,640]{2,1,0:T(8,128)(2,1)S(1)}, u32[]{:S(2)}, u32[]{:S(2)}) async-start(bf16[8,32,640]{2,1,0:T(8,128)(2,1)} %bitcast), calls=%async_computation | async-start | bytes 655360 | tf_op jit(solution)/shard_map/all_to_all | solution.py:27
Sparse Core Ops, SparseCore 0:
  10.5 32.8 all-gather.3
  44.9 157.1 all-gather.5
  210.6 80.1 all-gather.7
  293.9 49.5 reduce-scatter.3
where the time goes:
time: 364 us
  waiting for transfers between devices  303 us (83%)
  matrix products  20.2 us (6%)
  between operations  13.8 us (4%)
  local copies, waits for them, and re-layouts  11.5 us (3%)
  other arithmetic  7.9 us (2%)
  starting transfers between devices  7.28 us (2%)
    all_gather x1, waiting for transfers between devices, on_device(): panel = lax.all_gather(up_weight, 'row', axis=0, tiled=True)  159 us
    all_to_all x1, waiting for transfers between devices, on_device(): lax.all_to_all(whole_x, 'row', split_axis=1, concat_axis=0, tiled=True)  75.8 us
    all_gather x1, waiting for transfers between devices, on_device(): whole_x = lax.all_gather(activations, 'col', axis=1, tiled=True)  33.4 us
    unnamed x5, waiting for transfers between devices  32.1 us
    dot_general x1, matrix products, on_device(): pre = jnp.dot(whole_x, panel, preferred_element_type=jnp.float32)  8.38 us
    unnamed x7, local copies, waits for them, and re-layouts  8.15 us
    dot_general x1, matrix products, on_device(): lax.dot_general(slope, panel, (((1,), (1,)), ((), ())), preferred_element...  7.86 us
  transfers between devices with their start and end apart: 6, of which 5 were waited for; matrix products, arithmetic and copies ran while one was open for 7% of the time, Pallas kernels for 0%

commit v1 on v0

v1 whole, which is shorter than its diff:
```python
import jax
import jax.numpy as jnp
from jax import lax
from jax.sharding import PartitionSpec as P

grad_scale = 0.015625
cores = 2
streams = 2


def gelu_tanh(value):
    return 0.5 * value * (1.0 + jnp.tanh(0.7978845608 * (value + 0.044715 * value * value * value)))


def at(array, index, axis=0):
    return lax.dynamic_index_in_dim(array, index, axis, keepdims=False)


def wide(array):
    return array.astype(jnp.float32)


def narrow(array):
    return array.astype(jnp.bfloat16)


def on_device(activations, up_weight, hidden_cot, *, n_row, n_col):
    chips = n_col // cores
    row, col = lax.axis_index("row"), lax.axis_index("col")
    chip, core = col // cores, col % cores
    tok, width = activations.shape
    sub = tok // n_col
    depth, units = up_weight.shape
    per_chip = n_row // chips

    def across(array, flip):
        return lax.ppermute(array, "col", [(i, i ^ flip) for i in range(n_col)])

    def along(array, shift):
        return lax.ppermute(array, "row", [(i, (i + shift) % n_row) for i in range(n_row)])

    def by_core(own, other, axis):
        first = jnp.where(core == 0, own, other)
        second = jnp.where(core == 0, other, own)
        return jnp.stack([first, second], axis)

    halves = activations.reshape(chips, cores, sub, width)
    own = at(halves, core, 1)
    other = across(at(halves, 1 - core, 1), 1)
    pair = by_core(own, other, 2).reshape(chips, sub, cores * width)
    pieces = [at(pair, chip)]
    for e in range(1, chips):
        pieces.append(across(at(pair, chip ^ e), cores * e))
    fan = jnp.stack(pieces).reshape(chips, sub, per_chip, depth)

    def for_plane(plane):
        return at(at(fan, (plane // per_chip) ^ chip), plane % per_chip, 1)

    arrived = [for_plane(row)]
    for k in range(1, n_row):
        arrived.append(along(for_plane((row + k) % n_row), k))

    def gather(blocks):
        held = jnp.stack(blocks)
        laid = jnp.zeros((len(blocks), chips, sub, depth), jnp.bfloat16)
        for e in range(chips):
            piece = held if e == 0 else across(held, cores * e)
            laid = lax.dynamic_update_index_in_dim(laid, piece, chip ^ e, 1)
        return by_core(laid, across(laid, 1), 2).reshape(len(blocks), tok, depth)

    early = gather([arrived[1]])
    late = gather(arrived[2:] + arrived[:1])
    tokens = [late[-1], early[0]] + [late[i] for i in range(n_row - 2)]

    cut = units // streams
    parts = [up_weight[:, i * cut:(i + 1) * cut] for i in range(streams)]

    def term(k, i):
        return lax.dot_general(
            parts[i], tokens[k], (((0,), (1,)), ((), ())), preferred_element_type=jnp.float32
        )

    flow = [narrow(term(1, i)) for i in range(streams)]
    for k in list(range(2, n_row)) + [0]:
        flow = [along(f, 1) for f in flow]
        flow = [wide(f) + term(k, i) for i, f in enumerate(flow)]
        if k:
            flow = [narrow(f) for f in flow]

    cot = hidden_cot.T
    hidden, slopes = [], []
    for i in range(streams):
        hidden.append(narrow(gelu_tanh(flow[i])))
        _, pull = jax.vjp(gelu_tanh, flow[i])
        slopes.append(narrow(pull(wide(cot[i * cut:(i + 1) * cut]))[0]))
    hidden = jnp.concatenate(hidden).T

    ring = [slopes]
    for k in range(1, n_row):
        ring.append([along(s, 1) for s in ring[-1]])
    ring = [jnp.concatenate(s) for s in ring]

    def reduce(blocks):
        terms = [
            lax.dot_general(s, up_weight, (((0,), (1,)), ((), ())), preferred_element_type=jnp.float32)
            for s in blocks
        ]
        laid = narrow(jnp.stack(terms)).reshape(len(blocks), chips, cores, sub, depth)
        got = across(at(laid, 1 - core, 2), 1)
        mixed = narrow(wide(at(laid, core, 2)) + wide(got))
        total = wide(at(mixed, chip, 1))
        for e in range(1, chips):
            total = total + wide(across(at(mixed, chip ^ e, 1), cores * e))
        return narrow(total)

    sums = reduce(ring[:-1])
    last = reduce(ring[-1:])
    grads = [sums[k] for k in range(n_row - 1)] + [last[0]]
    placed = jnp.zeros((n_row, sub, depth), jnp.bfloat16)
    for k in range(n_row):
        block = grads[k] if k == 0 else along(grads[k], n_row - k)
        placed = lax.dynamic_update_index_in_dim(placed, block, (row + k) % n_row, 0)
    input_grad = placed.transpose(1, 0, 2).reshape(sub, n_row * depth)

    weight_grad = lax.dot_general(
        jnp.concatenate(ring, axis=1),
        jnp.concatenate(tokens, axis=0),
        (((1,), (0,)), ((), ())),
        preferred_element_type=jnp.float32,
    )
    return (hidden, input_grad, (weight_grad * grad_scale).T)


def solution(mesh):
    n_row, n_col = mesh.shape["row"], mesh.shape["col"]

    def body(activations, up_weight, hidden_cot):
        return on_device(activations, up_weight, hidden_cot, n_row=n_row, n_col=n_col)

    in_specs = (P("row", "col"), P("row", "col"), P("row", "col"))
    out_specs = (P("row", "col"), P(("row", "col"), None), P("row", "col"))
    return jax.shard_map(body, mesh=mesh, in_specs=in_specs, out_specs=out_specs, check_vma=False)
```

time: 364 us -> 150 us (0.41)
  waiting for transfers between devices: 303 us -> 80.7 us
  starting transfers between devices: 7.28 us -> 32.5 us
  between operations: 13.8 us -> 1.33 us
  matrix products: 20.2 us -> 12 us
    all_gather x3 -> x0, waiting for transfers between devices: 192 us -> none  [the longest x1 159 us: on_device(): panel = lax.all_gather(up_weight, 'row', axis=0, tiled=True)]
    ppermute x0 -> x38, waiting for transfers between devices: none -> 80.7 us  [the longest x18 56.2 us: along(): lax.ppermute(array, 'row', [(i, (i + shift) % n_row) for i in range(n_row)])]
    all_to_all x2 -> x0, waiting for transfers between devices: 78.7 us -> none  [the longest x1 75.8 us: on_device(): lax.all_to_all(whole_x, 'row', split_axis=1, concat_axis=0, tiled=True)]
    ppermute x0 -> x38, starting transfers between devices: none -> 32.5 us  [the longest x20 19.9 us: across(): return lax.ppermute(array, 'col', [(i, i ^ flip) for i in range(n_col)])]
    unnamed x5 -> x0, waiting for transfers between devices: 32.1 us -> none
    dynamic_update_slice x0 -> x11, local copies, waits for them, and re-layouts: none -> 10.3 us  [the longest x4 10.2 us: on_device(): lax.dynamic_update_index_in_dim(placed, block, (row + k) % n_row, 0)]
    dot_general x3 -> x13, matrix products: 20.2 us -> 12 us  [the longest x1 4.55 us: on_device(): lax.dot_general(jnp.concatenate(ring, axis=1), jnp.concatenate(tokens, ax...]
    unnamed x7 -> x36, local copies, waits for them, and re-layouts: 8.15 us -> 0.88 us
  transfers between devices with their start and end apart: 6 -> 38, of which waited for: 5 -> 23; matrix products, arithmetic and copies ran while one was open for 7% -> 13% of each run, Pallas kernels for 0% -> 0%
where the time goes in v1:
time: 150 us; the launch traced here: 149 us
  waiting for transfers between devices  80.7 us (54%)
  starting transfers between devices  32.5 us (22%)
  local copies, waits for them, and re-layouts  14.8 us (10%)
  matrix products  12 us (8%)
  other arithmetic  8.01 us (5%)
    ppermute x18, waiting for transfers between devices, along(): lax.ppermute(array, 'row', [(i, (i + shift) % n_row) for i in range(n_row)])  56.2 us
    ppermute x20, waiting for transfers between devices, across(): return lax.ppermute(array, 'col', [(i, i ^ flip) for i in range(n_col)])  24.5 us
    ppermute x20, starting transfers between devices, across(): return lax.ppermute(array, 'col', [(i, i ^ flip) for i in range(n_col)])  19.9 us
    ppermute x18, starting transfers between devices, along(): lax.ppermute(array, 'row', [(i, (i + shift) % n_row) for i in range(n_row)])  12.6 us
    dynamic_update_slice x4, local copies, waits for them, and re-layouts, on_device(): lax.dynamic_update_index_in_dim(placed, block, (row + k) % n_row, 0)  10.2 us
    dot_general x1, matrix products, on_device(): lax.dot_general(jnp.concatenate(ring, axis=1), jnp.concatenate(tokens, ax...  4.55 us
    convert_element_type x6, other arithmetic, narrow(): return array.astype(jnp.bfloat16)  4.41 us
    dot_general x8, matrix products, term(): lax.dot_general(parts[i], tokens[k], (((0,), (1,)), ((), ())), preferred_...  3.92 us
  transfers between devices with their start and end apart: 38, of which 23 were waited for; matrix products, arithmetic and copies ran while one was open for 13% of the time, Pallas kernels for 0%

profile of v1, /device:TPU:0, one launch (start us, length us, event | category | flops | bytes accessed | tf_op | source)
XLA Modules:
  0.0 149.3 jit_solution(7476179788061416726)
XLA Ops:
  0.7 0.9 dynamic-slice_bitcast_fusion.5
  1.6 0.5 collective-permute-start
  2.1 1.0 collective-permute-done
  3.1 1.0 fusion.54
  4.2 3.9 %collective-permute-start.3 = (bf16[32,1280]{1,0:T(8,128)(2,1)S(1)}, bf16[32,1280]{1,0:T(8,128)(2,1)S(1)}, u32[]{:S(2)}, u32[]{:S(2)}) collective-permute-start(bf16[32,1280]{1,0:T(8,128)(2,1)S(1)} %get-tuple-element.29), channel_id=1, source_target_pairs={{0,6},{1,7},{2,4},{3,5},{4,2},{5,3},{6,0},{7,1},{8,14},{9,15},{10,... | collective-permute-start | bytes 245768 | tf_op jit(solution)/shard_map/ppermute | solution.py:37
  8.1 0.5 collective-permute-start.1
  8.7 2.5 %collective-permute-done.3 = bf16[32,1280]{1,0:T(8,128)(2,1)S(1)} collective-permute-done((bf16[32,1280]{1,0:T(8,128)(2,1)S(1)}, bf16[32,1280]{1,0:T(8,128)(2,1)S(1)}, u32[]{:S(2)}, u32[]{:S(2)}) %collective-permute-start.3) | collective-permute-done | bytes 81952 | tf_op jit(solution)/shard_map/ppermute | solution.py:37
  11.2 1.6 %collective-permute-done.1 = bf16[32,1280]{1,0:T(8,128)(2,1)S(1)} collective-permute-done((bf16[32,1280]{1,0:T(8,128)(2,1)S(1)}, bf16[32,1280]{1,0:T(8,128)(2,1)S(1)}, u32[]{:S(2)}, u32[]{:S(2)}) %collective-permute-start.1) | collective-permute-done | bytes 81952 | tf_op jit(solution)/shard_map/ppermute | solution.py:37
  13.2 1.6 %collective-permute-start.4 = (bf16[32,1280]{1,0:T(8,128)(2,1)S(1)}, bf16[32,1280]{1,0:T(8,128)(2,1)S(1)}, u32[]{:S(2)}, u32[]{:S(2)}) collective-permute-start(bf16[32,1280]{1,0:T(8,128)(2,1)S(1)} %get-tuple-element.24), channel_id=1, source_target_pairs={{0,8},{8,16},{16,24},{24,0},{1,9},{9,17},{17,25},{25,1},{2,10},{10... | collective-permute-start | bytes 245768 | tf_op jit(solution)/shard_map/ppermute | solution.py:40
  14.8 2.6 %collective-permute-start.10 = (bf16[32,1280]{1,0:T(8,128)(2,1)S(1)}, bf16[32,1280]{1,0:T(8,128)(2,1)S(1)}, u32[]{:S(2)}, u32[]{:S(2)}) collective-permute-start(bf16[32,1280]{1,0:T(8,128)(2,1)S(1)} %get-tuple-element.27), channel_id=1, source_target_pairs={{0,16},{8,24},{16,0},{24,8},{1,17},{9,25},{17,1},{25,9},{2,18},{10... | collective-permute-start | bytes 245768 | tf_op jit(solution)/shard_map/ppermute | solution.py:40
  17.4 1.3 collective-permute-start.11
  18.7 1.7 %collective-permute-done.4 = bf16[32,1280]{1,0:T(8,128)(2,1)S(1)} collective-permute-done((bf16[32,1280]{1,0:T(8,128)(2,1)S(1)}, bf16[32,1280]{1,0:T(8,128)(2,1)S(1)}, u32[]{:S(2)}, u32[]{:S(2)}) %collective-permute-start.4) | collective-permute-done | bytes 81952 | tf_op jit(solution)/shard_map/ppermute | solution.py:40
  20.4 1.5 %collective-permute-start.5 = (bf16[1,32,1280]{2,1,0:T(8,128)(2,1)S(1)}, bf16[1,32,1280]{2,1,0:T(8,128)(2,1)S(1)}, u32[]{:S(2)}, u32[]{:S(2)}) collective-permute-start(bf16[1,32,1280]{2,1,0:T(8,128)(2,1)S(1)} %bitcast.187), channel_id=1, source_target_pairs={{0,2},{1,3},{2,0},{3,1},{4,6},{5,7},{6,4},{7,5},{8,10},{9,11},{10,... | collective-permute-start | bytes 245768 | tf_op jit(solution)/shard_map/ppermute | solution.py:37
  21.9 1.1 collective-permute-start.6
  23.0 0.9 collective-permute-start.7
  24.0 1.6 %collective-permute-start.12 = (bf16[3,32,1280]{2,1,0:T(8,128)(2,1)S(1)}, bf16[3,32,1280]{2,1,0:T(8,128)(2,1)S(1)}, u32[]{:S(2)}, u32[]{:S(2)}) collective-permute-start(bf16[3,32,1280]{2,1,0:T(8,128)(2,1)S(1)} %pad_maximum_fusion.4), channel_id=1, source_target_pairs={{0,2},{1,3},{2,0},{3,1},{4,6},{5,7},{6,4},{7,5},{8,10},{9,11},{10,... | collective-permute-start | bytes 737288 | tf_op jit(solution)/shard_map/ppermute | solution.py:37
  25.5 1.1 collective-permute-start.13
  26.8 1.0 collective-permute-start.14
  27.8 1.5 collective-permute-done.7
  29.4 4.3 %collective-permute-done.12 = bf16[3,32,1280]{2,1,0:T(8,128)(2,1)S(1)} collective-permute-done((bf16[3,32,1280]{2,1,0:T(8,128)(2,1)S(1)}, bf16[3,32,1280]{2,1,0:T(8,128)(2,1)S(1)}, u32[]{:S(2)}, u32[]{:S(2)}) %collective-permute-start.12) | collective-permute-done | bytes 245792 | tf_op jit(solution)/shard_map/ppermute | solution.py:37
  33.7 4.1 %collective-permute-done.13 = bf16[3,32,1280]{2,1,0:T(8,128)(2,1)S(1)} collective-permute-done((bf16[3,32,1280]{2,1,0:T(8,128)(2,1)S(1)}, bf16[3,32,1280]{2,1,0:T(8,128)(2,1)S(1)}, u32[]{:S(2)}, u32[]{:S(2)}) %collective-permute-start.13) | collective-permute-done | bytes 245792 | tf_op jit(solution)/shard_map/ppermute | solution.py:37
  38.6 2.2 %collective-permute-start.9 = (bf16[432,256]{1,0:T(8,128)(2,1)S(1)}, bf16[432,256]{1,0:T(8,128)(2,1)S(1)}, u32[]{:S(2)}, u32[]{:S(2)}) collective-permute-start(bf16[432,256]{1,0:T(8,128)(2,1)S(1)} %fusion.17), channel_id=1, source_target_pairs={{0,8},{8,16},{16,24},{24,0},{1,9},{9,17},{17,25},{25,1},{2,10},{10... | collective-permute-start | bytes 663560 | tf_op jit(solution)/shard_map/ppermute | solution.py:40
  42.1 6.6 %collective-permute-done.9 = bf16[432,256]{1,0:T(8,128)(2,1)S(1)} collective-permute-done((bf16[432,256]{1,0:T(8,128)(2,1)S(1)}, bf16[432,256]{1,0:T(8,128)(2,1)S(1)}, u32[]{:S(2)}, u32[]{:S(2)}) %collective-permute-start.9) | collective-permute-done | bytes 221216 | tf_op jit(solution)/shard_map/ppermute | solution.py:40
  50.5 2.5 %collective-permute-done.18 = bf16[432,256]{1,0:T(8,128)(2,1)S(1)} collective-permute-done((bf16[432,256]{1,0:T(8,128)(2,1)S(1)}, bf16[432,256]{1,0:T(8,128)(2,1)S(1)}, u32[]{:S(2)}, u32[]{:S(2)}) %collective-permute-start.18) | collective-permute-done | bytes 221216 | tf_op jit(solution)/shard_map/ppermute | solution.py:40
  53.5 0.8 collective-permute-start.19
  54.8 3.0 %collective-permute-done.16 = bf16[432,256]{1,0:T(8,128)(2,1)S(1)} collective-permute-done((bf16[432,256]{1,0:T(8,128)(2,1)S(1)}, bf16[432,256]{1,0:T(8,128)(2,1)S(1)}, u32[]{:S(2)}, u32[]{:S(2)}) %collective-permute-start.16) | collective-permute-done | bytes 221216 | tf_op jit(solution)/shard_map/ppermute | solution.py:40
  57.8 0.8 collective-permute-start.17
  58.6 5.1 %collective-permute-done.19 = bf16[432,256]{1,0:T(8,128)(2,1)S(1)} collective-permute-done((bf16[432,256]{1,0:T(8,128)(2,1)S(1)}, bf16[432,256]{1,0:T(8,128)(2,1)S(1)}, u32[]{:S(2)}, u32[]{:S(2)}) %collective-permute-start.19) | collective-permute-done | bytes 221216 | tf_op jit(solution)/shard_map/ppermute | solution.py:40
  63.8 0.5 convolution_bitcast_fusion.3
  64.3 4.1 %collective-permute-done.17 = bf16[432,256]{1,0:T(8,128)(2,1)S(1)} collective-permute-done((bf16[432,256]{1,0:T(8,128)(2,1)S(1)}, bf16[432,256]{1,0:T(8,128)(2,1)S(1)}, u32[]{:S(2)}, u32[]{:S(2)}) %collective-permute-start.17) | collective-permute-done | bytes 221216 | tf_op jit(solution)/shard_map/ppermute | solution.py:40
  68.4 3.5 %collective-permute-done.20 = bf16[432,256]{1,0:T(8,128)(2,1)S(1)} collective-permute-done((bf16[432,256]{1,0:T(8,128)(2,1)S(1)}, bf16[432,256]{1,0:T(8,128)(2,1)S(1)}, u32[]{:S(2)}, u32[]{:S(2)}) %collective-permute-start.20) | collective-permute-done | bytes 221216 | tf_op jit(solution)/shard_map/ppermute | solution.py:40
  72.0 1.7 %fusion.42 = (bf16[432,256]{1,0:T(8,128)(2,1)S(1)}, bf16[432,256]{1,0:T(8,128)(2,1)}, bf16[432,256]{1,0:T(8,128)(2,1)}, bf16[432,256]{1,0:T(8,128)(2,1)S(1)}) fusion(f32[432,256]{1,0:T(8,128)S(1)} %convolution_bitcast_fusion, bf16[432,256]{1,0:T(8,128)(2,1)S(1)} %collective-permute-done.20, bf16[864,256]{1,0:T(8,128)(2,1)S(1)} %bitcast.176, ...), kind=kLoop, calls=%fused_computation.80 | loop fusion | flops 6414336 | bytes 2654208 | tf_op jit(solution)/shard_map/convert_element_type | solution.py:24
  74.3 0.9 convolution_convert_fusion.3
  75.2 8.4 %collective-permute-done.21 = bf16[432,256]{1,0:T(8,128)(2,1)S(1)} collective-permute-done((bf16[432,256]{1,0:T(8,128)(2,1)S(1)}, bf16[432,256]{1,0:T(8,128)(2,1)S(1)}, u32[]{:S(2)}, u32[]{:S(2)}) %collective-permute-start.21) | collective-permute-done | bytes 221216 | tf_op jit(solution)/shard_map/ppermute | solution.py:40
  83.7 4.7 %collective-permute-done.22 = bf16[432,256]{1,0:T(8,128)(2,1)S(1)} collective-permute-done((bf16[432,256]{1,0:T(8,128)(2,1)S(1)}, bf16[432,256]{1,0:T(8,128)(2,1)S(1)}, u32[]{:S(2)}, u32[]{:S(2)}) %collective-permute-start.22) | collective-permute-done | bytes 221216 | tf_op jit(solution)/shard_map/ppermute | solution.py:40
  88.4 0.9 convolution_convert_fusion.2
  89.3 3.4 %collective-permute-done.23 = bf16[432,256]{1,0:T(8,128)(2,1)S(1)} collective-permute-done((bf16[432,256]{1,0:T(8,128)(2,1)S(1)}, bf16[432,256]{1,0:T(8,128)(2,1)S(1)}, u32[]{:S(2)}, u32[]{:S(2)}) %collective-permute-start.23) | collective-permute-done | bytes 221216 | tf_op jit(solution)/shard_map/ppermute | solution.py:40
  92.7 3.4 %collective-permute-done.24 = bf16[432,256]{1,0:T(8,128)(2,1)S(1)} collective-permute-done((bf16[432,256]{1,0:T(8,128)(2,1)S(1)}, bf16[432,256]{1,0:T(8,128)(2,1)S(1)}, u32[]{:S(2)}, u32[]{:S(2)}) %collective-permute-start.24) | collective-permute-done | bytes 221216 | tf_op jit(solution)/shard_map/ppermute | solution.py:40
  96.2 0.9 convolution_convert_fusion.1
  97.4 7.4 %collective-permute-done.31 = bf16[432,256]{1,0:T(8,128)(2,1)S(1)} collective-permute-done((bf16[432,256]{1,0:T(8,128)(2,1)S(1)}, bf16[432,256]{1,0:T(8,128)(2,1)S(1)}, u32[]{:S(2)}, u32[]{:S(2)}) %collective-permute-start.31) | collective-permute-done | bytes 221216 | tf_op jit(solution)/shard_map/ppermute | solution.py:40
  104.8 2.4 %collective-permute-done.32 = bf16[432,256]{1,0:T(8,128)(2,1)S(1)} collective-permute-done((bf16[432,256]{1,0:T(8,128)(2,1)S(1)}, bf16[432,256]{1,0:T(8,128)(2,1)S(1)}, u32[]{:S(2)}, u32[]{:S(2)}) %collective-permute-start.32) | collective-permute-done | bytes 221216 | tf_op jit(solution)/shard_map/ppermute | solution.py:40
  107.2 0.9 convolution_convert_fusion
  108.1 0.8 dynamic-slice_bitcast_fusion.1
  108.8 1.0 dynamic-slice_bitcast_fusion
  109.9 0.5 collective-permute-start.25
  110.4 1.8 %maximum_bitcast_fusion = bf16[256,864]{0,1:T(8,128)(2,1)} fusion(bf16[432,256]{1,0:T(8,128)(2,1)} %get-tuple-element.12, bf16[432,256]{1,0:T(8,128)(2,1)} %get-tuple-element.19), kind=kLoop, calls=%fused_computation.89 | loop fusion | flops 884736 | bytes 884736 | tf_op jit(solution)/shard_map/transpose | solution.py:96
  112.2 1.1 fusion.29
  113.3 0.6 collective-permute-start.34
  113.9 1.6 %collective-permute-start.35 = (bf16[1,32,1280]{2,1,0:T(8,128)(2,1)S(1)}, bf16[1,32,1280]{2,1,0:T(8,128)(2,1)S(1)}, u32[]{:S(2)}, u32[]{:S(2)}) collective-permute-start(bf16[1,32,1280]{2,1,0:T(8,128)(2,1)S(1)} %get-tuple-element.23), channel_id=1, source_target_pairs={{0,4},{1,5},{2,6},{3,7},{4,0},{5,1},{6,2},{7,3},{8,12},{9,13},{10,... | collective-permute-start | bytes 245768 | tf_op jit(solution)/shard_map/ppermute | solution.py:37
  115.5 1.4 collective-permute-start.36
  116.9 1.5 fusion.7
  118.5 0.6 collective-permute-start.26
  119.1 1.6 %collective-permute-start.27 = (bf16[3,32,1280]{2,1,0:T(8,128)(2,1)S(1)}, bf16[3,32,1280]{2,1,0:T(8,128)(2,1)S(1)}, u32[]{:S(2)}, u32[]{:S(2)}) collective-permute-start(bf16[3,32,1280]{2,1,0:T(8,128)(2,1)S(1)} %get-tuple-element.10), channel_id=1, source_target_pairs={{0,4},{1,5},{2,6},{3,7},{4,0},{5,1},{6,2},{7,3},{8,12},{9,13},{10,... | collective-permute-start | bytes 737288 | tf_op jit(solution)/shard_map/ppermute | solution.py:37
  120.7 1.4 collective-permute-start.28
  122.1 5.3 %collective-permute-done.26 = bf16[3,32,1280]{2,1,0:T(8,128)(2,1)S(1)} collective-permute-done((bf16[3,32,1280]{2,1,0:T(8,128)(2,1)S(1)}, bf16[3,32,1280]{2,1,0:T(8,128)(2,1)S(1)}, u32[]{:S(2)}, u32[]{:S(2)}) %collective-permute-start.26) | collective-permute-done | bytes 245792 | tf_op jit(solution)/shard_map/ppermute | solution.py:37
  127.4 2.8 %collective-permute-done.27 = bf16[3,32,1280]{2,1,0:T(8,128)(2,1)S(1)} collective-permute-done((bf16[3,32,1280]{2,1,0:T(8,128)(2,1)S(1)}, bf16[3,32,1280]{2,1,0:T(8,128)(2,1)S(1)}, u32[]{:S(2)}, u32[]{:S(2)}) %collective-permute-start.27) | collective-permute-done | bytes 245792 | tf_op jit(solution)/shard_map/ppermute | solution.py:37
  130.2 1.2 collective-permute-done.28
  131.8 1.3 collective-permute-start.30
  133.1 4.6 %convolution_multiply_fusion = f32[1280,864]{0,1:T(8,128)} fusion(bf16[256,1280]{1,0:T(8,128)(2,1)S(1)} %bitcast.175, bf16[256,1280]{1,0:T(8,128)(2,1)S(1)} %bitcast.169, bf16[256,1280]{1,0:T(8,128)(2,1)S(1)} %bitcast.166, bf16[256,1280]{1,0:T(8,128)(2,1)S(1)} %bitcast.172, bf16[864,256]{1,0:T(8,128)(2,1)S(1)} %constant_dynamic-update-slice_fusion.4, ...), kind=kOutput, calls=%fused_computation | convolution fusion | flops 2285363200 | bytes 8814592 | tf_op jit(solution)/shard_map/dot_general | solution.py:125
  138.0 2.5 %dynamic_update_slice.47 = bf16[4,32,1280]{2,0,1:T(4,128)(2,1)S(1)} dynamic-update-slice(bf16[4,32,1280]{2,0,1:T(4,128)(2,1)S(1)} %broadcast_in_dim.56, bf16[1,32,1280]{2,0,1:T(2,128)(2,1)S(1)} %copy.30, s32[]{:T(128)S(6)} %select_n.183, s32[]{:T(128)} %constant.209.clone.1, s32[]{:T(128)} %constant.209.clone.1) | dynamic-update-slice | bytes 163844 | tf_op jit(solution)/shard_map/jit(dynamic_update_index_in_dim)/dynamic_update_slice | solution.py:122
  140.8 2.5 %dynamic_update_slice.48 = bf16[4,32,1280]{2,0,1:T(4,128)(2,1)S(1)} dynamic-update-slice(bf16[4,32,1280]{2,0,1:T(4,128)(2,1)S(1)} %dynamic_update_slice.47, bf16[1,32,1280]{2,0,1:T(2,128)(2,1)S(1)} %copy.31, s32[]{:T(128)S(6)} %select_n.184, s32[]{:T(128)} %constant.209.clone.1, s32[]{:T(128)} %constant.209.clone.1) | dynamic-update-slice | bytes 163844 | tf_op jit(solution)/shard_map/jit(dynamic_update_index_in_dim)/dynamic_update_slice | solution.py:122
  143.4 2.5 %dynamic_update_slice.49 = bf16[4,32,1280]{2,0,1:T(4,128)(2,1)S(1)} dynamic-update-slice(bf16[4,32,1280]{2,0,1:T(4,128)(2,1)S(1)} %dynamic_update_slice.48, bf16[1,32,1280]{2,0,1:T(2,128)(2,1)S(1)} %copy.32, s32[]{:T(128)S(6)} %select_n.185, s32[]{:T(128)} %constant.209.clone.1, s32[]{:T(128)} %constant.209.clone.1) | dynamic-update-slice | bytes 163844 | tf_op jit(solution)/shard_map/jit(dynamic_update_index_in_dim)/dynamic_update_slice | solution.py:122
  146.0 2.5 %dynamic_update_slice.50 = bf16[4,32,1280]{2,0,1:T(4,128)(2,1)S(1)} dynamic-update-slice(bf16[4,32,1280]{2,0,1:T(4,128)(2,1)S(1)} %dynamic_update_slice.49, bf16[1,32,1280]{2,0,1:T(2,128)(2,1)S(1)} %copy.33, s32[]{:T(128)S(6)} %select_n.186, s32[]{:T(128)} %constant.209.clone.1, s32[]{:T(128)} %constant.209.clone.1) | dynamic-update-slice | bytes 163844 | tf_op jit(solution)/shard_map/jit(dynamic_update_index_in_dim)/dynamic_update_slice | solution.py:122
  148.5 0.8 copy.37
  (109 shorter events, 8.2 us)
Async XLA Ops:
  1.6 1.5 %collective-permute-start = (bf16[4,32,640]{2,1,0:T(8,128)(2,1)S(1)}, bf16[4,32,640]{2,1,0:T(8,128)(2,1)S(1)}, u32[]{:S(2)}, u32[]{:S(2)}) collective-permute-start(bf16[4,32,640]{2,1,0:T(8,128)(2,1)S(1)} %dynamic-slice_bitcast_fusion.5), channel_id=1, source_target_pairs={{0,1},{1,0},{2,3},{3,2},{4,5},{5,4},{6,7},{7,6},{8,9},{9,8},{10,11... | collective-permute-start | bytes 491528 | tf_op jit(solution)/shard_map/ppermute | solution.py:37
  4.2 7.0 %collective-permute-start.3 = (bf16[32,1280]{1,0:T(8,128)(2,1)S(1)}, bf16[32,1280]{1,0:T(8,128)(2,1)S(1)}, u32[]{:S(2)}, u32[]{:S(2)}) collective-permute-start(bf16[32,1280]{1,0:T(8,128)(2,1)S(1)} %get-tuple-element.29), channel_id=1, source_target_pairs={{0,6},{1,7},{2,4},{3,5},{4,2},{5,3},{6,0},{7,1},{8,14},{9,15},{10,... | collective-permute-start | bytes 245768 | tf_op jit(solution)/shard_map/ppermute | solution.py:37
  8.1 4.8 %collective-permute-start.1 = (bf16[32,1280]{1,0:T(8,128)(2,1)S(1)}, bf16[32,1280]{1,0:T(8,128)(2,1)S(1)}, u32[]{:S(2)}, u32[]{:S(2)}) collective-permute-start(bf16[32,1280]{1,0:T(8,128)(2,1)S(1)} %get-tuple-element.31), channel_id=1, source_target_pairs={{0,2},{1,3},{2,0},{3,1},{4,6},{5,7},{6,4},{7,5},{8,10},{9,11},{10,... | collective-permute-start | bytes 245768 | tf_op jit(solution)/shard_map/ppermute | solution.py:37
  8.6 4.4 %collective-permute-start.2 = (bf16[32,1280]{1,0:T(8,128)(2,1)S(1)}, bf16[32,1280]{1,0:T(8,128)(2,1)S(1)}, u32[]{:S(2)}, u32[]{:S(2)}) collective-permute-start(bf16[32,1280]{1,0:T(8,128)(2,1)S(1)} %get-tuple-element.30), channel_id=1, source_target_pairs={{0,4},{1,5},{2,6},{3,7},{4,0},{5,1},{6,2},{7,3},{8,12},{9,13},{10,... | collective-permute-start | bytes 245768 | tf_op jit(solution)/shard_map/ppermute | solution.py:37
  13.2 7.3 %collective-permute-start.4 = (bf16[32,1280]{1,0:T(8,128)(2,1)S(1)}, bf16[32,1280]{1,0:T(8,128)(2,1)S(1)}, u32[]{:S(2)}, u32[]{:S(2)}) collective-permute-start(bf16[32,1280]{1,0:T(8,128)(2,1)S(1)} %get-tuple-element.24), channel_id=1, source_target_pairs={{0,8},{8,16},{16,24},{24,0},{1,9},{9,17},{17,25},{25,1},{2,10},{10... | collective-permute-start | bytes 245768 | tf_op jit(solution)/shard_map/ppermute | solution.py:40
  14.8 9.1 %collective-permute-start.10 = (bf16[32,1280]{1,0:T(8,128)(2,1)S(1)}, bf16[32,1280]{1,0:T(8,128)(2,1)S(1)}, u32[]{:S(2)}, u32[]{:S(2)}) collective-permute-start(bf16[32,1280]{1,0:T(8,128)(2,1)S(1)} %get-tuple-element.27), channel_id=1, source_target_pairs={{0,16},{8,24},{16,0},{24,8},{1,17},{9,25},{17,1},{25,9},{2,18},{10... | collective-permute-start | bytes 245768 | tf_op jit(solution)/shard_map/ppermute | solution.py:40
  17.4 6.5 %collective-permute-start.11 = (bf16[32,1280]{1,0:T(8,128)(2,1)S(1)}, bf16[32,1280]{1,0:T(8,128)(2,1)S(1)}, u32[]{:S(2)}, u32[]{:S(2)}) collective-permute-start(bf16[32,1280]{1,0:T(8,128)(2,1)S(1)} %get-tuple-element.26), channel_id=1, source_target_pairs={{0,24},{8,0},{16,8},{24,16},{1,25},{9,1},{17,9},{25,17},{2,26},{10... | collective-permute-start | bytes 245768 | tf_op jit(solution)/shard_map/ppermute | solution.py:40
  20.4 6.4 %collective-permute-start.5 = (bf16[1,32,1280]{2,1,0:T(8,128)(2,1)S(1)}, bf16[1,32,1280]{2,1,0:T(8,128)(2,1)S(1)}, u32[]{:S(2)}, u32[]{:S(2)}) collective-permute-start(bf16[1,32,1280]{2,1,0:T(8,128)(2,1)S(1)} %bitcast.187), channel_id=1, source_target_pairs={{0,2},{1,3},{2,0},{3,1},{4,6},{5,7},{6,4},{7,5},{8,10},{9,11},{10,... | collective-permute-start | bytes 245768 | tf_op jit(solution)/shard_map/ppermute | solution.py:37
  21.9 5.9 %collective-permute-start.6 = (bf16[1,32,1280]{2,1,0:T(8,128)(2,1)S(1)}, bf16[1,32,1280]{2,1,0:T(8,128)(2,1)S(1)}, u32[]{:S(2)}, u32[]{:S(2)}) collective-permute-start(bf16[1,32,1280]{2,1,0:T(8,128)(2,1)S(1)} %bitcast.188), channel_id=1, source_target_pairs={{0,4},{1,5},{2,6},{3,7},{4,0},{5,1},{6,2},{7,3},{8,12},{9,13},{10,... | collective-permute-start | bytes 245768 | tf_op jit(solution)/shard_map/ppermute | solution.py:37
  23.0 6.3 %collective-permute-start.7 = (bf16[1,32,1280]{2,1,0:T(8,128)(2,1)S(1)}, bf16[1,32,1280]{2,1,0:T(8,128)(2,1)S(1)}, u32[]{:S(2)}, u32[]{:S(2)}) collective-permute-start(bf16[1,32,1280]{2,1,0:T(8,128)(2,1)S(1)} %bitcast.189), channel_id=1, source_target_pairs={{0,6},{1,7},{2,4},{3,5},{4,2},{5,3},{6,0},{7,1},{8,14},{9,15},{10,... | collective-permute-start | bytes 245768 | tf_op jit(solution)/shard_map/ppermute | solution.py:37
  24.0 9.7 %collective-permute-start.12 = (bf16[3,32,1280]{2,1,0:T(8,128)(2,1)S(1)}, bf16[3,32,1280]{2,1,0:T(8,128)(2,1)S(1)}, u32[]{:S(2)}, u32[]{:S(2)}) collective-permute-start(bf16[3,32,1280]{2,1,0:T(8,128)(2,1)S(1)} %pad_maximum_fusion.4), channel_id=1, source_target_pairs={{0,2},{1,3},{2,0},{3,1},{4,6},{5,7},{6,4},{7,5},{8,10},{9,11},{10,... | collective-permute-start | bytes 737288 | tf_op jit(solution)/shard_map/ppermute | solution.py:37
  25.5 12.3 %collective-permute-start.13 = (bf16[3,32,1280]{2,1,0:T(8,128)(2,1)S(1)}, bf16[3,32,1280]{2,1,0:T(8,128)(2,1)S(1)}, u32[]{:S(2)}, u32[]{:S(2)}) collective-permute-start(bf16[3,32,1280]{2,1,0:T(8,128)(2,1)S(1)} %pad_maximum_fusion.4), channel_id=1, source_target_pairs={{0,4},{1,5},{2,6},{3,7},{4,0},{5,1},{6,2},{7,3},{8,12},{9,13},{10,... | collective-permute-start | bytes 737288 | tf_op jit(solution)/shard_map/ppermute | solution.py:37
  26.8 11.0 %collective-permute-start.14 = (bf16[3,32,1280]{2,1,0:T(8,128)(2,1)S(1)}, bf16[3,32,1280]{2,1,0:T(8,128)(2,1)S(1)}, u32[]{:S(2)}, u32[]{:S(2)}) collective-permute-start(bf16[3,32,1280]{2,1,0:T(8,128)(2,1)S(1)} %pad_maximum_fusion.4), channel_id=1, source_target_pairs={{0,6},{1,7},{2,4},{3,5},{4,2},{5,3},{6,0},{7,1},{8,14},{9,15},{10,... | collective-permute-start | bytes 737288 | tf_op jit(solution)/shard_map/ppermute | solution.py:37
  27.8 10.3 %copy-start = (bf16[1280,864]{0,1:T(8,128)(2,1)S(1)}, bf16[1280,864]{0,1:T(8,128)(2,1)}, u32[]{:S(2)}) copy-start(bf16[1280,864]{0,1:T(8,128)(2,1)} %param.4) | copy-start | bytes 6635524
  29.3 8.6 %collective-permute-start.8 = (bf16[1,4,32,1280]{3,2,1,0:T(8,128)(2,1)S(1)}, bf16[1,4,32,1280]{3,2,1,0:T(8,128)(2,1)S(1)}, u32[]{:S(2)}, u32[]{:S(2)}) collective-permute-start(bf16[1,4,32,1280]{3,2,1,0:T(8,128)(2,1)S(1)} %bitcast_dynamic-update-slice_fusion.4), channel_id=1, source_target_pairs={{0,1},{1,0},{2,3},{3,2},{4,5},{5,4},{6,7},{7,6},{8,9},{9,8},{10,11... | collective-permute-start | bytes 983048 | tf_op jit(solution)/shard_map/ppermute | solution.py:37
  37.8 3.9 %collective-permute-start.15 = (bf16[3,4,32,1280]{3,2,1,0:T(8,128)(2,1)S(1)}, bf16[3,4,32,1280]{3,2,1,0:T(8,128)(2,1)S(1)}, u32[]{:S(2)}, u32[]{:S(2)}) collective-permute-start(bf16[3,4,32,1280]{3,2,1,0:T(8,128)(2,1)S(1)} %bitcast_dynamic-update-slice_fusion), channel_id=1, source_target_pairs={{0,1},{1,0},{2,3},{3,2},{4,5},{5,4},{6,7},{7,6},{8,9},{9,8},{10,11... | collective-permute-start | bytes 2949128 | tf_op jit(solution)/shard_map/ppermute | solution.py:37
  38.1 3.2 %copy-start.7 = (bf16[1,4,2,32,1280]{4,3,2,1,0:T(8,128)(2,1)}, bf16[1,4,2,32,1280]{4,3,2,1,0:T(8,128)(2,1)S(1)}, u32[]{:S(2)}) copy-start(bf16[1,4,2,32,1280]{4,3,2,1,0:T(8,128)(2,1)S(1)} %pad_maximum_fusion.2) | copy-start | bytes 1966084
  38.6 10.1 %collective-permute-start.9 = (bf16[432,256]{1,0:T(8,128)(2,1)S(1)}, bf16[432,256]{1,0:T(8,128)(2,1)S(1)}, u32[]{:S(2)}, u32[]{:S(2)}) collective-permute-start(bf16[432,256]{1,0:T(8,128)(2,1)S(1)} %fusion.17), channel_id=1, source_target_pairs={{0,8},{8,16},{16,24},{24,0},{1,9},{9,17},{17,25},{25,1},{2,10},{10... | collective-permute-start | bytes 663560 | tf_op jit(solution)/shard_map/ppermute | solution.py:40
  41.2 11.8 %collective-permute-start.18 = (bf16[432,256]{1,0:T(8,128)(2,1)S(1)}, bf16[432,256]{1,0:T(8,128)(2,1)S(1)}, u32[]{:S(2)}, u32[]{:S(2)}) collective-permute-start(bf16[432,256]{1,0:T(8,128)(2,1)S(1)} %fusion.18), channel_id=1, source_target_pairs={{0,8},{8,16},{16,24},{24,0},{1,9},{9,17},{17,25},{25,1},{2,10},{10... | collective-permute-start | bytes 663560 | tf_op jit(solution)/shard_map/ppermute | solution.py:40
  42.0 8.0 %copy-start.13 = (bf16[1,4,2,32,1280]{4,3,2,1,0:T(8,128)(2,1)}, bf16[1,4,2,32,1280]{4,3,2,1,0:T(8,128)(2,1)S(1)}, u32[]{:S(2)}) copy-start(bf16[1,4,2,32,1280]{4,3,2,1,0:T(8,128)(2,1)S(1)} %get-tuple-element.5) | copy-start | bytes 1966084
  42.1 11.0 %copy-start.9 = (bf16[1,4,2,32,1280]{4,3,2,1,0:T(8,128)(2,1)}, bf16[1,4,2,32,1280]{4,3,2,1,0:T(8,128)(2,1)S(1)}, u32[]{:S(2)}) copy-start(bf16[1,4,2,32,1280]{4,3,2,1,0:T(8,128)(2,1)S(1)} %get-tuple-element.3) | copy-start | bytes 1966084
  42.1 21.8 %copy-start.11 = (bf16[1,4,2,32,1280]{4,3,2,1,0:T(8,128)(2,1)}, bf16[1,4,2,32,1280]{4,3,2,1,0:T(8,128)(2,1)S(1)}, u32[]{:S(2)}) copy-start(bf16[1,4,2,32,1280]{4,3,2,1,0:T(8,128)(2,1)S(1)} %get-tuple-element.4) | copy-start | bytes 1966084
  49.2 8.6 %collective-permute-start.16 = (bf16[432,256]{1,0:T(8,128)(2,1)S(1)}, bf16[432,256]{1,0:T(8,128)(2,1)S(1)}, u32[]{:S(2)}, u32[]{:S(2)}) collective-permute-start(bf16[432,256]{1,0:T(8,128)(2,1)S(1)} %add_convert_fusion.3), channel_id=1, source_target_pairs={{0,8},{8,16},{16,24},{24,0},{1,9},{9,17},{17,25},{25,1},{2,10},{10... | collective-permute-start | bytes 663560 | tf_op jit(solution)/shard_map/ppermute | solution.py:40
  53.5 10.2 %collective-permute-start.19 = (bf16[432,256]{1,0:T(8,128)(2,1)S(1)}, bf16[432,256]{1,0:T(8,128)(2,1)S(1)}, u32[]{:S(2)}, u32[]{:S(2)}) collective-permute-start(bf16[432,256]{1,0:T(8,128)(2,1)S(1)} %add_convert_fusion.1), channel_id=1, source_target_pairs={{0,8},{8,16},{16,24},{24,0},{1,9},{9,17},{17,25},{25,1},{2,10},{10... | collective-permute-start | bytes 663560 | tf_op jit(solution)/shard_map/ppermute | solution.py:40
  54.8 17.2 %copy-start.15 = (bf16[256,864]{0,1:T(8,128)(2,1)S(1)}, bf16[256,864]{0,1:T(8,128)(2,1)}, u32[]{:S(2)}) copy-start(bf16[256,864]{0,1:T(8,128)(2,1)} %param.5) | copy-start | bytes 1327108
  57.8 10.6 %collective-permute-start.17 = (bf16[432,256]{1,0:T(8,128)(2,1)S(1)}, bf16[432,256]{1,0:T(8,128)(2,1)S(1)}, u32[]{:S(2)}, u32[]{:S(2)}) collective-permute-start(bf16[432,256]{1,0:T(8,128)(2,1)S(1)} %add_convert_fusion.2), channel_id=1, source_target_pairs={{0,8},{8,16},{16,24},{24,0},{1,9},{9,17},{17,25},{25,1},{2,10},{10... | collective-permute-start | bytes 663560 | tf_op jit(solution)/shard_map/ppermute | solution.py:40
  63.8 8.2 %collective-permute-start.20 = (bf16[432,256]{1,0:T(8,128)(2,1)S(1)}, bf16[432,256]{1,0:T(8,128)(2,1)S(1)}, u32[]{:S(2)}, u32[]{:S(2)}) collective-permute-start(bf16[432,256]{1,0:T(8,128)(2,1)S(1)} %add_convert_fusion), channel_id=1, source_target_pairs={{0,8},{8,16},{16,24},{24,0},{1,9},{9,17},{17,25},{25,1},{2,10},{10... | collective-permute-start | bytes 663560 | tf_op jit(solution)/shard_map/ppermute | solution.py:40
  73.6 15.7 %copy-start.3 = (bf16[432,256]{1,0:T(8,128)(2,1)}, bf16[432,256]{1,0:T(8,128)(2,1)S(1)}, u32[]{:S(2)}) copy-start(bf16[432,256]{1,0:T(8,128)(2,1)S(1)} %get-tuple-element.11) | copy-start | bytes 663556
  73.6 15.7 %copy-start.5 = (bf16[432,256]{1,0:T(8,128)(2,1)}, bf16[432,256]{1,0:T(8,128)(2,1)S(1)}, u32[]{:S(2)}) copy-start(bf16[432,256]{1,0:T(8,128)(2,1)S(1)} %get-tuple-element.20) | copy-start | bytes 663556
  73.6 10.0 %collective-permute-start.21 = (bf16[432,256]{1,0:T(8,128)(2,1)S(1)}, bf16[432,256]{1,0:T(8,128)(2,1)S(1)}, u32[]{:S(2)}, u32[]{:S(2)}) collective-permute-start(bf16[432,256]{1,0:T(8,128)(2,1)S(1)} %get-tuple-element.20), channel_id=1, source_target_pairs={{0,8},{8,16},{16,24},{24,0},{1,9},{9,17},{17,25},{25,1},{2,10},{10... | collective-permute-start | bytes 663560 | tf_op jit(solution)/shard_map/ppermute | solution.py:40
  73.9 14.5 %collective-permute-start.22 = (bf16[432,256]{1,0:T(8,128)(2,1)S(1)}, bf16[432,256]{1,0:T(8,128)(2,1)S(1)}, u32[]{:S(2)}, u32[]{:S(2)}) collective-permute-start(bf16[432,256]{1,0:T(8,128)(2,1)S(1)} %get-tuple-element.11), channel_id=1, source_target_pairs={{0,8},{8,16},{16,24},{24,0},{1,9},{9,17},{17,25},{25,1},{2,10},{10... | collective-permute-start | bytes 663560 | tf_op jit(solution)/shard_map/ppermute | solution.py:40
  83.7 9.0 %collective-permute-start.23 = (bf16[432,256]{1,0:T(8,128)(2,1)S(1)}, bf16[432,256]{1,0:T(8,128)(2,1)S(1)}, u32[]{:S(2)}, u32[]{:S(2)}) collective-permute-start(bf16[432,256]{1,0:T(8,128)(2,1)S(1)} %collective-permute-done.21), channel_id=1, source_target_pairs={{0,8},{8,16},{16,24},{24,0},{1,9},{9,17},{17,25},{25,1},{2,10},{10... | collective-permute-start | bytes 663560 | tf_op jit(solution)/shard_map/ppermute | solution.py:40
  88.4 7.7 %collective-permute-start.24 = (bf16[432,256]{1,0:T(8,128)(2,1)S(1)}, bf16[432,256]{1,0:T(8,128)(2,1)S(1)}, u32[]{:S(2)}, u32[]{:S(2)}) collective-permute-start(bf16[432,256]{1,0:T(8,128)(2,1)S(1)} %collective-permute-done.22), channel_id=1, source_target_pairs={{0,8},{8,16},{16,24},{24,0},{1,9},{9,17},{17,25},{25,1},{2,10},{10... | collective-permute-start | bytes 663560 | tf_op jit(solution)/shard_map/ppermute | solution.py:40
  96.2 1.0 copy-start.1
  97.0 7.8 %collective-permute-start.31 = (bf16[432,256]{1,0:T(8,128)(2,1)S(1)}, bf16[432,256]{1,0:T(8,128)(2,1)S(1)}, u32[]{:S(2)}, u32[]{:S(2)}) collective-permute-start(bf16[432,256]{1,0:T(8,128)(2,1)S(1)} %collective-permute-done.23), channel_id=1, source_target_pairs={{0,8},{8,16},{16,24},{24,0},{1,9},{9,17},{17,25},{25,1},{2,10},{10... | collective-permute-start | bytes 663560 | tf_op jit(solution)/shard_map/ppermute | solution.py:40
  97.1 10.1 %collective-permute-start.32 = (bf16[432,256]{1,0:T(8,128)(2,1)S(1)}, bf16[432,256]{1,0:T(8,128)(2,1)S(1)}, u32[]{:S(2)}, u32[]{:S(2)}) collective-permute-start(bf16[432,256]{1,0:T(8,128)(2,1)S(1)} %collective-permute-done.24), channel_id=1, source_target_pairs={{0,8},{8,16},{16,24},{24,0},{1,9},{9,17},{17,25},{25,1},{2,10},{10... | collective-permute-start | bytes 663560 | tf_op jit(solution)/shard_map/ppermute | solution.py:40
  108.8 3.4 %collective-permute-start.33 = (bf16[1,4,32,1280]{3,2,1,0:T(8,128)(2,1)}, bf16[1,4,32,1280]{3,2,1,0:T(8,128)(2,1)}, u32[]{:S(2)}, u32[]{:S(2)}) collective-permute-start(bf16[1,4,32,1280]{3,2,1,0:T(8,128)(2,1)} %dynamic-slice_bitcast_fusion.1), channel_id=1, source_target_pairs={{0,1},{1,0},{2,3},{3,2},{4,5},{5,4},{6,7},{7,6},{8,9},{9,8},{10,11... | collective-permute-start | bytes 983048 | tf_op jit(solution)/shard_map/ppermute | solution.py:37
  109.9 7.0 %collective-permute-start.25 = (bf16[3,4,32,1280]{3,2,1,0:T(8,128)(2,1)}, bf16[3,4,32,1280]{3,2,1,0:T(8,128)(2,1)}, u32[]{:S(2)}, u32[]{:S(2)}) collective-permute-start(bf16[3,4,32,1280]{3,2,1,0:T(8,128)(2,1)} %dynamic-slice_bitcast_fusion), channel_id=1, source_target_pairs={{0,1},{1,0},{2,3},{3,2},{4,5},{5,4},{6,7},{7,6},{8,9},{9,8},{10,11... | collective-permute-start | bytes 2949128 | tf_op jit(solution)/shard_map/ppermute | solution.py:37
  113.3 7.4 %collective-permute-start.34 = (bf16[1,32,1280]{2,1,0:T(8,128)(2,1)S(1)}, bf16[1,32,1280]{2,1,0:T(8,128)(2,1)S(1)}, u32[]{:S(2)}, u32[]{:S(2)}) collective-permute-start(bf16[1,32,1280]{2,1,0:T(8,128)(2,1)S(1)} %get-tuple-element.21), channel_id=1, source_target_pairs={{0,2},{1,3},{2,0},{3,1},{4,6},{5,7},{6,4},{7,5},{8,10},{9,11},{10,... | collective-permute-start | bytes 245768 | tf_op jit(solution)/shard_map/ppermute | solution.py:37
  113.9 8.1 %collective-permute-start.35 = (bf16[1,32,1280]{2,1,0:T(8,128)(2,1)S(1)}, bf16[1,32,1280]{2,1,0:T(8,128)(2,1)S(1)}, u32[]{:S(2)}, u32[]{:S(2)}) collective-permute-start(bf16[1,32,1280]{2,1,0:T(8,128)(2,1)S(1)} %get-tuple-element.23), channel_id=1, source_target_pairs={{0,4},{1,5},{2,6},{3,7},{4,0},{5,1},{6,2},{7,3},{8,12},{9,13},{10,... | collective-permute-start | bytes 245768 | tf_op jit(solution)/shard_map/ppermute | solution.py:37
  115.5 6.5 %collective-permute-start.36 = (bf16[1,32,1280]{2,1,0:T(8,128)(2,1)S(1)}, bf16[1,32,1280]{2,1,0:T(8,128)(2,1)S(1)}, u32[]{:S(2)}, u32[]{:S(2)}) collective-permute-start(bf16[1,32,1280]{2,1,0:T(8,128)(2,1)S(1)} %get-tuple-element.22), channel_id=1, source_target_pairs={{0,6},{1,7},{2,4},{3,5},{4,2},{5,3},{6,0},{7,1},{8,14},{9,15},{10,... | collective-permute-start | bytes 245768 | tf_op jit(solution)/shard_map/ppermute | solution.py:37
  118.3 14.7 %copy-start.2 = (bf16[864,256]{1,0:T(8,128)(2,1)S(1)}, bf16[864,256]{1,0:T(8,128)(2,1)}, u32[]{:S(2)}) copy-start(bf16[864,256]{1,0:T(8,128)(2,1)} %copy-done.1) | copy-start | bytes 1327108
  118.3 14.7 %copy-start.4 = (bf16[432,256]{1,0:T(8,128)(2,1)S(1)}, bf16[432,256]{1,0:T(8,128)(2,1)}, u32[]{:S(2)}) copy-start(bf16[432,256]{1,0:T(8,128)(2,1)} %copy-done.3) | copy-start | bytes 663556
  118.3 14.7 %copy-start.6 = (bf16[432,256]{1,0:T(8,128)(2,1)S(1)}, bf16[432,256]{1,0:T(8,128)(2,1)}, u32[]{:S(2)}) copy-start(bf16[432,256]{1,0:T(8,128)(2,1)} %copy-done.5) | copy-start | bytes 663556
  118.3 14.7 %copy-start.8 = (bf16[1,4,2,32,1280]{4,3,2,1,0:T(8,128)(2,1)S(1)}, bf16[1,4,2,32,1280]{4,3,2,1,0:T(8,128)(2,1)}, u32[]{:S(2)}) copy-start(bf16[1,4,2,32,1280]{4,3,2,1,0:T(8,128)(2,1)} %copy-done.7) | copy-start | bytes 1966084
  118.4 14.7 %copy-start.10 = (bf16[1,4,2,32,1280]{4,3,2,1,0:T(8,128)(2,1)S(1)}, bf16[1,4,2,32,1280]{4,3,2,1,0:T(8,128)(2,1)}, u32[]{:S(2)}) copy-start(bf16[1,4,2,32,1280]{4,3,2,1,0:T(8,128)(2,1)} %copy-done.9) | copy-start | bytes 1966084
  118.4 14.7 %copy-start.12 = (bf16[1,4,2,32,1280]{4,3,2,1,0:T(8,128)(2,1)S(1)}, bf16[1,4,2,32,1280]{4,3,2,1,0:T(8,128)(2,1)}, u32[]{:S(2)}) copy-start(bf16[1,4,2,32,1280]{4,3,2,1,0:T(8,128)(2,1)} %copy-done.11) | copy-start | bytes 1966084
  118.4 14.7 %copy-start.14 = (bf16[1,4,2,32,1280]{4,3,2,1,0:T(8,128)(2,1)S(1)}, bf16[1,4,2,32,1280]{4,3,2,1,0:T(8,128)(2,1)}, u32[]{:S(2)}) copy-start(bf16[1,4,2,32,1280]{4,3,2,1,0:T(8,128)(2,1)} %copy-done.13) | copy-start | bytes 1966084
  118.5 9.0 %collective-permute-start.26 = (bf16[3,32,1280]{2,1,0:T(8,128)(2,1)S(1)}, bf16[3,32,1280]{2,1,0:T(8,128)(2,1)S(1)}, u32[]{:S(2)}, u32[]{:S(2)}) collective-permute-start(bf16[3,32,1280]{2,1,0:T(8,128)(2,1)S(1)} %get-tuple-element.8), channel_id=1, source_target_pairs={{0,2},{1,3},{2,0},{3,1},{4,6},{5,7},{6,4},{7,5},{8,10},{9,11},{10,... | collective-permute-start | bytes 737288 | tf_op jit(solution)/shard_map/ppermute | solution.py:37
  119.1 11.1 %collective-permute-start.27 = (bf16[3,32,1280]{2,1,0:T(8,128)(2,1)S(1)}, bf16[3,32,1280]{2,1,0:T(8,128)(2,1)S(1)}, u32[]{:S(2)}, u32[]{:S(2)}) collective-permute-start(bf16[3,32,1280]{2,1,0:T(8,128)(2,1)S(1)} %get-tuple-element.10), channel_id=1, source_target_pairs={{0,4},{1,5},{2,6},{3,7},{4,0},{5,1},{6,2},{7,3},{8,12},{9,13},{10,... | collective-permute-start | bytes 737288 | tf_op jit(solution)/shard_map/ppermute | solution.py:37
  120.7 10.7 %collective-permute-start.28 = (bf16[3,32,1280]{2,1,0:T(8,128)(2,1)S(1)}, bf16[3,32,1280]{2,1,0:T(8,128)(2,1)S(1)}, u32[]{:S(2)}, u32[]{:S(2)}) collective-permute-start(bf16[3,32,1280]{2,1,0:T(8,128)(2,1)S(1)} %get-tuple-element.9), channel_id=1, source_target_pairs={{0,6},{1,7},{2,4},{3,5},{4,2},{5,3},{6,0},{7,1},{8,14},{9,15},{10,... | collective-permute-start | bytes 737288 | tf_op jit(solution)/shard_map/ppermute | solution.py:37
  122.1 15.6 %collective-permute-start.37 = (bf16[32,1280]{1,0:T(8,128)(2,1)S(1)}, bf16[32,1280]{1,0:T(8,128)(2,1)S(1)}, u32[]{:S(2)}, u32[]{:S(2)}) collective-permute-start(bf16[32,1280]{1,0:T(8,128)(2,1)S(1)} %fusion.59), channel_id=1, source_target_pairs={{0,8},{8,16},{16,24},{24,0},{1,9},{9,17},{17,25},{25,1},{2,10},{10... | collective-permute-start | bytes 245768 | tf_op jit(solution)/shard_map/ppermute | solution.py:40
  131.5 9.0 %collective-permute-start.29 = (bf16[32,1280]{1,0:T(8,128)(2,1)S(1)}, bf16[32,1280]{1,0:T(8,128)(2,1)S(1)}, u32[]{:S(2)}, u32[]{:S(2)}) collective-permute-start(bf16[32,1280]{1,0:T(8,128)(2,1)S(1)} %get-tuple-element.33), channel_id=1, source_target_pairs={{0,24},{8,0},{16,8},{24,16},{1,25},{9,1},{17,9},{25,17},{2,26},{10... | collective-permute-start | bytes 245768 | tf_op jit(solution)/shard_map/ppermute | solution.py:40
  131.8 8.9 %collective-permute-start.30 = (bf16[32,1280]{1,0:T(8,128)(2,1)S(1)}, bf16[32,1280]{1,0:T(8,128)(2,1)S(1)}, u32[]{:S(2)}, u32[]{:S(2)}) collective-permute-start(bf16[32,1280]{1,0:T(8,128)(2,1)S(1)} %get-tuple-element.32), channel_id=1, source_target_pairs={{0,16},{8,24},{16,0},{24,8},{1,17},{9,25},{17,1},{25,9},{2,18},{10... | collective-permute-start | bytes 245768 | tf_op jit(solution)/shard_map/ppermute | solution.py:40

commit v2 on v0

v2 whole, which is shorter than its diff:
```python
import jax
import jax.numpy as jnp
from jax import lax
from jax.sharding import PartitionSpec as P

grad_scale = 0.015625
cores = 2
streams = 2


def gelu_tanh(value):
    return 0.5 * value * (1.0 + jnp.tanh(0.7978845608 * (value + 0.044715 * value * value * value)))


def at(array, index, axis=0):
    return lax.dynamic_index_in_dim(array, index, axis, keepdims=False)


def wide(array):
    return array.astype(jnp.float32)


def narrow(array):
    return array.astype(jnp.bfloat16)


def after(array, *others):
    return lax.optimization_barrier((array, others))[0]


def product(left, right, axes):
    return lax.dot_general(left, right, (axes, ((), ())), preferred_element_type=jnp.float32)


def on_device(activations, up_weight, hidden_cot, *, n_row, n_col):
    chips = n_col // cores
    row, col = lax.axis_index("row"), lax.axis_index("col")
    chip, core = col // cores, col % cores
    tok, width = activations.shape
    sub = tok // n_col
    depth, units = up_weight.shape
    cut = units // streams
    flipped = up_weight.T

    def across(array, flip):
        return lax.ppermute(array, "col", [(i, i ^ flip) for i in range(n_col)])

    def along(array, shift):
        return lax.ppermute(array, "row", [(i, (i + shift) % n_row) for i in range(n_row)])

    def split(array):
        return [array[i * cut:(i + 1) * cut] for i in range(streams)]

    halved = depth == cores * width
    if halved:
        shares = activations.reshape(chips, tok // chips, width)
        fan = jnp.stack(
            [at(shares, chip)] + [across(at(shares, chip ^ e), cores * e) for e in range(1, chips)]
        )

        def for_plane(plane):
            return at(fan, plane ^ chip)
    else:
        fan = lax.all_to_all(
            activations.reshape(n_col, sub, width), "col", split_axis=0, concat_axis=0, tiled=True
        )
        fan = fan.transpose(1, 0, 2).reshape(sub, n_row, depth)

        def for_plane(plane):
            return at(fan, plane, 1)

    arrived = [for_plane(row)] + [along(for_plane((row + k) % n_row), k) for k in range(1, n_row)]

    def fetch(blocks):
        held = jnp.stack(blocks)
        return [held] + [across(held, cores * e) for e in range(1, chips)]

    def lay(pieces):
        count, part, breadth = pieces[0].shape
        laid = jnp.zeros((count, chips, part, breadth), jnp.bfloat16)
        for e, piece in enumerate(pieces):
            laid = lax.dynamic_update_index_in_dim(laid, piece, chip ^ e, 1)
        return laid

    def gather(pieces):
        own, other = lay(pieces), lay([across(piece, 1) for piece in pieces])
        first, second = jnp.where(core == 0, own, other), jnp.where(core == 0, other, own)
        whole = jnp.stack([first, second], 3 if halved else 2).reshape(-1, tok, depth)
        return [whole[i] for i in range(whole.shape[0])]

    order = list(range(1, n_row)) + [0]
    early = fetch([arrived[order[0]]])
    late = fetch(after([arrived[k] for k in order[1:]], early[1]))
    tokens = gather(early) + gather(late)

    def term(j):
        return [product(part, tokens[j], ((1,), (1,))) for part in split(flipped)]

    flow = [narrow(t) for t in term(0)]
    for j in range(1, n_row):
        flow = [wide(along(f, 1)) + t for f, t in zip(flow, term(j))]
        if j < n_row - 1:
            flow = [narrow(f) for f in flow]

    hidden, slopes = [], []
    for value, cot in zip(flow, split(hidden_cot.T)):
        hidden.append(narrow(gelu_tanh(value)))
        _, pull = jax.vjp(gelu_tanh, value)
        slopes.append(narrow(pull(wide(cot))[0]))
    hidden = jnp.concatenate(hidden).T

    ring = [slopes]
    for k in range(1, n_row - 1):
        ring.append([along(s, 1) for s in ring[-1]])
    ring = [jnp.concatenate(s) for s in ring]
    ring.append(along(ring[-1], 1))

    def meet(blocks):
        terms = [narrow(product(block, flipped, ((0,), (0,)))) for block in blocks]
        laid = jnp.stack(terms).reshape(len(blocks), chips, cores, sub, depth)
        got = across(at(laid, 1 - core, 2), 1)
        return wide(at(laid, core, 2)) + wide(got)

    def fan_out(both):
        return [at(both, chip, 1)] + [narrow(at(both, chip ^ e, 1)) for e in range(1, chips)]

    def finish(parts):
        total = parts[0]
        for e in range(1, chips):
            total = total + wide(across(parts[e], cores * e))
        total = narrow(total)
        return [total[i] for i in range(total.shape[0])]

    parts = fan_out(meet(ring[:-1]))
    sums = finish(parts) + finish(fan_out(meet([after(ring[-1], parts)])))
    placed = [sums[0]] + [along(sums[k], n_row - k) for k in range(1, n_row)]
    step = 1
    while step < n_row:
        turned = [placed[(k - step) % n_row] for k in range(n_row)]
        placed = [jnp.where(row & step, t, p) for t, p in zip(turned, placed)]
        step *= 2
    input_grad = jnp.concatenate(placed, axis=1)

    weight_grad = product(
        jnp.concatenate(ring[1:] + ring[:1], axis=1), jnp.concatenate(tokens, axis=0), ((1,), (0,))
    )
    return (hidden, input_grad, (weight_grad * grad_scale).T)


def solution(mesh):
    n_row, n_col = mesh.shape["row"], mesh.shape["col"]

    def body(activations, up_weight, hidden_cot):
        return on_device(activations, up_weight, hidden_cot, n_row=n_row, n_col=n_col)

    in_specs = (P("row", "col"), P("row", "col"), P("row", "col"))
    out_specs = (P("row", "col"), P(("row", "col"), None), P("row", "col"))
    return jax.shard_map(body, mesh=mesh, in_specs=in_specs, out_specs=out_specs, check_vma=False)
```

time: 364 us -> 130 us (0.36)
  waiting for transfers between devices: 303 us -> 77.5 us
  starting transfers between devices: 7.28 us -> 27.5 us
  between operations: 13.8 us -> 1.3 us
  matrix products: 20.2 us -> 11.9 us
  local copies, waits for them, and re-layouts: 11.5 us -> 6.7 us
    all_gather x3 -> x0, waiting for transfers between devices: 192 us -> none  [the longest x1 159 us: on_device(): panel = lax.all_gather(up_weight, 'row', axis=0, tiled=True)]
    all_to_all x2 -> x0, waiting for transfers between devices: 78.7 us -> none  [the longest x1 75.8 us: on_device(): lax.all_to_all(whole_x, 'row', split_axis=1, concat_axis=0, tiled=True)]
    ppermute x0 -> x42, waiting for transfers between devices: none -> 77.5 us  [the longest x17 46.8 us: along(): lax.ppermute(array, 'row', [(i, (i + shift) % n_row) for i in range(n_row)])]
    unnamed x5 -> x0, waiting for transfers between devices: 32.1 us -> none
    ppermute x0 -> x42, starting transfers between devices: none -> 27.5 us  [the longest x25 19.5 us: across(): return lax.ppermute(array, 'col', [(i, i ^ flip) for i in range(n_col)])]
    dot_general x3 -> x13, matrix products: 20.2 us -> 11.9 us  [product(): lax.dot_general(left, right, (axes, ((), ())), preferred_element_type=jnp...]
    all_to_all x2 -> x0, starting transfers between devices: 7.12 us -> none  [the longest x1 3.68 us: on_device(): lax.all_to_all(whole_x, 'row', split_axis=1, concat_axis=0, tiled=True)]
    unnamed x7 -> x27, local copies, waits for them, and re-layouts: 8.15 us -> 1.22 us
  transfers between devices with their start and end apart: 6 -> 42, of which waited for: 5 -> 31; matrix products, arithmetic and copies ran while one was open for 7% -> 12% of each run, Pallas kernels for 0% -> 0%
where the time goes in v2:
time: 130 us
  waiting for transfers between devices  77.5 us (60%)
  starting transfers between devices  27.5 us (21%)
  matrix products  11.9 us (9%)
  local copies, waits for them, and re-layouts  6.7 us (5%)
  other arithmetic  4.95 us (4%)
  between operations  1.3 us (1%)
    ppermute x17, waiting for transfers between devices, along(): lax.ppermute(array, 'row', [(i, (i + shift) % n_row) for i in range(n_row)])  46.8 us
    ppermute x25, waiting for transfers between devices, across(): return lax.ppermute(array, 'col', [(i, i ^ flip) for i in range(n_col)])  30.7 us
    ppermute x25, starting transfers between devices, across(): return lax.ppermute(array, 'col', [(i, i ^ flip) for i in range(n_col)])  19.5 us
    dot_general x13, matrix products, product(): lax.dot_general(left, right, (axes, ((), ())), preferred_element_type=jnp...  11.9 us
    ppermute x17, starting transfers between devices, along(): lax.ppermute(array, 'row', [(i, (i + shift) % n_row) for i in range(n_row)])  7.93 us
  transfers between devices with their start and end apart: 42, of which 31 were waited for; matrix products, arithmetic and copies ran while one was open for 12% of the time, Pallas kernels for 0%

profile of v2, /device:TPU:0, one launch (start us, length us, event | category | flops | bytes accessed | tf_op | source)
XLA Modules:
  0.0 129.8 jit_solution(675332905122224410)
XLA Ops:
  0.7 1.0 constant_dynamic-slice_fusion.2
  1.7 3.0 %collective-permute-start = (bf16[64,640]{1,0:T(8,128)(2,1)S(1)}, bf16[64,640]{1,0:T(8,128)(2,1)S(1)}, u32[]{:S(2)}, u32[]{:S(2)}) collective-permute-start(bf16[64,640]{1,0:T(8,128)(2,1)S(1)} %get-tuple-element.45), channel_id=1, source_target_pairs={{0,2},{1,3},{2,0},{3,1},{4,6},{5,7},{6,4},{7,5},{8,10},{9,11},{10,... | collective-permute-start | bytes 245768 | tf_op jit(solution)/shard_map/ppermute | solution.py:46
  4.7 1.5 %collective-permute-start.1 = (bf16[64,640]{1,0:T(8,128)(2,1)S(1)}, bf16[64,640]{1,0:T(8,128)(2,1)S(1)}, u32[]{:S(2)}, u32[]{:S(2)}) collective-permute-start(bf16[64,640]{1,0:T(8,128)(2,1)S(1)} %get-tuple-element.44), channel_id=1, source_target_pairs={{0,4},{1,5},{2,6},{3,7},{4,0},{5,1},{6,2},{7,3},{8,12},{9,13},{10,... | collective-permute-start | bytes 245768 | tf_op jit(solution)/shard_map/ppermute | solution.py:46
  6.3 1.2 collective-permute-done
  7.4 2.6 %collective-permute-done.1 = bf16[64,640]{1,0:T(8,128)(2,1)S(1)} collective-permute-done((bf16[64,640]{1,0:T(8,128)(2,1)S(1)}, bf16[64,640]{1,0:T(8,128)(2,1)S(1)}, u32[]{:S(2)}, u32[]{:S(2)}) %collective-permute-start.1) | collective-permute-done | bytes 81952 | tf_op jit(solution)/shard_map/ppermute | solution.py:46
  10.0 1.5 %collective-permute-done.2 = bf16[64,640]{1,0:T(8,128)(2,1)S(1)} collective-permute-done((bf16[64,640]{1,0:T(8,128)(2,1)S(1)}, bf16[64,640]{1,0:T(8,128)(2,1)S(1)}, u32[]{:S(2)}, u32[]{:S(2)}) %collective-permute-start.2) | collective-permute-done | bytes 81952 | tf_op jit(solution)/shard_map/ppermute | solution.py:46
  11.7 1.6 %collective-permute-start.3 = (bf16[64,640]{1,0:T(8,128)(2,1)S(1)}, bf16[64,640]{1,0:T(8,128)(2,1)S(1)}, u32[]{:S(2)}, u32[]{:S(2)}) collective-permute-start(bf16[64,640]{1,0:T(8,128)(2,1)S(1)} %get-tuple-element.38), channel_id=1, source_target_pairs={{0,8},{8,16},{16,24},{24,0},{1,9},{9,17},{17,25},{25,1},{2,10},{10... | collective-permute-start | bytes 245768 | tf_op jit(solution)/shard_map/ppermute | solution.py:49
  13.3 2.6 %collective-permute-start.12 = (bf16[64,640]{1,0:T(8,128)(2,1)S(1)}, bf16[64,640]{1,0:T(8,128)(2,1)S(1)}, u32[]{:S(2)}, u32[]{:S(2)}) collective-permute-start(bf16[64,640]{1,0:T(8,128)(2,1)S(1)} %get-tuple-element.41), channel_id=1, source_target_pairs={{0,16},{8,24},{16,0},{24,8},{1,17},{9,25},{17,1},{25,9},{2,18},{10... | collective-permute-start | bytes 245768 | tf_op jit(solution)/shard_map/ppermute | solution.py:49
  15.9 1.3 %collective-permute-start.13 = (bf16[64,640]{1,0:T(8,128)(2,1)S(1)}, bf16[64,640]{1,0:T(8,128)(2,1)S(1)}, u32[]{:S(2)}, u32[]{:S(2)}) collective-permute-start(bf16[64,640]{1,0:T(8,128)(2,1)S(1)} %get-tuple-element.40), channel_id=1, source_target_pairs={{0,24},{8,0},{16,8},{24,16},{1,25},{9,1},{17,9},{25,17},{2,26},{10... | collective-permute-start | bytes 245768 | tf_op jit(solution)/shard_map/ppermute | solution.py:49
  17.3 1.3 collective-permute-done.3
  18.5 0.9 collective-permute-start.4
  19.4 0.7 collective-permute-start.5
  20.1 0.6 collective-permute-done.12
  20.7 1.5 %collective-permute-start.6 = (bf16[1,64,640]{2,1,0:T(8,128)(2,1)S(1)}, bf16[1,64,640]{2,1,0:T(8,128)(2,1)S(1)}, u32[]{:S(2)}, u32[]{:S(2)}) collective-permute-start(bf16[1,64,640]{2,1,0:T(8,128)(2,1)S(1)} %bitcast.231), channel_id=1, source_target_pairs={{0,6},{1,7},{2,4},{3,5},{4,2},{5,3},{6,0},{7,1},{8,14},{9,15},{10,... | collective-permute-start | bytes 245768 | tf_op jit(solution)/shard_map/ppermute | solution.py:46
  22.1 1.2 collective-permute-done.4
  23.5 0.9 collective-permute-start.14
  24.4 0.8 collective-permute-start.15
  25.3 2.0 %collective-permute-start.16 = (bf16[3,64,640]{2,1,0:T(8,128)(2,1)S(1)}, bf16[3,64,640]{2,1,0:T(8,128)(2,1)S(1)}, u32[]{:S(2)}, u32[]{:S(2)}) collective-permute-start(bf16[3,64,640]{2,1,0:T(8,128)(2,1)S(1)} %pad_maximum_fusion.5), channel_id=1, source_target_pairs={{0,6},{1,7},{2,4},{3,5},{4,2},{5,3},{6,0},{7,1},{8,14},{9,15},{10,... | collective-permute-start | bytes 737288 | tf_op jit(solution)/shard_map/ppermute | solution.py:46
  27.5 1.1 collective-permute-done.8
  28.8 1.1 collective-permute-done.9
  30.1 1.1 collective-permute-done.10
  31.4 0.7 copy.23
  32.1 0.8 copy-done
  34.1 1.6 %collective-permute-start.23 = (bf16[432,256]{1,0:T(8,128)(2,1)S(1)}, bf16[432,256]{1,0:T(8,128)(2,1)S(1)}, u32[]{:S(2)}, u32[]{:S(2)}) collective-permute-start(bf16[432,256]{1,0:T(8,128)(2,1)S(1)} %fusion.17), channel_id=1, source_target_pairs={{0,8},{8,16},{16,24},{24,0},{1,9},{9,17},{17,25},{25,1},{2,10},{10... | collective-permute-start | bytes 663560 | tf_op jit(solution)/shard_map/ppermute | solution.py:49
  35.7 2.1 %collective-permute-done.15 = bf16[3,64,640]{2,1,0:T(8,128)(2,1)S(1)} collective-permute-done((bf16[3,64,640]{2,1,0:T(8,128)(2,1)S(1)}, bf16[3,64,640]{2,1,0:T(8,128)(2,1)S(1)}, u32[]{:S(2)}, u32[]{:S(2)}) %collective-permute-start.15) | collective-permute-done | bytes 245792 | tf_op jit(solution)/shard_map/ppermute | solution.py:46
  37.8 0.6 collective-permute-start.19
  38.7 0.6 collective-permute-done.18
  40.5 0.7 copy.31
  41.3 2.7 %collective-permute-done.11 = bf16[432,256]{1,0:T(8,128)(2,1)S(1)} collective-permute-done((bf16[432,256]{1,0:T(8,128)(2,1)S(1)}, bf16[432,256]{1,0:T(8,128)(2,1)S(1)}, u32[]{:S(2)}, u32[]{:S(2)}) %collective-permute-start.11) | collective-permute-done | bytes 221216 | tf_op jit(solution)/shard_map/ppermute | solution.py:49
  44.6 0.7 copy.32
  46.3 2.0 %collective-permute-done.23 = bf16[432,256]{1,0:T(8,128)(2,1)S(1)} collective-permute-done((bf16[432,256]{1,0:T(8,128)(2,1)S(1)}, bf16[432,256]{1,0:T(8,128)(2,1)S(1)}, u32[]{:S(2)}, u32[]{:S(2)}) %collective-permute-start.23) | collective-permute-done | bytes 221216 | tf_op jit(solution)/shard_map/ppermute | solution.py:49
  48.9 0.7 copy.33
  50.2 2.9 %collective-permute-done.21 = bf16[432,256]{1,0:T(8,128)(2,1)S(1)} collective-permute-done((bf16[432,256]{1,0:T(8,128)(2,1)S(1)}, bf16[432,256]{1,0:T(8,128)(2,1)S(1)}, u32[]{:S(2)}, u32[]{:S(2)}) %collective-permute-start.21) | collective-permute-done | bytes 221216 | tf_op jit(solution)/shard_map/ppermute | solution.py:49
  53.2 5.9 %collective-permute-done.24 = bf16[432,256]{1,0:T(8,128)(2,1)S(1)} collective-permute-done((bf16[432,256]{1,0:T(8,128)(2,1)S(1)}, bf16[432,256]{1,0:T(8,128)(2,1)S(1)}, u32[]{:S(2)}, u32[]{:S(2)}) %collective-permute-start.24) | collective-permute-done | bytes 221216 | tf_op jit(solution)/shard_map/ppermute | solution.py:49
  59.7 4.1 %collective-permute-done.22 = bf16[432,256]{1,0:T(8,128)(2,1)S(1)} collective-permute-done((bf16[432,256]{1,0:T(8,128)(2,1)S(1)}, bf16[432,256]{1,0:T(8,128)(2,1)S(1)}, u32[]{:S(2)}, u32[]{:S(2)}) %collective-permute-start.22) | collective-permute-done | bytes 221216 | tf_op jit(solution)/shard_map/ppermute | solution.py:49
  63.8 3.1 %collective-permute-done.25 = bf16[432,256]{1,0:T(8,128)(2,1)S(1)} collective-permute-done((bf16[432,256]{1,0:T(8,128)(2,1)S(1)}, bf16[432,256]{1,0:T(8,128)(2,1)S(1)}, u32[]{:S(2)}, u32[]{:S(2)}) %collective-permute-start.25) | collective-permute-done | bytes 221216 | tf_op jit(solution)/shard_map/ppermute | solution.py:49
  66.9 1.0 fusion.37
  68.0 0.9 convolution_convert_fusion.3
  68.9 8.5 %collective-permute-done.26 = bf16[432,256]{1,0:T(8,128)(2,1)S(1)} collective-permute-done((bf16[432,256]{1,0:T(8,128)(2,1)S(1)}, bf16[432,256]{1,0:T(8,128)(2,1)S(1)}, u32[]{:S(2)}, u32[]{:S(2)}) %collective-permute-start.26) | collective-permute-done | bytes 221216 | tf_op jit(solution)/shard_map/ppermute | solution.py:49
  77.4 4.7 %collective-permute-done.27 = bf16[432,256]{1,0:T(8,128)(2,1)S(1)} collective-permute-done((bf16[432,256]{1,0:T(8,128)(2,1)S(1)}, bf16[432,256]{1,0:T(8,128)(2,1)S(1)}, u32[]{:S(2)}, u32[]{:S(2)}) %collective-permute-start.27) | collective-permute-done | bytes 221216 | tf_op jit(solution)/shard_map/ppermute | solution.py:49
  82.1 0.9 convolution_convert_fusion.2
  83.0 3.4 %collective-permute-done.28 = bf16[432,256]{1,0:T(8,128)(2,1)S(1)} collective-permute-done((bf16[432,256]{1,0:T(8,128)(2,1)S(1)}, bf16[432,256]{1,0:T(8,128)(2,1)S(1)}, u32[]{:S(2)}, u32[]{:S(2)}) %collective-permute-start.28) | collective-permute-done | bytes 221216 | tf_op jit(solution)/shard_map/ppermute | solution.py:49
  86.4 3.4 %collective-permute-done.29 = bf16[432,256]{1,0:T(8,128)(2,1)S(1)} collective-permute-done((bf16[432,256]{1,0:T(8,128)(2,1)S(1)}, bf16[432,256]{1,0:T(8,128)(2,1)S(1)}, u32[]{:S(2)}, u32[]{:S(2)}) %collective-permute-start.29) | collective-permute-done | bytes 221216 | tf_op jit(solution)/shard_map/ppermute | solution.py:49
  89.9 0.9 convolution_convert_fusion.1
  91.3 2.6 %collective-permute-done.30 = bf16[3,4,32,1280]{3,2,0,1:T(8,128)(2,1)S(1)} collective-permute-done((bf16[3,4,32,1280]{3,2,0,1:T(8,128)(2,1)S(1)}, bf16[3,4,32,1280]{3,2,0,1:T(8,128)(2,1)S(1)}, u32[]{:S(2)}, u32[]{:S(2)}) %collective-permute-start.30) | collective-permute-done | bytes 983072 | tf_op jit(solution)/shard_map/ppermute | solution.py:46
  94.2 0.9 collective-permute-start.31
  95.1 0.7 collective-permute-start.32
  95.8 1.9 %collective-permute-start.33 = (bf16[3,32,1280]{2,1,0:T(8,128)(2,1)S(1)}, bf16[3,32,1280]{2,1,0:T(8,128)(2,1)S(1)}, u32[]{:S(2)}, u32[]{:S(2)}) collective-permute-start(bf16[3,32,1280]{2,1,0:T(8,128)(2,1)S(1)} %get-tuple-element.14), channel_id=1, source_target_pairs={{0,6},{1,7},{2,4},{3,5},{4,2},{5,3},{6,0},{7,1},{8,14},{9,15},{10,... | collective-permute-start | bytes 737288 | tf_op jit(solution)/shard_map/ppermute | solution.py:46
  97.7 5.3 %collective-permute-done.31 = bf16[3,32,1280]{2,1,0:T(8,128)(2,1)S(1)} collective-permute-done((bf16[3,32,1280]{2,1,0:T(8,128)(2,1)S(1)}, bf16[3,32,1280]{2,1,0:T(8,128)(2,1)S(1)}, u32[]{:S(2)}, u32[]{:S(2)}) %collective-permute-start.31) | collective-permute-done | bytes 245792 | tf_op jit(solution)/shard_map/ppermute | solution.py:46
  103.0 5.1 %collective-permute-done.32 = bf16[3,32,1280]{2,1,0:T(8,128)(2,1)S(1)} collective-permute-done((bf16[3,32,1280]{2,1,0:T(8,128)(2,1)S(1)}, bf16[3,32,1280]{2,1,0:T(8,128)(2,1)S(1)}, u32[]{:S(2)}, u32[]{:S(2)}) %collective-permute-start.32) | collective-permute-done | bytes 245792 | tf_op jit(solution)/shard_map/ppermute | solution.py:46
  108.2 2.7 %collective-permute-done.36 = bf16[864,256]{1,0:T(8,128)(2,1)S(1)} collective-permute-done((bf16[864,256]{1,0:T(8,128)(2,1)S(1)}, bf16[864,256]{1,0:T(8,128)(2,1)S(1)}, u32[]{:S(2)}, u32[]{:S(2)}) %collective-permute-start.36) | collective-permute-done | bytes 442400 | tf_op jit(solution)/shard_map/ppermute | solution.py:49
  110.9 0.9 convolution_convert_fusion
  111.8 0.8 dynamic-slice_bitcast_fusion.1
  112.6 0.8 maximum_bitcast_fusion
  113.3 1.2 collective-permute-done.37
  114.5 1.0 convert_add_fusion.1
  115.6 0.9 collective-permute-start.38
  116.5 0.7 collective-permute-start.39
  117.2 1.9 %collective-permute-start.40 = (bf16[1,32,1280]{2,1,0:T(8,128)(2,1)S(1)}, bf16[1,32,1280]{2,1,0:T(8,128)(2,1)S(1)}, u32[]{:S(2)}, u32[]{:S(2)}) collective-permute-start(bf16[1,32,1280]{2,1,0:T(8,128)(2,1)S(1)} %get-tuple-element.28), channel_id=1, source_target_pairs={{0,6},{1,7},{2,4},{3,5},{4,2},{5,3},{6,0},{7,1},{8,14},{9,15},{10,... | collective-permute-start | bytes 245768 | tf_op jit(solution)/shard_map/ppermute | solution.py:46
  119.3 0.8 collective-permute-done.38
  120.1 2.6 %collective-permute-done.39 = bf16[1,32,1280]{2,1,0:T(8,128)(2,1)S(1)} collective-permute-done((bf16[1,32,1280]{2,1,0:T(8,128)(2,1)S(1)}, bf16[1,32,1280]{2,1,0:T(8,128)(2,1)S(1)}, u32[]{:S(2)}, u32[]{:S(2)}) %collective-permute-start.39) | collective-permute-done | bytes 81952 | tf_op jit(solution)/shard_map/ppermute | solution.py:46
  122.9 4.6 %convolution_multiply_fusion = f32[1280,864]{0,1:T(8,128)} fusion(bf16[256,1280]{1,0:T(8,128)(2,1)S(1)} %bitcast.218, bf16[256,1280]{1,0:T(8,128)(2,1)S(1)} %bitcast.215, bf16[256,1280]{1,0:T(8,128)(2,1)S(1)} %bitcast.212, bf16[256,1280]{1,0:T(8,128)(2,1)S(1)} %bitcast.209, bf16[432,256]{1,0:T(8,128)(2,1)S(1)} %get-tuple-element.23, ...), kind=kOutput, calls=%fused_computation | convolution fusion | flops 2285363200 | bytes 8814592 | tf_op jit(solution)/shard_map/dot_general | solution.py:32
  127.4 1.6 %collective-permute-done.41 = bf16[32,1280]{1,0:T(8,128)(2,1)S(1)} collective-permute-done((bf16[32,1280]{1,0:T(8,128)(2,1)S(1)}, bf16[32,1280]{1,0:T(8,128)(2,1)S(1)}, u32[]{:S(2)}, u32[]{:S(2)}) %collective-permute-start.41) | collective-permute-done | bytes 81952 | tf_op jit(solution)/shard_map/ppermute | solution.py:49
  129.1 0.7 pad_maximum_fusion.4
  (110 shorter events, 8.9 us)
Async XLA Ops:
  1.7 5.7 %collective-permute-start = (bf16[64,640]{1,0:T(8,128)(2,1)S(1)}, bf16[64,640]{1,0:T(8,128)(2,1)S(1)}, u32[]{:S(2)}, u32[]{:S(2)}) collective-permute-start(bf16[64,640]{1,0:T(8,128)(2,1)S(1)} %get-tuple-element.45), channel_id=1, source_target_pairs={{0,2},{1,3},{2,0},{3,1},{4,6},{5,7},{6,4},{7,5},{8,10},{9,11},{10,... | collective-permute-start | bytes 245768 | tf_op jit(solution)/shard_map/ppermute | solution.py:46
  4.7 5.3 %collective-permute-start.1 = (bf16[64,640]{1,0:T(8,128)(2,1)S(1)}, bf16[64,640]{1,0:T(8,128)(2,1)S(1)}, u32[]{:S(2)}, u32[]{:S(2)}) collective-permute-start(bf16[64,640]{1,0:T(8,128)(2,1)S(1)} %get-tuple-element.44), channel_id=1, source_target_pairs={{0,4},{1,5},{2,6},{3,7},{4,0},{5,1},{6,2},{7,3},{8,12},{9,13},{10,... | collective-permute-start | bytes 245768 | tf_op jit(solution)/shard_map/ppermute | solution.py:46
  6.2 5.3 %collective-permute-start.2 = (bf16[64,640]{1,0:T(8,128)(2,1)S(1)}, bf16[64,640]{1,0:T(8,128)(2,1)S(1)}, u32[]{:S(2)}, u32[]{:S(2)}) collective-permute-start(bf16[64,640]{1,0:T(8,128)(2,1)S(1)} %get-tuple-element.43), channel_id=1, source_target_pairs={{0,6},{1,7},{2,4},{3,5},{4,2},{5,3},{6,0},{7,1},{8,14},{9,15},{10,... | collective-permute-start | bytes 245768 | tf_op jit(solution)/shard_map/ppermute | solution.py:46
  11.7 6.8 %collective-permute-start.3 = (bf16[64,640]{1,0:T(8,128)(2,1)S(1)}, bf16[64,640]{1,0:T(8,128)(2,1)S(1)}, u32[]{:S(2)}, u32[]{:S(2)}) collective-permute-start(bf16[64,640]{1,0:T(8,128)(2,1)S(1)} %get-tuple-element.38), channel_id=1, source_target_pairs={{0,8},{8,16},{16,24},{24,0},{1,9},{9,17},{17,25},{25,1},{2,10},{10... | collective-permute-start | bytes 245768 | tf_op jit(solution)/shard_map/ppermute | solution.py:49
  13.3 7.4 %collective-permute-start.12 = (bf16[64,640]{1,0:T(8,128)(2,1)S(1)}, bf16[64,640]{1,0:T(8,128)(2,1)S(1)}, u32[]{:S(2)}, u32[]{:S(2)}) collective-permute-start(bf16[64,640]{1,0:T(8,128)(2,1)S(1)} %get-tuple-element.41), channel_id=1, source_target_pairs={{0,16},{8,24},{16,0},{24,8},{1,17},{9,25},{17,1},{25,9},{2,18},{10... | collective-permute-start | bytes 245768 | tf_op jit(solution)/shard_map/ppermute | solution.py:49
  15.9 6.2 %collective-permute-start.13 = (bf16[64,640]{1,0:T(8,128)(2,1)S(1)}, bf16[64,640]{1,0:T(8,128)(2,1)S(1)}, u32[]{:S(2)}, u32[]{:S(2)}) collective-permute-start(bf16[64,640]{1,0:T(8,128)(2,1)S(1)} %get-tuple-element.40), channel_id=1, source_target_pairs={{0,24},{8,0},{16,8},{24,16},{1,25},{9,1},{17,9},{25,17},{2,26},{10... | collective-permute-start | bytes 245768 | tf_op jit(solution)/shard_map/ppermute | solution.py:49
  18.5 5.9 %collective-permute-start.7 = (bf16[1,64,640]{2,1,0:T(8,128)(2,1)S(1)}, bf16[1,64,640]{2,1,0:T(8,128)(2,1)S(1)}, u32[]{:S(2)}, u32[]{:S(2)}) collective-permute-start(bf16[1,64,640]{2,1,0:T(8,128)(2,1)S(1)} %bitcast.228), channel_id=1, source_target_pairs={{0,1},{1,0},{2,3},{3,2},{4,5},{5,4},{6,7},{7,6},{8,9},{9,8},{10,11... | collective-permute-start | bytes 245768 | tf_op jit(solution)/shard_map/ppermute | solution.py:46
  18.5 4.9 %collective-permute-start.4 = (bf16[1,64,640]{2,1,0:T(8,128)(2,1)S(1)}, bf16[1,64,640]{2,1,0:T(8,128)(2,1)S(1)}, u32[]{:S(2)}, u32[]{:S(2)}) collective-permute-start(bf16[1,64,640]{2,1,0:T(8,128)(2,1)S(1)} %bitcast.229), channel_id=1, source_target_pairs={{0,2},{1,3},{2,0},{3,1},{4,6},{5,7},{6,4},{7,5},{8,10},{9,11},{10,... | collective-permute-start | bytes 245768 | tf_op jit(solution)/shard_map/ppermute | solution.py:46
  19.4 5.9 %collective-permute-start.5 = (bf16[1,64,640]{2,1,0:T(8,128)(2,1)S(1)}, bf16[1,64,640]{2,1,0:T(8,128)(2,1)S(1)}, u32[]{:S(2)}, u32[]{:S(2)}) collective-permute-start(bf16[1,64,640]{2,1,0:T(8,128)(2,1)S(1)} %bitcast.230), channel_id=1, source_target_pairs={{0,4},{1,5},{2,6},{3,7},{4,0},{5,1},{6,2},{7,3},{8,12},{9,13},{10,... | collective-permute-start | bytes 245768 | tf_op jit(solution)/shard_map/ppermute | solution.py:46
  20.7 6.6 %collective-permute-start.6 = (bf16[1,64,640]{2,1,0:T(8,128)(2,1)S(1)}, bf16[1,64,640]{2,1,0:T(8,128)(2,1)S(1)}, u32[]{:S(2)}, u32[]{:S(2)}) collective-permute-start(bf16[1,64,640]{2,1,0:T(8,128)(2,1)S(1)} %bitcast.231), channel_id=1, source_target_pairs={{0,6},{1,7},{2,4},{3,5},{4,2},{5,3},{6,0},{7,1},{8,14},{9,15},{10,... | collective-permute-start | bytes 245768 | tf_op jit(solution)/shard_map/ppermute | solution.py:46
  23.4 15.0 %collective-permute-start.17 = (bf16[3,64,640]{2,1,0:T(8,128)(2,1)S(1)}, bf16[3,64,640]{2,1,0:T(8,128)(2,1)S(1)}, u32[]{:S(2)}, u32[]{:S(2)}) collective-permute-start(bf16[3,64,640]{2,1,0:T(8,128)(2,1)S(1)} %pad_maximum_fusion.5), channel_id=1, source_target_pairs={{0,1},{1,0},{2,3},{3,2},{4,5},{5,4},{6,7},{7,6},{8,9},{9,8},{10,11... | collective-permute-start | bytes 737288 | tf_op jit(solution)/shard_map/ppermute | solution.py:46
  23.5 10.6 %collective-permute-start.14 = (bf16[3,64,640]{2,1,0:T(8,128)(2,1)S(1)}, bf16[3,64,640]{2,1,0:T(8,128)(2,1)S(1)}, u32[]{:S(2)}, u32[]{:S(2)}) collective-permute-start(bf16[3,64,640]{2,1,0:T(8,128)(2,1)S(1)} %pad_maximum_fusion.5), channel_id=1, source_target_pairs={{0,2},{1,3},{2,0},{3,1},{4,6},{5,7},{6,4},{7,5},{8,10},{9,11},{10,... | collective-permute-start | bytes 737288 | tf_op jit(solution)/shard_map/ppermute | solution.py:46
  24.4 13.4 %collective-permute-start.15 = (bf16[3,64,640]{2,1,0:T(8,128)(2,1)S(1)}, bf16[3,64,640]{2,1,0:T(8,128)(2,1)S(1)}, u32[]{:S(2)}, u32[]{:S(2)}) collective-permute-start(bf16[3,64,640]{2,1,0:T(8,128)(2,1)S(1)} %pad_maximum_fusion.5), channel_id=1, source_target_pairs={{0,4},{1,5},{2,6},{3,7},{4,0},{5,1},{6,2},{7,3},{8,12},{9,13},{10,... | collective-permute-start | bytes 737288 | tf_op jit(solution)/shard_map/ppermute | solution.py:46
  25.3 12.6 %collective-permute-start.16 = (bf16[3,64,640]{2,1,0:T(8,128)(2,1)S(1)}, bf16[3,64,640]{2,1,0:T(8,128)(2,1)S(1)}, u32[]{:S(2)}, u32[]{:S(2)}) collective-permute-start(bf16[3,64,640]{2,1,0:T(8,128)(2,1)S(1)} %pad_maximum_fusion.5), channel_id=1, source_target_pairs={{0,6},{1,7},{2,4},{3,5},{4,2},{5,3},{6,0},{7,1},{8,14},{9,15},{10,... | collective-permute-start | bytes 737288 | tf_op jit(solution)/shard_map/ppermute | solution.py:46
  27.3 1.3 %collective-permute-start.8 = (bf16[1,64,640]{2,1,0:T(8,128)(2,1)S(1)}, bf16[1,64,640]{2,1,0:T(8,128)(2,1)S(1)}, u32[]{:S(2)}, u32[]{:S(2)}) collective-permute-start(bf16[1,64,640]{2,1,0:T(8,128)(2,1)S(1)} %collective-permute-done.4), channel_id=1, source_target_pairs={{0,1},{1,0},{2,3},{3,2},{4,5},{5,4},{6,7},{7,6},{8,9},{9,8},{10,11... | collective-permute-start | bytes 245768 | tf_op jit(solution)/shard_map/ppermute | solution.py:46
  28.6 1.3 collective-permute-start.9
  29.9 1.3 collective-permute-start.10
  31.3 1.6 %copy-start = (bf16[1280,864]{0,1:T(8,128)(2,1)S(1)}, bf16[1280,864]{0,1:T(8,128)(2,1)}, u32[]{:S(2)}) copy-start(bf16[1280,864]{0,1:T(8,128)(2,1)} %param.4) | copy-start | bytes 6635524
  33.9 10.1 %collective-permute-start.11 = (bf16[432,256]{1,0:T(8,128)(2,1)S(1)}, bf16[432,256]{1,0:T(8,128)(2,1)S(1)}, u32[]{:S(2)}, u32[]{:S(2)}) collective-permute-start(bf16[432,256]{1,0:T(8,128)(2,1)S(1)} %fusion.16), channel_id=1, source_target_pairs={{0,8},{8,16},{16,24},{24,0},{1,9},{9,17},{17,25},{25,1},{2,10},{10... | collective-permute-start | bytes 663560 | tf_op jit(solution)/shard_map/ppermute | solution.py:49
  34.1 14.3 %collective-permute-start.23 = (bf16[432,256]{1,0:T(8,128)(2,1)S(1)}, bf16[432,256]{1,0:T(8,128)(2,1)S(1)}, u32[]{:S(2)}, u32[]{:S(2)}) collective-permute-start(bf16[432,256]{1,0:T(8,128)(2,1)S(1)} %fusion.17), channel_id=1, source_target_pairs={{0,8},{8,16},{16,24},{24,0},{1,9},{9,17},{17,25},{25,1},{2,10},{10... | collective-permute-start | bytes 663560 | tf_op jit(solution)/shard_map/ppermute | solution.py:49
  37.8 1.5 %collective-permute-start.18 = (bf16[3,64,640]{2,1,0:T(8,128)(2,1)S(1)}, bf16[3,64,640]{2,1,0:T(8,128)(2,1)S(1)}, u32[]{:S(2)}, u32[]{:S(2)}) collective-permute-start(bf16[3,64,640]{2,1,0:T(8,128)(2,1)S(1)} %collective-permute-done.14), channel_id=1, source_target_pairs={{0,1},{1,0},{2,3},{3,2},{4,5},{5,4},{6,7},{7,6},{8,9},{9,8},{10,11... | collective-permute-start | bytes 737288 | tf_op jit(solution)/shard_map/ppermute | solution.py:46
  37.8 1.8 %collective-permute-start.19 = (bf16[3,64,640]{2,1,0:T(8,128)(2,1)S(1)}, bf16[3,64,640]{2,1,0:T(8,128)(2,1)S(1)}, u32[]{:S(2)}, u32[]{:S(2)}) collective-permute-start(bf16[3,64,640]{2,1,0:T(8,128)(2,1)S(1)} %collective-permute-done.15), channel_id=1, source_target_pairs={{0,1},{1,0},{2,3},{3,2},{4,5},{5,4},{6,7},{7,6},{8,9},{9,8},{10,11... | collective-permute-start | bytes 737288 | tf_op jit(solution)/shard_map/ppermute | solution.py:46
  38.5 1.6 %collective-permute-start.20 = (bf16[3,64,640]{2,1,0:T(8,128)(2,1)S(1)}, bf16[3,64,640]{2,1,0:T(8,128)(2,1)S(1)}, u32[]{:S(2)}, u32[]{:S(2)}) collective-permute-start(bf16[3,64,640]{2,1,0:T(8,128)(2,1)S(1)} %collective-permute-done.16), channel_id=1, source_target_pairs={{0,1},{1,0},{2,3},{3,2},{4,5},{5,4},{6,7},{7,6},{8,9},{9,8},{10,11... | collective-permute-start | bytes 737288 | tf_op jit(solution)/shard_map/ppermute | solution.py:46
  41.3 7.1 %copy-start.1 = (bf16[32,8,2,640]{3,1,2,0:T(8,128)(2,1)}, bf16[32,8,2,640]{3,1,2,0:T(8,128)(2,1)S(1)}, u32[]{:S(2)}) copy-start(bf16[32,8,2,640]{3,1,2,0:T(8,128)(2,1)S(1)} %copy.43) | copy-start | bytes 1966084
  44.5 8.6 %collective-permute-start.21 = (bf16[432,256]{1,0:T(8,128)(2,1)S(1)}, bf16[432,256]{1,0:T(8,128)(2,1)S(1)}, u32[]{:S(2)}, u32[]{:S(2)}) collective-permute-start(bf16[432,256]{1,0:T(8,128)(2,1)S(1)} %add_convert_fusion.4), channel_id=1, source_target_pairs={{0,8},{8,16},{16,24},{24,0},{1,9},{9,17},{17,25},{25,1},{2,10},{10... | collective-permute-start | bytes 663560 | tf_op jit(solution)/shard_map/ppermute | solution.py:49
  45.3 1.0 copy-start.3
  48.9 10.2 %collective-permute-start.24 = (bf16[432,256]{1,0:T(8,128)(2,1)S(1)}, bf16[432,256]{1,0:T(8,128)(2,1)S(1)}, u32[]{:S(2)}, u32[]{:S(2)}) collective-permute-start(bf16[432,256]{1,0:T(8,128)(2,1)S(1)} %add_convert_fusion.2), channel_id=1, source_target_pairs={{0,8},{8,16},{16,24},{24,0},{1,9},{9,17},{17,25},{25,1},{2,10},{10... | collective-permute-start | bytes 663560 | tf_op jit(solution)/shard_map/ppermute | solution.py:49
  49.7 10.0 %copy-start.5 = (bf16[32,8,2,640]{3,1,2,0:T(8,128)(2,1)}, bf16[32,8,2,640]{3,1,2,0:T(8,128)(2,1)S(1)}, u32[]{:S(2)}) copy-start(bf16[32,8,2,640]{3,1,2,0:T(8,128)(2,1)S(1)} %copy.45) | copy-start | bytes 1966084
  50.2 16.7 %copy-start.9 = (bf16[256,864]{0,1:T(8,128)(2,1)S(1)}, bf16[256,864]{0,1:T(8,128)(2,1)}, u32[]{:S(2)}) copy-start(bf16[256,864]{0,1:T(8,128)(2,1)} %param.5) | copy-start | bytes 1327108
  53.2 10.7 %collective-permute-start.22 = (bf16[432,256]{1,0:T(8,128)(2,1)S(1)}, bf16[432,256]{1,0:T(8,128)(2,1)S(1)}, u32[]{:S(2)}, u32[]{:S(2)}) collective-permute-start(bf16[432,256]{1,0:T(8,128)(2,1)S(1)} %add_convert_fusion.3), channel_id=1, source_target_pairs={{0,8},{8,16},{16,24},{24,0},{1,9},{9,17},{17,25},{25,1},{2,10},{10... | collective-permute-start | bytes 663560 | tf_op jit(solution)/shard_map/ppermute | solution.py:49
  59.1 7.8 %collective-permute-start.25 = (bf16[432,256]{1,0:T(8,128)(2,1)S(1)}, bf16[432,256]{1,0:T(8,128)(2,1)S(1)}, u32[]{:S(2)}, u32[]{:S(2)}) collective-permute-start(bf16[432,256]{1,0:T(8,128)(2,1)S(1)} %add_convert_fusion.1), channel_id=1, source_target_pairs={{0,8},{8,16},{16,24},{24,0},{1,9},{9,17},{17,25},{25,1},{2,10},{10... | collective-permute-start | bytes 663560 | tf_op jit(solution)/shard_map/ppermute | solution.py:49
  67.9 9.5 %collective-permute-start.26 = (bf16[432,256]{1,0:T(8,128)(2,1)S(1)}, bf16[432,256]{1,0:T(8,128)(2,1)S(1)}, u32[]{:S(2)}, u32[]{:S(2)}) collective-permute-start(bf16[432,256]{1,0:T(8,128)(2,1)S(1)} %get-tuple-element.37), channel_id=1, source_target_pairs={{0,8},{8,16},{16,24},{24,0},{1,9},{9,17},{17,25},{25,1},{2,10},{10... | collective-permute-start | bytes 663560 | tf_op jit(solution)/shard_map/ppermute | solution.py:49
  68.0 14.1 %collective-permute-start.27 = (bf16[432,256]{1,0:T(8,128)(2,1)S(1)}, bf16[432,256]{1,0:T(8,128)(2,1)S(1)}, u32[]{:S(2)}, u32[]{:S(2)}) collective-permute-start(bf16[432,256]{1,0:T(8,128)(2,1)S(1)} %get-tuple-element.23), channel_id=1, source_target_pairs={{0,8},{8,16},{16,24},{24,0},{1,9},{9,17},{17,25},{25,1},{2,10},{10... | collective-permute-start | bytes 663560 | tf_op jit(solution)/shard_map/ppermute | solution.py:49
  77.4 9.0 %collective-permute-start.28 = (bf16[432,256]{1,0:T(8,128)(2,1)S(1)}, bf16[432,256]{1,0:T(8,128)(2,1)S(1)}, u32[]{:S(2)}, u32[]{:S(2)}) collective-permute-start(bf16[432,256]{1,0:T(8,128)(2,1)S(1)} %collective-permute-done.26), channel_id=1, source_target_pairs={{0,8},{8,16},{16,24},{24,0},{1,9},{9,17},{17,25},{25,1},{2,10},{10... | collective-permute-start | bytes 663560 | tf_op jit(solution)/shard_map/ppermute | solution.py:49
  82.1 7.7 %collective-permute-start.29 = (bf16[432,256]{1,0:T(8,128)(2,1)S(1)}, bf16[432,256]{1,0:T(8,128)(2,1)S(1)}, u32[]{:S(2)}, u32[]{:S(2)}) collective-permute-start(bf16[432,256]{1,0:T(8,128)(2,1)S(1)} %collective-permute-done.27), channel_id=1, source_target_pairs={{0,8},{8,16},{16,24},{24,0},{1,9},{9,17},{17,25},{25,1},{2,10},{10... | collective-permute-start | bytes 663560 | tf_op jit(solution)/shard_map/ppermute | solution.py:49
  91.2 2.6 %collective-permute-start.30 = (bf16[3,4,32,1280]{3,2,0,1:T(8,128)(2,1)S(1)}, bf16[3,4,32,1280]{3,2,0,1:T(8,128)(2,1)S(1)}, u32[]{:S(2)}, u32[]{:S(2)}) collective-permute-start(bf16[3,4,32,1280]{3,2,0,1:T(8,128)(2,1)S(1)} %bitcast.204), channel_id=1, source_target_pairs={{0,1},{1,0},{2,3},{3,2},{4,5},{5,4},{6,7},{7,6},{8,9},{9,8},{10,11... | collective-permute-start | bytes 2949128 | tf_op jit(solution)/shard_map/ppermute | solution.py:46
  94.2 8.9 %collective-permute-start.31 = (bf16[3,32,1280]{2,1,0:T(8,128)(2,1)S(1)}, bf16[3,32,1280]{2,1,0:T(8,128)(2,1)S(1)}, u32[]{:S(2)}, u32[]{:S(2)}) collective-permute-start(bf16[3,32,1280]{2,1,0:T(8,128)(2,1)S(1)} %get-tuple-element.13), channel_id=1, source_target_pairs={{0,2},{1,3},{2,0},{3,1},{4,6},{5,7},{6,4},{7,5},{8,10},{9,11},{10,... | collective-permute-start | bytes 737288 | tf_op jit(solution)/shard_map/ppermute | solution.py:46
  95.1 13.0 %collective-permute-start.32 = (bf16[3,32,1280]{2,1,0:T(8,128)(2,1)S(1)}, bf16[3,32,1280]{2,1,0:T(8,128)(2,1)S(1)}, u32[]{:S(2)}, u32[]{:S(2)}) collective-permute-start(bf16[3,32,1280]{2,1,0:T(8,128)(2,1)S(1)} %get-tuple-element.15), channel_id=1, source_target_pairs={{0,4},{1,5},{2,6},{3,7},{4,0},{5,1},{6,2},{7,3},{8,12},{9,13},{10,... | collective-permute-start | bytes 737288 | tf_op jit(solution)/shard_map/ppermute | solution.py:46
  95.8 12.3 %collective-permute-start.33 = (bf16[3,32,1280]{2,1,0:T(8,128)(2,1)S(1)}, bf16[3,32,1280]{2,1,0:T(8,128)(2,1)S(1)}, u32[]{:S(2)}, u32[]{:S(2)}) collective-permute-start(bf16[3,32,1280]{2,1,0:T(8,128)(2,1)S(1)} %get-tuple-element.14), channel_id=1, source_target_pairs={{0,6},{1,7},{2,4},{3,5},{4,2},{5,3},{6,0},{7,1},{8,14},{9,15},{10,... | collective-permute-start | bytes 737288 | tf_op jit(solution)/shard_map/ppermute | solution.py:46
  97.7 13.2 %collective-permute-start.36 = (bf16[864,256]{1,0:T(8,128)(2,1)S(1)}, bf16[864,256]{1,0:T(8,128)(2,1)S(1)}, u32[]{:S(2)}, u32[]{:S(2)}) collective-permute-start(bf16[864,256]{1,0:T(8,128)(2,1)S(1)} %constant_dynamic-update-slice_fusion.2), channel_id=1, source_target_pairs={{0,8},{8,16},{16,24},{24,0},{1,9},{9,17},{17,25},{25,1},{2,10},{10... | collective-permute-start | bytes 1327112 | tf_op jit(solution)/shard_map/ppermute | solution.py:49
  110.9 0.9 copy-start.7
  112.5 2.0 %collective-permute-start.37 = (bf16[1,4,32,1280]{3,2,1,0:T(8,128)(2,1)}, bf16[1,4,32,1280]{3,2,1,0:T(8,128)(2,1)}, u32[]{:S(2)}, u32[]{:S(2)}) collective-permute-start(bf16[1,4,32,1280]{3,2,1,0:T(8,128)(2,1)} %dynamic-slice_bitcast_fusion.1), channel_id=1, source_target_pairs={{0,1},{1,0},{2,3},{3,2},{4,5},{5,4},{6,7},{7,6},{8,9},{9,8},{10,11... | collective-permute-start | bytes 983048 | tf_op jit(solution)/shard_map/ppermute | solution.py:46
  112.5 10.3 %copy-start.2 = (bf16[32,8,2,640]{3,1,2,0:T(8,128)(2,1)S(1)}, bf16[32,8,2,640]{3,1,2,0:T(8,128)(2,1)}, u32[]{:S(2)}) copy-start(bf16[32,8,2,640]{3,1,2,0:T(8,128)(2,1)} %copy-done.1) | copy-start | bytes 1966084
  112.5 10.3 %copy-start.4 = (bf16[32,8,2,640]{3,1,2,0:T(8,128)(2,1)S(1)}, bf16[32,8,2,640]{3,1,2,0:T(8,128)(2,1)}, u32[]{:S(2)}) copy-start(bf16[32,8,2,640]{3,1,2,0:T(8,128)(2,1)} %copy-done.3) | copy-start | bytes 1966084
  112.5 10.3 %copy-start.6 = (bf16[32,8,2,640]{3,1,2,0:T(8,128)(2,1)S(1)}, bf16[32,8,2,640]{3,1,2,0:T(8,128)(2,1)}, u32[]{:S(2)}) copy-start(bf16[32,8,2,640]{3,1,2,0:T(8,128)(2,1)} %copy-done.5) | copy-start | bytes 1966084
  112.5 10.3 %copy-start.8 = (bf16[864,256]{1,0:T(8,128)(2,1)S(1)}, bf16[864,256]{1,0:T(8,128)(2,1)}, u32[]{:S(2)}) copy-start(bf16[864,256]{1,0:T(8,128)(2,1)} %copy-done.7) | copy-start | bytes 1327108
  115.6 4.6 %collective-permute-start.38 = (bf16[1,32,1280]{2,1,0:T(8,128)(2,1)S(1)}, bf16[1,32,1280]{2,1,0:T(8,128)(2,1)S(1)}, u32[]{:S(2)}, u32[]{:S(2)}) collective-permute-start(bf16[1,32,1280]{2,1,0:T(8,128)(2,1)S(1)} %get-tuple-element.27), channel_id=1, source_target_pairs={{0,2},{1,3},{2,0},{3,1},{4,6},{5,7},{6,4},{7,5},{8,10},{9,11},{10,... | collective-permute-start | bytes 245768 | tf_op jit(solution)/shard_map/ppermute | solution.py:46
  116.5 6.2 %collective-permute-start.39 = (bf16[1,32,1280]{2,1,0:T(8,128)(2,1)S(1)}, bf16[1,32,1280]{2,1,0:T(8,128)(2,1)S(1)}, u32[]{:S(2)}, u32[]{:S(2)}) collective-permute-start(bf16[1,32,1280]{2,1,0:T(8,128)(2,1)S(1)} %get-tuple-element.29), channel_id=1, source_target_pairs={{0,4},{1,5},{2,6},{3,7},{4,0},{5,1},{6,2},{7,3},{8,12},{9,13},{10,... | collective-permute-start | bytes 245768 | tf_op jit(solution)/shard_map/ppermute | solution.py:46
  117.2 5.5 %collective-permute-start.40 = (bf16[1,32,1280]{2,1,0:T(8,128)(2,1)S(1)}, bf16[1,32,1280]{2,1,0:T(8,128)(2,1)S(1)}, u32[]{:S(2)}, u32[]{:S(2)}) collective-permute-start(bf16[1,32,1280]{2,1,0:T(8,128)(2,1)S(1)} %get-tuple-element.28), channel_id=1, source_target_pairs={{0,6},{1,7},{2,4},{3,5},{4,2},{5,3},{6,0},{7,1},{8,14},{9,15},{10,... | collective-permute-start | bytes 245768 | tf_op jit(solution)/shard_map/ppermute | solution.py:46
  119.2 8.3 %collective-permute-start.34 = (bf16[32,1280]{1,0:T(8,128)(2,1)S(1)}, bf16[32,1280]{1,0:T(8,128)(2,1)S(1)}, u32[]{:S(2)}, u32[]{:S(2)}) collective-permute-start(bf16[32,1280]{1,0:T(8,128)(2,1)S(1)} %get-tuple-element.46), channel_id=1, source_target_pairs={{0,24},{8,0},{16,8},{24,16},{1,25},{9,1},{17,9},{25,17},{2,26},{10... | collective-permute-start | bytes 245768 | tf_op jit(solution)/shard_map/ppermute | solution.py:49
  119.2 8.2 %collective-permute-start.35 = (bf16[32,1280]{1,0:T(8,128)(2,1)S(1)}, bf16[32,1280]{1,0:T(8,128)(2,1)S(1)}, u32[]{:S(2)}, u32[]{:S(2)}) collective-permute-start(bf16[32,1280]{1,0:T(8,128)(2,1)S(1)} %get-tuple-element.47), channel_id=1, source_target_pairs={{0,16},{8,24},{16,0},{24,8},{1,17},{9,25},{17,1},{25,9},{2,18},{10... | collective-permute-start | bytes 245768 | tf_op jit(solution)/shard_map/ppermute | solution.py:49
  122.8 6.3 %collective-permute-start.41 = (bf16[32,1280]{1,0:T(8,128)(2,1)S(1)}, bf16[32,1280]{1,0:T(8,128)(2,1)S(1)}, u32[]{:S(2)}, u32[]{:S(2)}) collective-permute-start(bf16[32,1280]{1,0:T(8,128)(2,1)S(1)} %fusion.58), channel_id=1, source_target_pairs={{0,8},{8,16},{16,24},{24,0},{1,9},{9,17},{17,25},{25,1},{2,10},{10... | collective-permute-start | bytes 245768 | tf_op jit(solution)/shard_map/ppermute | solution.py:49

commit v3 on v2

--- a/solution.py
+++ b/solution.py
@@ -42,11 +42,20 @@
     cut = units // streams
     flipped = up_weight.T
 
+    plane_at = list(range(0, n_row, 2)) + list(range(1, n_row, 2))[::-1]
+    spot_of = [plane_at.index(i) for i in range(n_row)]
+    spot = jnp.where(row % 2 == 0, row // 2, n_row - 1 - row // 2)
+
+    def plane_after(k):
+        there = (spot + k) % n_row
+        return jnp.where(there < (n_row + 1) // 2, 2 * there, 2 * (n_row - 1 - there) + 1)
+
     def across(array, flip):
         return lax.ppermute(array, "col", [(i, i ^ flip) for i in range(n_col)])
 
     def along(array, shift):
-        return lax.ppermute(array, "row", [(i, (i + shift) % n_row) for i in range(n_row)])
+        pairs = [(plane_at[i], plane_at[(i + shift) % n_row]) for i in range(n_row)]
+        return lax.ppermute(array, "row", pairs)
 
     def split(array):
         return [array[i * cut:(i + 1) * cut] for i in range(streams)]
@@ -69,7 +78,7 @@
         def for_plane(plane):
             return at(fan, plane, 1)
 
-    arrived = [for_plane(row)] + [along(for_plane((row + k) % n_row), k) for k in range(1, n_row)]
+    arrived = [for_plane(row)] + [along(for_plane(plane_after(k)), k) for k in range(1, n_row)]
 
     def fetch(blocks):
         held = jnp.stack(blocks)
@@ -82,23 +91,35 @@
             laid = lax.dynamic_update_index_in_dim(laid, piece, chip ^ e, 1)
         return laid
 
+    def blocks_of(whole):
+        whole = whole.reshape(-1, tok, depth)
+        return [whole[i] for i in range(whole.shape[0])]
+
+    def gather_one(pieces):
+        pairs = [list(range(i, i + cores)) for i in range(0, n_col, cores)]
+        return blocks_of(lax.all_gather(lay(pieces), "col", axis=3 if halved else 2, axis_index_groups=pairs))
+
     def gather(pieces):
-        own, other = lay(pieces), lay([across(piece, 1) for piece in pieces])
+        others = [across(piece, 1) for piece in pieces]
+        own, other = lay(pieces), lay(others)
         first, second = jnp.where(core == 0, own, other), jnp.where(core == 0, other, own)
-        whole = jnp.stack([first, second], 3 if halved else 2).reshape(-1, tok, depth)
-        return [whole[i] for i in range(whole.shape[0])]
+        return blocks_of(jnp.stack([first, second], 3 if halved else 2))
+
+    def terms_of(tokens):
+        return [product(part, tokens, ((1,), (1,))) for part in split(flipped)]
 
     order = list(range(1, n_row)) + [0]
     early = fetch([arrived[order[0]]])
     late = fetch(after([arrived[k] for k in order[1:]], early[1]))
-    tokens = gather(early) + gather(late)
+    tokens = gather_one(early)
 
-    def term(j):
-        return [product(part, tokens[j], ((1,), (1,))) for part in split(flipped)]
-
-    flow = [narrow(t) for t in term(0)]
+    flow = [narrow(t) for t in terms_of(tokens[0])]
     for j in range(1, n_row):
-        flow = [wide(along(f, 1)) + t for f, t in zip(flow, term(j))]
+        flow = [along(f, 1) for f in flow]
+        if j == 1:
+            tokens += gather(late)
+            terms = [terms_of(t) for t in tokens[1:]]
+        flow = [wide(f) + t for f, t in zip(flow, terms[j - 1])]
         if j < n_row - 1:
             flow = [narrow(f) for f in flow]
 
@@ -110,39 +131,47 @@
     hidden = jnp.concatenate(hidden).T
 
     ring = [slopes]
-    for k in range(1, n_row - 1):
-        ring.append([along(s, 1) for s in ring[-1]])
-    ring = [jnp.concatenate(s) for s in ring]
-    ring.append(along(ring[-1], 1))
+    for k in range(1, n_row):
+        if k < n_row - 1:
+            ring.append([along(s, 1) for s in ring[-1]])
+        else:
+            ring.append(split(along(jnp.concatenate(ring[-1]), 1)))
 
     def meet(blocks):
-        terms = [narrow(product(block, flipped, ((0,), (0,)))) for block in blocks]
+        terms = [narrow(product(jnp.concatenate(b), flipped, ((0,), (0,)))) for b in blocks]
         laid = jnp.stack(terms).reshape(len(blocks), chips, cores, sub, depth)
-        got = across(at(laid, 1 - core, 2), 1)
-        return wide(at(laid, core, 2)) + wide(got)
-
-    def fan_out(both):
+        give = at(laid, 1 - core, 2)
+        if len(blocks) == 1:
+            got = across(give, 1)
+        else:
+            half = chips // 2
+            got = jnp.concatenate([across(give[:, :half], 1), across(give[:, half:], 1)], axis=1)
+        both = wide(at(laid, core, 2)) + wide(got)
         return [at(both, chip, 1)] + [narrow(at(both, chip ^ e, 1)) for e in range(1, chips)]
 
-    def finish(parts):
-        total = parts[0]
-        for e in range(1, chips):
-            total = total + wide(across(parts[e], cores * e))
+    def exchange(mixed):
+        return mixed[:1] + [across(mixed[e], cores * e) for e in range(1, chips)]
+
+    def finish(pieces):
+        total = pieces[0]
+        for piece in pieces[1:]:
+            total = total + wide(piece)
         total = narrow(total)
         return [total[i] for i in range(total.shape[0])]
 
-    parts = fan_out(meet(ring[:-1]))
-    sums = finish(parts) + finish(fan_out(meet([after(ring[-1], parts)])))
+    pieces = [exchange(meet(ring[:-1])), exchange(meet(ring[-1:]))]
+    sums = finish(pieces[0]) + finish(pieces[1])
     placed = [sums[0]] + [along(sums[k], n_row - k) for k in range(1, n_row)]
     step = 1
     while step < n_row:
         turned = [placed[(k - step) % n_row] for k in range(n_row)]
-        placed = [jnp.where(row & step, t, p) for t, p in zip(turned, placed)]
+        placed = [jnp.where(spot & step, t, p) for t, p in zip(turned, placed)]
         step *= 2
-    input_grad = jnp.concatenate(placed, axis=1)
+    input_grad = jnp.concatenate([placed[spot_of[p]] for p in range(n_row)], axis=1)
 
+    whole = [jnp.concatenate(s) for s in ring]
     weight_grad = product(
-        jnp.concatenate(ring[1:] + ring[:1], axis=1), jnp.concatenate(tokens, axis=0), ((1,), (0,))
+        jnp.concatenate(whole[1:] + whole[:1], axis=1), jnp.concatenate(tokens, axis=0), ((1,), (0,))
     )
     return (hidden, input_grad, (weight_grad * grad_scale).T)
 

time: 130 us -> 123 us (0.946)
  waiting for transfers between devices: 77.5 us -> 39.3 us
  starting transfers between devices: 27.5 us -> 55.1 us
  blocking collectives: 0 us -> 2.28 us
  other arithmetic: 4.95 us -> 6.78 us
    ppermute x17, starting transfers between devices: 7.93 us -> 35.1 us  [along(): return lax.ppermute(array, 'row', pairs)]
    ppermute x17, waiting for transfers between devices: 46.8 us -> 24.2 us  [along(): return lax.ppermute(array, 'row', pairs)]
    ppermute x25 -> x22, waiting for transfers between devices: 30.7 us -> 15.1 us  [across(): return lax.ppermute(array, 'col', [(i, i ^ flip) for i in range(n_col)])]
    all_gather x0 -> x1, blocking collectives: none -> 2.28 us  [gather_one(): lax.all_gather(lay(pieces), 'col', axis=3 if halved else 2, axis_index_gr...]
    slice x3 -> x4, local copies, waits for them, and re-layouts: 2.03 us -> 3.04 us  [the longest x3 2.03 us: blocks_of(): return [whole[i] for i in range(whole.shape[0])]]
    ppermute x25 -> x22, starting transfers between devices: 19.5 us -> 20.1 us  [across(): return lax.ppermute(array, 'col', [(i, i ^ flip) for i in range(n_col)])]
  transfers between devices with their start and end apart: 42 -> 39, of which waited for: 31 -> 20; matrix products, arithmetic and copies ran while one was open for 12% -> 15% of each run, Pallas kernels for 0% -> 0%
where the time goes in v3:
time: 123 us
  starting transfers between devices  55.1 us (45%)
  waiting for transfers between devices  39.3 us (32%)
  matrix products  11.9 us (10%)
  other arithmetic  6.78 us (6%)
  local copies, waits for them, and re-layouts  6.16 us (5%)
  blocking collectives  2.28 us (2%)
  between operations  1.31 us (1%)
    ppermute x17, starting transfers between devices, along(): return lax.ppermute(array, 'row', pairs)  35.1 us
    ppermute x17, waiting for transfers between devices, along(): return lax.ppermute(array, 'row', pairs)  24.2 us
    ppermute x22, starting transfers between devices, across(): return lax.ppermute(array, 'col', [(i, i ^ flip) for i in range(n_col)])  20.1 us
    ppermute x22, waiting for transfers between devices, across(): return lax.ppermute(array, 'col', [(i, i ^ flip) for i in range(n_col)])  15.1 us
    dot_general x13, matrix products, product(): lax.dot_general(left, right, (axes, ((), ())), preferred_element_type=jnp...  11.9 us
  transfers between devices with their start and end apart: 39, of which 20 were waited for; matrix products, arithmetic and copies ran while one was open for 15% of the time, Pallas kernels for 0%

profile of v3, /device:TPU:0, one launch (start us, length us, event | category | flops | bytes accessed | tf_op | source)
XLA Modules:
  0.0 122.9 jit_solution(7834253195319220553)
XLA Ops:
  0.7 1.0 constant_dynamic-slice_fusion.2
  1.7 3.0 %collective-permute-start = (bf16[64,640]{1,0:T(8,128)(2,1)S(1)}, bf16[64,640]{1,0:T(8,128)(2,1)S(1)}, u32[]{:S(2)}, u32[]{:S(2)}) collective-permute-start(bf16[64,640]{1,0:T(8,128)(2,1)S(1)} %get-tuple-element.41), channel_id=1, source_target_pairs={{0,2},{1,3},{2,0},{3,1},{4,6},{5,7},{6,4},{7,5},{8,10},{9,11},{10,... | collective-permute-start | bytes 245768 | tf_op jit(solution)/shard_map/ppermute | solution.py:54
  4.7 1.5 %collective-permute-start.1 = (bf16[64,640]{1,0:T(8,128)(2,1)S(1)}, bf16[64,640]{1,0:T(8,128)(2,1)S(1)}, u32[]{:S(2)}, u32[]{:S(2)}) collective-permute-start(bf16[64,640]{1,0:T(8,128)(2,1)S(1)} %get-tuple-element.40), channel_id=1, source_target_pairs={{0,4},{1,5},{2,6},{3,7},{4,0},{5,1},{6,2},{7,3},{8,12},{9,13},{10,... | collective-permute-start | bytes 245768 | tf_op jit(solution)/shard_map/ppermute | solution.py:54
  6.3 1.2 collective-permute-done
  7.4 2.6 %collective-permute-done.1 = bf16[64,640]{1,0:T(8,128)(2,1)S(1)} collective-permute-done((bf16[64,640]{1,0:T(8,128)(2,1)S(1)}, bf16[64,640]{1,0:T(8,128)(2,1)S(1)}, u32[]{:S(2)}, u32[]{:S(2)}) %collective-permute-start.1) | collective-permute-done | bytes 81952 | tf_op jit(solution)/shard_map/ppermute | solution.py:54
  10.0 1.5 %collective-permute-done.2 = bf16[64,640]{1,0:T(8,128)(2,1)S(1)} collective-permute-done((bf16[64,640]{1,0:T(8,128)(2,1)S(1)}, bf16[64,640]{1,0:T(8,128)(2,1)S(1)}, u32[]{:S(2)}, u32[]{:S(2)}) %collective-permute-start.2) | collective-permute-done | bytes 81952 | tf_op jit(solution)/shard_map/ppermute | solution.py:54
  11.7 2.6 %collective-permute-start.3 = (bf16[64,640]{1,0:T(8,128)(2,1)S(1)}, bf16[64,640]{1,0:T(8,128)(2,1)S(1)}, u32[]{:S(2)}, u32[]{:S(2)}) collective-permute-start(bf16[64,640]{1,0:T(8,128)(2,1)S(1)} %get-tuple-element.34), channel_id=1, source_target_pairs={{0,16},{16,24},{24,8},{8,0},{1,17},{17,25},{25,9},{9,1},{2,18},{18... | collective-permute-start | bytes 245768 | tf_op jit(solution)/shard_map/ppermute | solution.py:58
  14.3 1.3 %collective-permute-start.8 = (bf16[64,640]{1,0:T(8,128)(2,1)S(1)}, bf16[64,640]{1,0:T(8,128)(2,1)S(1)}, u32[]{:S(2)}, u32[]{:S(2)}) collective-permute-start(bf16[64,640]{1,0:T(8,128)(2,1)S(1)} %get-tuple-element.37), channel_id=1, source_target_pairs={{0,24},{16,8},{24,0},{8,16},{1,25},{17,9},{25,1},{9,17},{2,26},{18... | collective-permute-start | bytes 245768 | tf_op jit(solution)/shard_map/ppermute | solution.py:58
  15.7 0.8 collective-permute-start.9
  16.5 0.9 collective-permute-start.4
  17.4 0.6 collective-permute-start.5
  18.0 1.9 %collective-permute-start.6 = (bf16[1,64,640]{2,1,0:T(8,128)(2,1)S(1)}, bf16[1,64,640]{2,1,0:T(8,128)(2,1)S(1)}, u32[]{:S(2)}, u32[]{:S(2)}) collective-permute-start(bf16[1,64,640]{2,1,0:T(8,128)(2,1)S(1)} %bitcast.231), channel_id=1, source_target_pairs={{0,6},{1,7},{2,4},{3,5},{4,2},{5,3},{6,0},{7,1},{8,14},{9,15},{10,... | collective-permute-start | bytes 245768 | tf_op jit(solution)/shard_map/ppermute | solution.py:54
  20.0 0.7 collective-permute-done.8
  20.7 1.3 %collective-permute-done.9 = bf16[64,640]{1,0:T(8,128)(2,1)S(1)} collective-permute-done((bf16[64,640]{1,0:T(8,128)(2,1)S(1)}, bf16[64,640]{1,0:T(8,128)(2,1)S(1)}, u32[]{:S(2)}, u32[]{:S(2)}) %collective-permute-start.9) | collective-permute-done | bytes 81952 | tf_op jit(solution)/shard_map/ppermute | solution.py:58
  22.1 1.1 collective-permute-start.10
  23.1 0.6 collective-permute-start.11
  23.8 1.9 %collective-permute-start.12 = (bf16[3,64,640]{2,1,0:T(8,128)(2,1)S(1)}, bf16[3,64,640]{2,1,0:T(8,128)(2,1)S(1)}, u32[]{:S(2)}, u32[]{:S(2)}) collective-permute-start(bf16[3,64,640]{2,1,0:T(8,128)(2,1)S(1)} %pad_maximum_fusion.4), channel_id=1, source_target_pairs={{0,6},{1,7},{2,4},{3,5},{4,2},{5,3},{6,0},{7,1},{8,14},{9,15},{10,... | collective-permute-start | bytes 737288 | tf_op jit(solution)/shard_map/ppermute | solution.py:54
  25.8 2.3 %all_gather.19 = bf16[1,4,64,2,640]{4,2,1,0,3:T(8,128)(2,1)S(1)} all-gather(bf16[1,4,64,1,640]{4,2,1,0,3:T(8,128)(2,1)S(1)} %bitcast_dynamic-update-slice_fusion.8), channel_id=1, replica_groups={{0,1},{2,3},{4,5},{6,7},{8,9},{10,11},{12,13},{14,15},{16,17},{18,19},{..., dimensions={3}, use_global_device_ids=true | all-gather | bytes 983040 | tf_op jit(solution)/shard_map/all_gather | solution.py:100
  28.0 0.7 copy.47
  30.0 2.5 %collective-permute-start.7 = (bf16[432,256]{1,0:T(8,128)(2,1)S(1)}, bf16[432,256]{1,0:T(8,128)(2,1)S(1)}, u32[]{:S(2)}, u32[]{:S(2)}) collective-permute-start(bf16[432,256]{1,0:T(8,128)(2,1)S(1)} %fusion.16), channel_id=1, source_target_pairs={{0,16},{16,24},{24,8},{8,0},{1,17},{17,25},{25,9},{9,1},{2,18},{18... | collective-permute-start | bytes 663560 | tf_op jit(solution)/shard_map/ppermute | solution.py:58
  32.4 0.9 collective-permute-start.19
  33.3 3.1 %collective-permute-done.11 = bf16[3,64,640]{2,1,0:T(8,128)(2,1)S(1)} collective-permute-done((bf16[3,64,640]{2,1,0:T(8,128)(2,1)S(1)}, bf16[3,64,640]{2,1,0:T(8,128)(2,1)S(1)}, u32[]{:S(2)}, u32[]{:S(2)}) %collective-permute-start.11) | collective-permute-done | bytes 245792 | tf_op jit(solution)/shard_map/ppermute | solution.py:54
  36.5 0.6 collective-permute-start.15
  37.3 0.6 collective-permute-done.14
  39.1 0.7 copy.55
  40.4 2.3 %collective-permute-start.17 = (bf16[432,256]{1,0:T(8,128)(2,1)S(1)}, bf16[432,256]{1,0:T(8,128)(2,1)S(1)}, u32[]{:S(2)}, u32[]{:S(2)}) collective-permute-start(bf16[432,256]{1,0:T(8,128)(2,1)S(1)} %add_convert_fusion.3), channel_id=1, source_target_pairs={{0,16},{16,24},{24,8},{8,0},{1,17},{17,25},{25,9},{9,1},{2,18},{18... | collective-permute-start | bytes 663560 | tf_op jit(solution)/shard_map/ppermute | solution.py:58
  42.8 0.7 copy.56
  45.0 1.0 collective-permute-start.20
  46.1 0.7 copy.57
  47.4 1.2 collective-permute-done.17
  48.6 3.4 %collective-permute-start.18 = (bf16[432,256]{1,0:T(8,128)(2,1)S(1)}, bf16[432,256]{1,0:T(8,128)(2,1)S(1)}, u32[]{:S(2)}, u32[]{:S(2)}) collective-permute-start(bf16[432,256]{1,0:T(8,128)(2,1)S(1)} %add_convert_fusion.2), channel_id=1, source_target_pairs={{0,16},{16,24},{24,8},{8,0},{1,17},{17,25},{25,9},{9,1},{2,18},{18... | collective-permute-start | bytes 663560 | tf_op jit(solution)/shard_map/ppermute | solution.py:58
  52.0 1.4 %collective-permute-done.20 = bf16[432,256]{1,0:T(8,128)(2,1)S(1)} collective-permute-done((bf16[432,256]{1,0:T(8,128)(2,1)S(1)}, bf16[432,256]{1,0:T(8,128)(2,1)S(1)}, u32[]{:S(2)}, u32[]{:S(2)}) %collective-permute-start.20) | collective-permute-done | bytes 221216 | tf_op jit(solution)/shard_map/ppermute | solution.py:58
  53.4 3.3 %collective-permute-start.21 = (bf16[432,256]{1,0:T(8,128)(2,1)S(1)}, bf16[432,256]{1,0:T(8,128)(2,1)S(1)}, u32[]{:S(2)}, u32[]{:S(2)}) collective-permute-start(bf16[432,256]{1,0:T(8,128)(2,1)S(1)} %add_convert_fusion), channel_id=1, source_target_pairs={{0,16},{16,24},{24,8},{8,0},{1,17},{17,25},{25,9},{9,1},{2,18},{18... | collective-permute-start | bytes 663560 | tf_op jit(solution)/shard_map/ppermute | solution.py:58
  57.3 0.9 collective-permute-done.18
  58.1 4.1 %collective-permute-done.21 = bf16[432,256]{1,0:T(8,128)(2,1)S(1)} collective-permute-done((bf16[432,256]{1,0:T(8,128)(2,1)S(1)}, bf16[432,256]{1,0:T(8,128)(2,1)S(1)}, u32[]{:S(2)}, u32[]{:S(2)}) %collective-permute-start.21) | collective-permute-done | bytes 221216 | tf_op jit(solution)/shard_map/ppermute | solution.py:58
  62.3 1.7 %fusion.40 = (bf16[432,256]{1,0:T(8,128)(2,1)S(1)}, bf16[432,256]{1,0:T(8,128)(2,1)}, bf16[432,256]{1,0:T(8,128)(2,1)}, bf16[432,256]{1,0:T(8,128)(2,1)S(1)}) fusion(f32[432,256]{1,0:T(8,128)S(1)} %convolution_bitcast_fusion, bf16[432,256]{1,0:T(8,128)(2,1)S(1)} %collective-permute-done.21, bf16[864,256]{1,0:T(8,128)(2,1)S(1)} %bitcast.220, ...), kind=kLoop, calls=%fused_computation.81 | loop fusion | flops 6414336 | bytes 2654208 | tf_op jit(solution)/shard_map/convert_element_type | solution.py:24
  63.9 3.2 %collective-permute-start.22 = (bf16[432,256]{1,0:T(8,128)(2,1)S(1)}, bf16[432,256]{1,0:T(8,128)(2,1)S(1)}, u32[]{:S(2)}, u32[]{:S(2)}) collective-permute-start(bf16[432,256]{1,0:T(8,128)(2,1)S(1)} %get-tuple-element.33), channel_id=1, source_target_pairs={{0,16},{16,24},{24,8},{8,0},{1,17},{17,25},{25,9},{9,1},{2,18},{18... | collective-permute-start | bytes 663560 | tf_op jit(solution)/shard_map/ppermute | solution.py:58
  67.1 0.9 convolution_convert_fusion.3
  68.0 5.0 %collective-permute-done.22 = bf16[432,256]{1,0:T(8,128)(2,1)S(1)} collective-permute-done((bf16[432,256]{1,0:T(8,128)(2,1)S(1)}, bf16[432,256]{1,0:T(8,128)(2,1)S(1)}, u32[]{:S(2)}, u32[]{:S(2)}) %collective-permute-start.22) | collective-permute-done | bytes 221216 | tf_op jit(solution)/shard_map/ppermute | solution.py:58
  73.0 3.4 %collective-permute-start.24 = (bf16[432,256]{1,0:T(8,128)(2,1)S(1)}, bf16[432,256]{1,0:T(8,128)(2,1)S(1)}, u32[]{:S(2)}, u32[]{:S(2)}) collective-permute-start(bf16[432,256]{1,0:T(8,128)(2,1)S(1)} %collective-permute-done.22), channel_id=1, source_target_pairs={{0,16},{16,24},{24,8},{8,0},{1,17},{17,25},{25,9},{9,1},{2,18},{18... | collective-permute-start | bytes 663560 | tf_op jit(solution)/shard_map/ppermute | solution.py:58
  76.4 1.3 %collective-permute-done.23 = bf16[432,256]{1,0:T(8,128)(2,1)S(1)} collective-permute-done((bf16[432,256]{1,0:T(8,128)(2,1)S(1)}, bf16[432,256]{1,0:T(8,128)(2,1)S(1)}, u32[]{:S(2)}, u32[]{:S(2)}) %collective-permute-start.23) | collective-permute-done | bytes 221216 | tf_op jit(solution)/shard_map/ppermute | solution.py:58
  77.7 3.4 %collective-permute-start.25 = (bf16[432,256]{1,0:T(8,128)(2,1)S(1)}, bf16[432,256]{1,0:T(8,128)(2,1)S(1)}, u32[]{:S(2)}, u32[]{:S(2)}) collective-permute-start(bf16[432,256]{1,0:T(8,128)(2,1)S(1)} %collective-permute-done.23), channel_id=1, source_target_pairs={{0,16},{16,24},{24,8},{8,0},{1,17},{17,25},{25,9},{9,1},{2,18},{18... | collective-permute-start | bytes 663560 | tf_op jit(solution)/shard_map/ppermute | solution.py:58
  81.1 0.9 convolution_convert_fusion.2
  82.5 3.1 %collective-permute-done.25 = bf16[432,256]{1,0:T(8,128)(2,1)S(1)} collective-permute-done((bf16[432,256]{1,0:T(8,128)(2,1)S(1)}, bf16[432,256]{1,0:T(8,128)(2,1)S(1)}, u32[]{:S(2)}, u32[]{:S(2)}) %collective-permute-start.25) | collective-permute-done | bytes 221216 | tf_op jit(solution)/shard_map/ppermute | solution.py:58
  85.7 0.9 convolution_convert_fusion.1
  87.0 1.0 fusion.64
  88.0 0.5 collective-permute-start.27
  88.5 1.8 %maximum_bitcast_fusion = bf16[256,864]{0,1:T(8,128)(2,1)} fusion(bf16[432,256]{1,0:T(8,128)(2,1)} %get-tuple-element.22, bf16[432,256]{1,0:T(8,128)(2,1)} %get-tuple-element.32), kind=kLoop, calls=%fused_computation.90 | loop fusion | flops 884736 | bytes 884736 | tf_op jit(solution)/shard_map/transpose | solution.py:131
  90.4 3.3 %collective-permute-start.33 = (bf16[864,256]{1,0:T(8,128)(2,1)}, bf16[864,256]{1,0:T(8,128)(2,1)S(1)}, u32[]{:S(2)}, u32[]{:S(2)}) collective-permute-start(bf16[864,256]{1,0:T(8,128)(2,1)} %copy-done.3), channel_id=1, source_target_pairs={{0,16},{16,24},{24,8},{8,0},{1,17},{17,25},{25,9},{9,1},{2,18},{18... | collective-permute-start | bytes 1327112 | tf_op jit(solution)/shard_map/ppermute | solution.py:58
  93.7 1.4 %convert_add_fusion = f32[3,4,32,1280]{3,2,0,1:T(8,128)S(1)} fusion(bf16[3,2,32,1280]{3,2,0,1:T(8,128)(2,1)} %collective-permute-done.27, bf16[3,2,32,1280]{3,2,0,1:T(8,128)(2,1)} %collective-permute-done.26, bf16[3,4,1,32,1280]{4,3,2,1,0:T(8,128)(2,1)S(1)} %get-tuple-element.12), kind=kLoop, calls=%fused_computation.17 | loop fusion | flops 1966080 | bytes 3932160 | tf_op jit(solution)/shard_map/add | solution.py:149
  95.3 1.2 collective-permute-start.28
  96.7 2.1 %collective-permute-start.30 = (bf16[3,32,1280]{2,1,0:T(8,128)(2,1)S(1)}, bf16[3,32,1280]{2,1,0:T(8,128)(2,1)S(1)}, u32[]{:S(2)}, u32[]{:S(2)}) collective-permute-start(bf16[3,32,1280]{2,1,0:T(8,128)(2,1)S(1)} %get-tuple-element.10), channel_id=1, source_target_pairs={{0,6},{1,7},{2,4},{3,5},{4,2},{5,3},{6,0},{7,1},{8,14},{9,15},{10,... | collective-permute-start | bytes 737288 | tf_op jit(solution)/shard_map/ppermute | solution.py:54
  98.8 4.8 %collective-permute-done.33 = bf16[864,256]{1,0:T(8,128)(2,1)S(1)} collective-permute-done((bf16[864,256]{1,0:T(8,128)(2,1)}, bf16[864,256]{1,0:T(8,128)(2,1)S(1)}, u32[]{:S(2)}, u32[]{:S(2)}) %collective-permute-start.33) | collective-permute-done | bytes 442400 | tf_op jit(solution)/shard_map/ppermute | solution.py:58
  103.6 0.9 convolution_convert_fusion
  104.7 4.3 %collective-permute-done.29 = bf16[3,32,1280]{2,1,0:T(8,128)(2,1)S(1)} collective-permute-done((bf16[3,32,1280]{2,1,0:T(8,128)(2,1)S(1)}, bf16[3,32,1280]{2,1,0:T(8,128)(2,1)S(1)}, u32[]{:S(2)}, u32[]{:S(2)}) %collective-permute-start.29) | collective-permute-done | bytes 245792 | tf_op jit(solution)/shard_map/ppermute | solution.py:54
  109.3 1.0 collective-permute-start.35
  110.2 0.8 collective-permute-start.36
  111.1 1.8 %collective-permute-start.37 = (bf16[1,32,1280]{2,1,0:T(8,128)(2,1)S(1)}, bf16[1,32,1280]{2,1,0:T(8,128)(2,1)S(1)}, u32[]{:S(2)}, u32[]{:S(2)}) collective-permute-start(bf16[1,32,1280]{2,1,0:T(8,128)(2,1)S(1)} %get-tuple-element.26), channel_id=1, source_target_pairs={{0,6},{1,7},{2,4},{3,5},{4,2},{5,3},{6,0},{7,1},{8,14},{9,15},{10,... | collective-permute-start | bytes 245768 | tf_op jit(solution)/shard_map/ppermute | solution.py:54
  112.9 0.6 collective-permute-start.31
  113.5 1.9 %collective-permute-start.32 = (bf16[32,1280]{1,0:T(8,128)(2,1)S(1)}, bf16[32,1280]{1,0:T(8,128)(2,1)S(1)}, u32[]{:S(2)}, u32[]{:S(2)}) collective-permute-start(bf16[32,1280]{1,0:T(8,128)(2,1)S(1)} %get-tuple-element.42), channel_id=1, source_target_pairs={{0,24},{16,8},{24,0},{8,16},{1,25},{17,9},{25,1},{9,17},{2,26},{18... | collective-permute-start | bytes 245768 | tf_op jit(solution)/shard_map/ppermute | solution.py:58
  115.3 1.1 collective-permute-done.37
  116.5 1.0 collective-permute-start.38
  117.5 4.6 %convolution_multiply_fusion = f32[1280,864]{0,1:T(8,128)} fusion(bf16[256,1280]{1,0:T(8,128)(2,1)S(1)} %bitcast.219, bf16[256,1280]{1,0:T(8,128)(2,1)S(1)} %bitcast.216, bf16[256,1280]{1,0:T(8,128)(2,1)S(1)} %bitcast.213, bf16[256,1280]{1,0:T(8,128)(2,1)S(1)} %bitcast.210, bf16[432,256]{1,0:T(8,128)(2,1)S(1)} %get-tuple-element.21, ...), kind=kOutput, calls=%fused_computation | convolution fusion | flops 2285363200 | bytes 8814592 | tf_op jit(solution)/shard_map/dot_general | solution.py:32
  122.2 0.7 pad_maximum_fusion.3
  (111 shorter events, 8.2 us)
Async XLA Ops:
  1.7 5.7 %collective-permute-start = (bf16[64,640]{1,0:T(8,128)(2,1)S(1)}, bf16[64,640]{1,0:T(8,128)(2,1)S(1)}, u32[]{:S(2)}, u32[]{:S(2)}) collective-permute-start(bf16[64,640]{1,0:T(8,128)(2,1)S(1)} %get-tuple-element.41), channel_id=1, source_target_pairs={{0,2},{1,3},{2,0},{3,1},{4,6},{5,7},{6,4},{7,5},{8,10},{9,11},{10,... | collective-permute-start | bytes 245768 | tf_op jit(solution)/shard_map/ppermute | solution.py:54
  4.7 5.3 %collective-permute-start.1 = (bf16[64,640]{1,0:T(8,128)(2,1)S(1)}, bf16[64,640]{1,0:T(8,128)(2,1)S(1)}, u32[]{:S(2)}, u32[]{:S(2)}) collective-permute-start(bf16[64,640]{1,0:T(8,128)(2,1)S(1)} %get-tuple-element.40), channel_id=1, source_target_pairs={{0,4},{1,5},{2,6},{3,7},{4,0},{5,1},{6,2},{7,3},{8,12},{9,13},{10,... | collective-permute-start | bytes 245768 | tf_op jit(solution)/shard_map/ppermute | solution.py:54
  6.2 5.3 %collective-permute-start.2 = (bf16[64,640]{1,0:T(8,128)(2,1)S(1)}, bf16[64,640]{1,0:T(8,128)(2,1)S(1)}, u32[]{:S(2)}, u32[]{:S(2)}) collective-permute-start(bf16[64,640]{1,0:T(8,128)(2,1)S(1)} %get-tuple-element.39), channel_id=1, source_target_pairs={{0,6},{1,7},{2,4},{3,5},{4,2},{5,3},{6,0},{7,1},{8,14},{9,15},{10,... | collective-permute-start | bytes 245768 | tf_op jit(solution)/shard_map/ppermute | solution.py:54
  11.7 4.8 %collective-permute-start.3 = (bf16[64,640]{1,0:T(8,128)(2,1)S(1)}, bf16[64,640]{1,0:T(8,128)(2,1)S(1)}, u32[]{:S(2)}, u32[]{:S(2)}) collective-permute-start(bf16[64,640]{1,0:T(8,128)(2,1)S(1)} %get-tuple-element.34), channel_id=1, source_target_pairs={{0,16},{16,24},{24,8},{8,0},{1,17},{17,25},{25,9},{9,1},{2,18},{18... | collective-permute-start | bytes 245768 | tf_op jit(solution)/shard_map/ppermute | solution.py:58
  14.3 6.3 %collective-permute-start.8 = (bf16[64,640]{1,0:T(8,128)(2,1)S(1)}, bf16[64,640]{1,0:T(8,128)(2,1)S(1)}, u32[]{:S(2)}, u32[]{:S(2)}) collective-permute-start(bf16[64,640]{1,0:T(8,128)(2,1)S(1)} %get-tuple-element.37), channel_id=1, source_target_pairs={{0,24},{16,8},{24,0},{8,16},{1,25},{17,9},{25,1},{9,17},{2,26},{18... | collective-permute-start | bytes 245768 | tf_op jit(solution)/shard_map/ppermute | solution.py:58
  15.7 6.3 %collective-permute-start.9 = (bf16[64,640]{1,0:T(8,128)(2,1)S(1)}, bf16[64,640]{1,0:T(8,128)(2,1)S(1)}, u32[]{:S(2)}, u32[]{:S(2)}) collective-permute-start(bf16[64,640]{1,0:T(8,128)(2,1)S(1)} %get-tuple-element.36), channel_id=1, source_target_pairs={{0,8},{16,0},{24,16},{8,24},{1,9},{17,1},{25,17},{9,25},{2,10},{18... | collective-permute-start | bytes 245768 | tf_op jit(solution)/shard_map/ppermute | solution.py:58
  16.5 5.5 %collective-permute-start.4 = (bf16[1,64,640]{2,1,0:T(8,128)(2,1)S(1)}, bf16[1,64,640]{2,1,0:T(8,128)(2,1)S(1)}, u32[]{:S(2)}, u32[]{:S(2)}) collective-permute-start(bf16[1,64,640]{2,1,0:T(8,128)(2,1)S(1)} %bitcast.229), channel_id=1, source_target_pairs={{0,2},{1,3},{2,0},{3,1},{4,6},{5,7},{6,4},{7,5},{8,10},{9,11},{10,... | collective-permute-start | bytes 245768 | tf_op jit(solution)/shard_map/ppermute | solution.py:54
  17.4 6.3 %collective-permute-start.5 = (bf16[1,64,640]{2,1,0:T(8,128)(2,1)S(1)}, bf16[1,64,640]{2,1,0:T(8,128)(2,1)S(1)}, u32[]{:S(2)}, u32[]{:S(2)}) collective-permute-start(bf16[1,64,640]{2,1,0:T(8,128)(2,1)S(1)} %bitcast.230), channel_id=1, source_target_pairs={{0,4},{1,5},{2,6},{3,7},{4,0},{5,1},{6,2},{7,3},{8,12},{9,13},{10,... | collective-permute-start | bytes 245768 | tf_op jit(solution)/shard_map/ppermute | solution.py:54
  18.0 7.7 %collective-permute-start.6 = (bf16[1,64,640]{2,1,0:T(8,128)(2,1)S(1)}, bf16[1,64,640]{2,1,0:T(8,128)(2,1)S(1)}, u32[]{:S(2)}, u32[]{:S(2)}) collective-permute-start(bf16[1,64,640]{2,1,0:T(8,128)(2,1)S(1)} %bitcast.231), channel_id=1, source_target_pairs={{0,6},{1,7},{2,4},{3,5},{4,2},{5,3},{6,0},{7,1},{8,14},{9,15},{10,... | collective-permute-start | bytes 245768 | tf_op jit(solution)/shard_map/ppermute | solution.py:54
  21.9 6.9 %copy-start = (bf16[1280,864]{0,1:T(8,128)(2,1)S(1)}, bf16[1280,864]{0,1:T(8,128)(2,1)}, u32[]{:S(2)}) copy-start(bf16[1280,864]{0,1:T(8,128)(2,1)} %param.4) | copy-start | bytes 6635524
  22.0 15.1 %collective-permute-start.13 = (bf16[3,64,640]{2,1,0:T(8,128)(2,1)S(1)}, bf16[3,64,640]{2,1,0:T(8,128)(2,1)S(1)}, u32[]{:S(2)}, u32[]{:S(2)}) collective-permute-start(bf16[3,64,640]{2,1,0:T(8,128)(2,1)S(1)} %pad_maximum_fusion.4), channel_id=1, source_target_pairs={{0,1},{1,0},{2,3},{3,2},{4,5},{5,4},{6,7},{7,6},{8,9},{9,8},{10,11... | collective-permute-start | bytes 737288 | tf_op jit(solution)/shard_map/ppermute | solution.py:54
  22.1 10.4 %collective-permute-start.10 = (bf16[3,64,640]{2,1,0:T(8,128)(2,1)S(1)}, bf16[3,64,640]{2,1,0:T(8,128)(2,1)S(1)}, u32[]{:S(2)}, u32[]{:S(2)}) collective-permute-start(bf16[3,64,640]{2,1,0:T(8,128)(2,1)S(1)} %pad_maximum_fusion.4), channel_id=1, source_target_pairs={{0,2},{1,3},{2,0},{3,1},{4,6},{5,7},{6,4},{7,5},{8,10},{9,11},{10,... | collective-permute-start | bytes 737288 | tf_op jit(solution)/shard_map/ppermute | solution.py:54
  23.1 13.3 %collective-permute-start.11 = (bf16[3,64,640]{2,1,0:T(8,128)(2,1)S(1)}, bf16[3,64,640]{2,1,0:T(8,128)(2,1)S(1)}, u32[]{:S(2)}, u32[]{:S(2)}) collective-permute-start(bf16[3,64,640]{2,1,0:T(8,128)(2,1)S(1)} %pad_maximum_fusion.4), channel_id=1, source_target_pairs={{0,4},{1,5},{2,6},{3,7},{4,0},{5,1},{6,2},{7,3},{8,12},{9,13},{10,... | collective-permute-start | bytes 737288 | tf_op jit(solution)/shard_map/ppermute | solution.py:54
  23.8 12.7 %collective-permute-start.12 = (bf16[3,64,640]{2,1,0:T(8,128)(2,1)S(1)}, bf16[3,64,640]{2,1,0:T(8,128)(2,1)S(1)}, u32[]{:S(2)}, u32[]{:S(2)}) collective-permute-start(bf16[3,64,640]{2,1,0:T(8,128)(2,1)S(1)} %pad_maximum_fusion.4), channel_id=1, source_target_pairs={{0,6},{1,7},{2,4},{3,5},{4,2},{5,3},{6,0},{7,1},{8,14},{9,15},{10,... | collective-permute-start | bytes 737288 | tf_op jit(solution)/shard_map/ppermute | solution.py:54
  28.8 1.0 copy-start.7
  30.0 9.9 %collective-permute-start.7 = (bf16[432,256]{1,0:T(8,128)(2,1)S(1)}, bf16[432,256]{1,0:T(8,128)(2,1)S(1)}, u32[]{:S(2)}, u32[]{:S(2)}) collective-permute-start(bf16[432,256]{1,0:T(8,128)(2,1)S(1)} %fusion.16), channel_id=1, source_target_pairs={{0,16},{16,24},{24,8},{8,0},{1,17},{17,25},{25,9},{9,1},{2,18},{18... | collective-permute-start | bytes 663560 | tf_op jit(solution)/shard_map/ppermute | solution.py:58
  32.4 12.1 %collective-permute-start.19 = (bf16[432,256]{1,0:T(8,128)(2,1)S(1)}, bf16[432,256]{1,0:T(8,128)(2,1)S(1)}, u32[]{:S(2)}, u32[]{:S(2)}) collective-permute-start(bf16[432,256]{1,0:T(8,128)(2,1)S(1)} %fusion.17), channel_id=1, source_target_pairs={{0,16},{16,24},{24,8},{8,0},{1,17},{17,25},{25,9},{9,1},{2,18},{18... | collective-permute-start | bytes 663560 | tf_op jit(solution)/shard_map/ppermute | solution.py:58
  36.4 1.5 %collective-permute-start.14 = (bf16[3,64,640]{2,1,0:T(8,128)(2,1)S(1)}, bf16[3,64,640]{2,1,0:T(8,128)(2,1)S(1)}, u32[]{:S(2)}, u32[]{:S(2)}) collective-permute-start(bf16[3,64,640]{2,1,0:T(8,128)(2,1)S(1)} %collective-permute-done.10), channel_id=1, source_target_pairs={{0,1},{1,0},{2,3},{3,2},{4,5},{5,4},{6,7},{7,6},{8,9},{9,8},{10,11... | collective-permute-start | bytes 737288 | tf_op jit(solution)/shard_map/ppermute | solution.py:54
  36.5 1.8 %collective-permute-start.15 = (bf16[3,64,640]{2,1,0:T(8,128)(2,1)S(1)}, bf16[3,64,640]{2,1,0:T(8,128)(2,1)S(1)}, u32[]{:S(2)}, u32[]{:S(2)}) collective-permute-start(bf16[3,64,640]{2,1,0:T(8,128)(2,1)S(1)} %collective-permute-done.11), channel_id=1, source_target_pairs={{0,1},{1,0},{2,3},{3,2},{4,5},{5,4},{6,7},{7,6},{8,9},{9,8},{10,11... | collective-permute-start | bytes 737288 | tf_op jit(solution)/shard_map/ppermute | solution.py:54
  37.1 1.6 %collective-permute-start.16 = (bf16[3,64,640]{2,1,0:T(8,128)(2,1)S(1)}, bf16[3,64,640]{2,1,0:T(8,128)(2,1)S(1)}, u32[]{:S(2)}, u32[]{:S(2)}) collective-permute-start(bf16[3,64,640]{2,1,0:T(8,128)(2,1)S(1)} %collective-permute-done.12), channel_id=1, source_target_pairs={{0,1},{1,0},{2,3},{3,2},{4,5},{5,4},{6,7},{7,6},{8,9},{9,8},{10,11... | collective-permute-start | bytes 737288 | tf_op jit(solution)/shard_map/ppermute | solution.py:54
  39.9 4.6 %copy-start.9 = (bf16[32,8,2,640]{3,1,2,0:T(8,128)(2,1)}, bf16[32,8,2,640]{3,1,2,0:T(8,128)(2,1)S(1)}, u32[]{:S(2)}) copy-start(bf16[32,8,2,640]{3,1,2,0:T(8,128)(2,1)S(1)} %copy.67) | copy-start | bytes 1966084
  40.4 8.1 %collective-permute-start.17 = (bf16[432,256]{1,0:T(8,128)(2,1)S(1)}, bf16[432,256]{1,0:T(8,128)(2,1)S(1)}, u32[]{:S(2)}, u32[]{:S(2)}) collective-permute-start(bf16[432,256]{1,0:T(8,128)(2,1)S(1)} %add_convert_fusion.3), channel_id=1, source_target_pairs={{0,16},{16,24},{24,8},{8,0},{1,17},{17,25},{25,9},{9,1},{2,18},{18... | collective-permute-start | bytes 663560 | tf_op jit(solution)/shard_map/ppermute | solution.py:58
  43.5 1.0 copy-start.11
  45.0 8.4 %collective-permute-start.20 = (bf16[432,256]{1,0:T(8,128)(2,1)S(1)}, bf16[432,256]{1,0:T(8,128)(2,1)S(1)}, u32[]{:S(2)}, u32[]{:S(2)}) collective-permute-start(bf16[432,256]{1,0:T(8,128)(2,1)S(1)} %add_convert_fusion.1), channel_id=1, source_target_pairs={{0,16},{16,24},{24,8},{8,0},{1,17},{17,25},{25,9},{9,1},{2,18},{18... | collective-permute-start | bytes 663560 | tf_op jit(solution)/shard_map/ppermute | solution.py:58
  46.8 10.4 %copy-start.13 = (bf16[32,8,2,640]{3,1,2,0:T(8,128)(2,1)}, bf16[32,8,2,640]{3,1,2,0:T(8,128)(2,1)S(1)}, u32[]{:S(2)}) copy-start(bf16[32,8,2,640]{3,1,2,0:T(8,128)(2,1)S(1)} %copy.69) | copy-start | bytes 1966084
  47.3 14.9 %copy-start.15 = (bf16[256,864]{0,1:T(8,128)(2,1)S(1)}, bf16[256,864]{0,1:T(8,128)(2,1)}, u32[]{:S(2)}) copy-start(bf16[256,864]{0,1:T(8,128)(2,1)} %param.5) | copy-start | bytes 1327108
  48.6 9.5 %collective-permute-start.18 = (bf16[432,256]{1,0:T(8,128)(2,1)S(1)}, bf16[432,256]{1,0:T(8,128)(2,1)S(1)}, u32[]{:S(2)}, u32[]{:S(2)}) collective-permute-start(bf16[432,256]{1,0:T(8,128)(2,1)S(1)} %add_convert_fusion.2), channel_id=1, source_target_pairs={{0,16},{16,24},{24,8},{8,0},{1,17},{17,25},{25,9},{9,1},{2,18},{18... | collective-permute-start | bytes 663560 | tf_op jit(solution)/shard_map/ppermute | solution.py:58
  53.4 8.8 %collective-permute-start.21 = (bf16[432,256]{1,0:T(8,128)(2,1)S(1)}, bf16[432,256]{1,0:T(8,128)(2,1)S(1)}, u32[]{:S(2)}, u32[]{:S(2)}) collective-permute-start(bf16[432,256]{1,0:T(8,128)(2,1)S(1)} %add_convert_fusion), channel_id=1, source_target_pairs={{0,16},{16,24},{24,8},{8,0},{1,17},{17,25},{25,9},{9,1},{2,18},{18... | collective-permute-start | bytes 663560 | tf_op jit(solution)/shard_map/ppermute | solution.py:58
  63.9 18.1 %copy-start.5 = (bf16[432,256]{1,0:T(8,128)(2,1)}, bf16[432,256]{1,0:T(8,128)(2,1)S(1)}, u32[]{:S(2)}) copy-start(bf16[432,256]{1,0:T(8,128)(2,1)S(1)} %get-tuple-element.33) | copy-start | bytes 663556
  63.9 9.1 %collective-permute-start.22 = (bf16[432,256]{1,0:T(8,128)(2,1)S(1)}, bf16[432,256]{1,0:T(8,128)(2,1)S(1)}, u32[]{:S(2)}, u32[]{:S(2)}) collective-permute-start(bf16[432,256]{1,0:T(8,128)(2,1)S(1)} %get-tuple-element.33), channel_id=1, source_target_pairs={{0,16},{16,24},{24,8},{8,0},{1,17},{17,25},{25,9},{9,1},{2,18},{18... | collective-permute-start | bytes 663560 | tf_op jit(solution)/shard_map/ppermute | solution.py:58
  67.1 10.6 %collective-permute-start.23 = (bf16[432,256]{1,0:T(8,128)(2,1)S(1)}, bf16[432,256]{1,0:T(8,128)(2,1)S(1)}, u32[]{:S(2)}, u32[]{:S(2)}) collective-permute-start(bf16[432,256]{1,0:T(8,128)(2,1)S(1)} %get-tuple-element.21), channel_id=1, source_target_pairs={{0,16},{16,24},{24,8},{8,0},{1,17},{17,25},{25,9},{9,1},{2,18},{18... | collective-permute-start | bytes 663560 | tf_op jit(solution)/shard_map/ppermute | solution.py:58
  73.0 9.5 %collective-permute-start.24 = (bf16[432,256]{1,0:T(8,128)(2,1)S(1)}, bf16[432,256]{1,0:T(8,128)(2,1)S(1)}, u32[]{:S(2)}, u32[]{:S(2)}) collective-permute-start(bf16[432,256]{1,0:T(8,128)(2,1)S(1)} %collective-permute-done.22), channel_id=1, source_target_pairs={{0,16},{16,24},{24,8},{8,0},{1,17},{17,25},{25,9},{9,1},{2,18},{18... | collective-permute-start | bytes 663560 | tf_op jit(solution)/shard_map/ppermute | solution.py:58
  77.7 7.9 %collective-permute-start.25 = (bf16[432,256]{1,0:T(8,128)(2,1)S(1)}, bf16[432,256]{1,0:T(8,128)(2,1)S(1)}, u32[]{:S(2)}, u32[]{:S(2)}) collective-permute-start(bf16[432,256]{1,0:T(8,128)(2,1)S(1)} %collective-permute-done.23), channel_id=1, source_target_pairs={{0,16},{16,24},{24,8},{8,0},{1,17},{17,25},{25,9},{9,1},{2,18},{18... | collective-permute-start | bytes 663560 | tf_op jit(solution)/shard_map/ppermute | solution.py:58
  81.1 5.4 %copy-start.1 = (bf16[864,256]{1,0:T(8,128)(2,1)}, bf16[864,256]{1,0:T(8,128)(2,1)S(1)}, u32[]{:S(2)}) copy-start(bf16[864,256]{1,0:T(8,128)(2,1)S(1)} %constant_dynamic-update-slice_fusion) | copy-start | bytes 1327108
  85.7 0.9 copy-start.3
  88.0 5.7 %collective-permute-start.26 = (bf16[3,2,32,1280]{3,2,0,1:T(8,128)(2,1)}, bf16[3,2,32,1280]{3,2,0,1:T(8,128)(2,1)}, u32[]{:S(2)}, u32[]{:S(2)}) collective-permute-start(bf16[3,2,32,1280]{3,2,0,1:T(8,128)(2,1)} %get-tuple-element.19), channel_id=1, source_target_pairs={{0,1},{1,0},{2,3},{3,2},{4,5},{5,4},{6,7},{7,6},{8,9},{9,8},{10,11... | collective-permute-start | bytes 1474568 | tf_op jit(solution)/shard_map/ppermute | solution.py:54
  88.0 5.7 %collective-permute-start.27 = (bf16[3,2,32,1280]{3,2,0,1:T(8,128)(2,1)}, bf16[3,2,32,1280]{3,2,0,1:T(8,128)(2,1)}, u32[]{:S(2)}, u32[]{:S(2)}) collective-permute-start(bf16[3,2,32,1280]{3,2,0,1:T(8,128)(2,1)} %get-tuple-element.20), channel_id=1, source_target_pairs={{0,1},{1,0},{2,3},{3,2},{4,5},{5,4},{6,7},{7,6},{8,9},{9,8},{10,11... | collective-permute-start | bytes 1474568 | tf_op jit(solution)/shard_map/ppermute | solution.py:54
  90.4 13.3 %collective-permute-start.33 = (bf16[864,256]{1,0:T(8,128)(2,1)}, bf16[864,256]{1,0:T(8,128)(2,1)S(1)}, u32[]{:S(2)}, u32[]{:S(2)}) collective-permute-start(bf16[864,256]{1,0:T(8,128)(2,1)} %copy-done.3), channel_id=1, source_target_pairs={{0,16},{16,24},{24,8},{8,0},{1,17},{17,25},{25,9},{9,1},{2,18},{18... | collective-permute-start | bytes 1327112 | tf_op jit(solution)/shard_map/ppermute | solution.py:58
  95.3 9.4 %collective-permute-start.28 = (bf16[3,32,1280]{2,1,0:T(8,128)(2,1)S(1)}, bf16[3,32,1280]{2,1,0:T(8,128)(2,1)S(1)}, u32[]{:S(2)}, u32[]{:S(2)}) collective-permute-start(bf16[3,32,1280]{2,1,0:T(8,128)(2,1)S(1)} %get-tuple-element.9), channel_id=1, source_target_pairs={{0,2},{1,3},{2,0},{3,1},{4,6},{5,7},{6,4},{7,5},{8,10},{9,11},{10,... | collective-permute-start | bytes 737288 | tf_op jit(solution)/shard_map/ppermute | solution.py:54
  96.4 12.6 %collective-permute-start.29 = (bf16[3,32,1280]{2,1,0:T(8,128)(2,1)S(1)}, bf16[3,32,1280]{2,1,0:T(8,128)(2,1)S(1)}, u32[]{:S(2)}, u32[]{:S(2)}) collective-permute-start(bf16[3,32,1280]{2,1,0:T(8,128)(2,1)S(1)} %get-tuple-element.11), channel_id=1, source_target_pairs={{0,4},{1,5},{2,6},{3,7},{4,0},{5,1},{6,2},{7,3},{8,12},{9,13},{10,... | collective-permute-start | bytes 737288 | tf_op jit(solution)/shard_map/ppermute | solution.py:54
  96.7 12.3 %collective-permute-start.30 = (bf16[3,32,1280]{2,1,0:T(8,128)(2,1)S(1)}, bf16[3,32,1280]{2,1,0:T(8,128)(2,1)S(1)}, u32[]{:S(2)}, u32[]{:S(2)}) collective-permute-start(bf16[3,32,1280]{2,1,0:T(8,128)(2,1)S(1)} %get-tuple-element.10), channel_id=1, source_target_pairs={{0,6},{1,7},{2,4},{3,5},{4,2},{5,3},{6,0},{7,1},{8,14},{9,15},{10,... | collective-permute-start | bytes 737288 | tf_op jit(solution)/shard_map/ppermute | solution.py:54
  104.6 12.9 %copy-start.2 = (bf16[864,256]{1,0:T(8,128)(2,1)S(1)}, bf16[864,256]{1,0:T(8,128)(2,1)}, u32[]{:S(2)}) copy-start(bf16[864,256]{1,0:T(8,128)(2,1)} %copy-done.1) | copy-start | bytes 1327108
  104.6 12.9 %copy-start.4 = (bf16[864,256]{1,0:T(8,128)(2,1)S(1)}, bf16[864,256]{1,0:T(8,128)(2,1)}, u32[]{:S(2)}) copy-start(bf16[864,256]{1,0:T(8,128)(2,1)} %copy-done.3) | copy-start | bytes 1327108
  104.6 12.9 %copy-start.6 = (bf16[432,256]{1,0:T(8,128)(2,1)S(1)}, bf16[432,256]{1,0:T(8,128)(2,1)}, u32[]{:S(2)}) copy-start(bf16[432,256]{1,0:T(8,128)(2,1)} %copy-done.5) | copy-start | bytes 663556
  104.6 12.9 %copy-start.8 = (bf16[32,8,2,640]{3,1,2,0:T(8,128)(2,1)S(1)}, bf16[32,8,2,640]{3,1,2,0:T(8,128)(2,1)}, u32[]{:S(2)}) copy-start(bf16[32,8,2,640]{3,1,2,0:T(8,128)(2,1)} %copy-done.7) | copy-start | bytes 1966084
  104.6 12.9 %copy-start.10 = (bf16[32,8,2,640]{3,1,2,0:T(8,128)(2,1)S(1)}, bf16[32,8,2,640]{3,1,2,0:T(8,128)(2,1)}, u32[]{:S(2)}) copy-start(bf16[32,8,2,640]{3,1,2,0:T(8,128)(2,1)} %copy-done.9) | copy-start | bytes 1966084
  104.6 12.9 %copy-start.12 = (bf16[32,8,2,640]{3,1,2,0:T(8,128)(2,1)S(1)}, bf16[32,8,2,640]{3,1,2,0:T(8,128)(2,1)}, u32[]{:S(2)}) copy-start(bf16[32,8,2,640]{3,1,2,0:T(8,128)(2,1)} %copy-done.11) | copy-start | bytes 1966084
  104.6 12.9 %copy-start.14 = (bf16[32,8,2,640]{3,1,2,0:T(8,128)(2,1)S(1)}, bf16[32,8,2,640]{3,1,2,0:T(8,128)(2,1)}, u32[]{:S(2)}) copy-start(bf16[32,8,2,640]{3,1,2,0:T(8,128)(2,1)} %copy-done.13) | copy-start | bytes 1966084
  104.6 4.5 %collective-permute-start.34 = (bf16[1,4,32,1280]{3,2,1,0:T(8,128)(2,1)S(1)}, bf16[1,4,32,1280]{3,2,1,0:T(8,128)(2,1)S(1)}, u32[]{:S(2)}, u32[]{:S(2)}) collective-permute-start(bf16[1,4,32,1280]{3,2,1,0:T(8,128)(2,1)S(1)} %dynamic-slice_bitcast_fusion), channel_id=1, source_target_pairs={{0,1},{1,0},{2,3},{3,2},{4,5},{5,4},{6,7},{7,6},{8,9},{9,8},{10,11... | collective-permute-start | bytes 983048 | tf_op jit(solution)/shard_map/ppermute | solution.py:54
  109.3 6.1 %collective-permute-start.35 = (bf16[1,32,1280]{2,1,0:T(8,128)(2,1)S(1)}, bf16[1,32,1280]{2,1,0:T(8,128)(2,1)S(1)}, u32[]{:S(2)}, u32[]{:S(2)}) collective-permute-start(bf16[1,32,1280]{2,1,0:T(8,128)(2,1)S(1)} %get-tuple-element.25), channel_id=1, source_target_pairs={{0,2},{1,3},{2,0},{3,1},{4,6},{5,7},{6,4},{7,5},{8,10},{9,11},{10,... | collective-permute-start | bytes 245768 | tf_op jit(solution)/shard_map/ppermute | solution.py:54
  110.2 5.1 %collective-permute-start.36 = (bf16[1,32,1280]{2,1,0:T(8,128)(2,1)S(1)}, bf16[1,32,1280]{2,1,0:T(8,128)(2,1)S(1)}, u32[]{:S(2)}, u32[]{:S(2)}) collective-permute-start(bf16[1,32,1280]{2,1,0:T(8,128)(2,1)S(1)} %get-tuple-element.27), channel_id=1, source_target_pairs={{0,4},{1,5},{2,6},{3,7},{4,0},{5,1},{6,2},{7,3},{8,12},{9,13},{10,... | collective-permute-start | bytes 245768 | tf_op jit(solution)/shard_map/ppermute | solution.py:54
  111.1 5.3 %collective-permute-start.37 = (bf16[1,32,1280]{2,1,0:T(8,128)(2,1)S(1)}, bf16[1,32,1280]{2,1,0:T(8,128)(2,1)S(1)}, u32[]{:S(2)}, u32[]{:S(2)}) collective-permute-start(bf16[1,32,1280]{2,1,0:T(8,128)(2,1)S(1)} %get-tuple-element.26), channel_id=1, source_target_pairs={{0,6},{1,7},{2,4},{3,5},{4,2},{5,3},{6,0},{7,1},{8,14},{9,15},{10,... | collective-permute-start | bytes 245768 | tf_op jit(solution)/shard_map/ppermute | solution.py:54
  112.9 9.2 %collective-permute-start.31 = (bf16[32,1280]{1,0:T(8,128)(2,1)S(1)}, bf16[32,1280]{1,0:T(8,128)(2,1)S(1)}, u32[]{:S(2)}, u32[]{:S(2)}) collective-permute-start(bf16[32,1280]{1,0:T(8,128)(2,1)S(1)} %get-tuple-element.43), channel_id=1, source_target_pairs={{0,8},{16,0},{24,16},{8,24},{1,9},{17,1},{25,17},{9,25},{2,10},{18... | collective-permute-start | bytes 245768 | tf_op jit(solution)/shard_map/ppermute | solution.py:58
  113.5 8.6 %collective-permute-start.32 = (bf16[32,1280]{1,0:T(8,128)(2,1)S(1)}, bf16[32,1280]{1,0:T(8,128)(2,1)S(1)}, u32[]{:S(2)}, u32[]{:S(2)}) collective-permute-start(bf16[32,1280]{1,0:T(8,128)(2,1)S(1)} %get-tuple-element.42), channel_id=1, source_target_pairs={{0,24},{16,8},{24,0},{8,16},{1,25},{17,9},{25,1},{9,17},{2,26},{18... | collective-permute-start | bytes 245768 | tf_op jit(solution)/shard_map/ppermute | solution.py:58
  116.5 5.6 %collective-permute-start.38 = (bf16[32,1280]{1,0:T(8,128)(2,1)S(1)}, bf16[32,1280]{1,0:T(8,128)(2,1)S(1)}, u32[]{:S(2)}, u32[]{:S(2)}) collective-permute-start(bf16[32,1280]{1,0:T(8,128)(2,1)S(1)} %fusion.61), channel_id=1, source_target_pairs={{0,16},{16,24},{24,8},{8,0},{1,17},{17,25},{25,9},{9,1},{2,18},{18... | collective-permute-start | bytes 245768 | tf_op jit(solution)/shard_map/ppermute | solution.py:58

commit v4 on v3

--- a/solution.py
+++ b/solution.py
@@ -5,7 +5,6 @@
 
 grad_scale = 0.015625
 cores = 2
-streams = 2
 
 
 def gelu_tanh(value):
@@ -39,7 +38,7 @@
     tok, width = activations.shape
     sub = tok // n_col
     depth, units = up_weight.shape
-    cut = units // streams
+    cuts = [0, (units // 2 - 32) // 16 * 16, units]
     flipped = up_weight.T
 
     plane_at = list(range(0, n_row, 2)) + list(range(1, n_row, 2))[::-1]
@@ -58,7 +57,7 @@
         return lax.ppermute(array, "row", pairs)
 
     def split(array):
-        return [array[i * cut:(i + 1) * cut] for i in range(streams)]
+        return [array[a:b] for a, b in zip(cuts, cuts[1:])]
 
     halved = depth == cores * width
     if halved:
@@ -133,9 +132,9 @@
     ring = [slopes]
     for k in range(1, n_row):
         if k < n_row - 1:
-            ring.append([along(s, 1) for s in ring[-1]])
+            ring.append([along(s, n_row - 1) for s in ring[-1]])
         else:
-            ring.append(split(along(jnp.concatenate(ring[-1]), 1)))
+            ring.append(split(along(jnp.concatenate(ring[-1]), n_row - 1)))
 
     def meet(blocks):
         terms = [narrow(product(jnp.concatenate(b), flipped, ((0,), (0,)))) for b in blocks]
@@ -161,7 +160,9 @@
 
     pieces = [exchange(meet(ring[:-1])), exchange(meet(ring[-1:]))]
     sums = finish(pieces[0]) + finish(pieces[1])
-    placed = [sums[0]] + [along(sums[k], n_row - k) for k in range(1, n_row)]
+    placed = [None] * n_row
+    for k in range(n_row):
+        placed[(n_row - k) % n_row] = along(sums[k], k) if k else sums[k]
     step = 1
     while step < n_row:
         turned = [placed[(k - step) % n_row] for k in range(n_row)]
@@ -171,7 +172,7 @@
 
     whole = [jnp.concatenate(s) for s in ring]
     weight_grad = product(
-        jnp.concatenate(whole[1:] + whole[:1], axis=1), jnp.concatenate(tokens, axis=0), ((1,), (0,))
+        jnp.concatenate(whole[:0:-1] + whole[:1], axis=1), jnp.concatenate(tokens, axis=0), ((1,), (0,))
     )
     return (hidden, input_grad, (weight_grad * grad_scale).T)
 

time: 123 us -> 119 us (0.967)
  starting transfers between devices: 55.1 us -> 46.8 us
  waiting for transfers between devices: 39.3 us -> 43.5 us
    ppermute x17, starting transfers between devices: 35.1 us -> 26.8 us  [along(): return lax.ppermute(array, 'row', pairs)]
    ppermute x17, waiting for transfers between devices: 24.2 us -> 30.5 us  [along(): return lax.ppermute(array, 'row', pairs)]
    ppermute x22, waiting for transfers between devices: 15.1 us -> 13 us  [across(): return lax.ppermute(array, 'col', [(i, i ^ flip) for i in range(n_col)])]
  transfers between devices with their start and end apart: 39 -> 39, of which waited for: 20 -> 21; matrix products, arithmetic and copies ran while one was open for 15% -> 17% of each run, Pallas kernels for 0% -> 0%
where the time goes in v4:
time: 119 us
  starting transfers between devices  46.8 us (39%)
  waiting for transfers between devices  43.5 us (37%)
  matrix products  11.9 us (10%)
  other arithmetic  6.6 us (6%)
  local copies, waits for them, and re-layouts  6.17 us (5%)
  blocking collectives  2.28 us (2%)
  between operations  1.35 us (1%)
    ppermute x17, waiting for transfers between devices, along(): return lax.ppermute(array, 'row', pairs)  30.5 us
    ppermute x17, starting transfers between devices, along(): return lax.ppermute(array, 'row', pairs)  26.8 us
    ppermute x22, starting transfers between devices, across(): return lax.ppermute(array, 'col', [(i, i ^ flip) for i in range(n_col)])  20.1 us
    ppermute x22, waiting for transfers between devices, across(): return lax.ppermute(array, 'col', [(i, i ^ flip) for i in range(n_col)])  13 us
    dot_general x13, matrix products, product(): lax.dot_general(left, right, (axes, ((), ())), preferred_element_type=jnp...  11.9 us
  transfers between devices with their start and end apart: 39, of which 21 were waited for; matrix products, arithmetic and copies ran while one was open for 17% of the time, Pallas kernels for 0%

profile of v4, /device:TPU:0, one launch (start us, length us, event | category | flops | bytes accessed | tf_op | source)
XLA Modules:
  0.0 118.7 jit_solution(9114587741253598150)
XLA Ops:
  0.7 1.0 constant_dynamic-slice_fusion.2
  1.7 3.0 %collective-permute-start = (bf16[64,640]{1,0:T(8,128)(2,1)S(1)}, bf16[64,640]{1,0:T(8,128)(2,1)S(1)}, u32[]{:S(2)}, u32[]{:S(2)}) collective-permute-start(bf16[64,640]{1,0:T(8,128)(2,1)S(1)} %get-tuple-element.39), channel_id=1, source_target_pairs={{0,2},{1,3},{2,0},{3,1},{4,6},{5,7},{6,4},{7,5},{8,10},{9,11},{10,... | collective-permute-start | bytes 245768 | tf_op jit(solution)/shard_map/ppermute | solution.py:53
  4.7 1.5 %collective-permute-start.1 = (bf16[64,640]{1,0:T(8,128)(2,1)S(1)}, bf16[64,640]{1,0:T(8,128)(2,1)S(1)}, u32[]{:S(2)}, u32[]{:S(2)}) collective-permute-start(bf16[64,640]{1,0:T(8,128)(2,1)S(1)} %get-tuple-element.38), channel_id=1, source_target_pairs={{0,4},{1,5},{2,6},{3,7},{4,0},{5,1},{6,2},{7,3},{8,12},{9,13},{10,... | collective-permute-start | bytes 245768 | tf_op jit(solution)/shard_map/ppermute | solution.py:53
  6.3 1.2 collective-permute-done
  7.4 2.6 %collective-permute-done.1 = bf16[64,640]{1,0:T(8,128)(2,1)S(1)} collective-permute-done((bf16[64,640]{1,0:T(8,128)(2,1)S(1)}, bf16[64,640]{1,0:T(8,128)(2,1)S(1)}, u32[]{:S(2)}, u32[]{:S(2)}) %collective-permute-start.1) | collective-permute-done | bytes 81952 | tf_op jit(solution)/shard_map/ppermute | solution.py:53
  10.0 1.5 %collective-permute-done.2 = bf16[64,640]{1,0:T(8,128)(2,1)S(1)} collective-permute-done((bf16[64,640]{1,0:T(8,128)(2,1)S(1)}, bf16[64,640]{1,0:T(8,128)(2,1)S(1)}, u32[]{:S(2)}, u32[]{:S(2)}) %collective-permute-start.2) | collective-permute-done | bytes 81952 | tf_op jit(solution)/shard_map/ppermute | solution.py:53
  11.7 2.6 %collective-permute-start.3 = (bf16[64,640]{1,0:T(8,128)(2,1)S(1)}, bf16[64,640]{1,0:T(8,128)(2,1)S(1)}, u32[]{:S(2)}, u32[]{:S(2)}) collective-permute-start(bf16[64,640]{1,0:T(8,128)(2,1)S(1)} %get-tuple-element.32), channel_id=1, source_target_pairs={{0,16},{16,24},{24,8},{8,0},{1,17},{17,25},{25,9},{9,1},{2,18},{18... | collective-permute-start | bytes 245768 | tf_op jit(solution)/shard_map/ppermute | solution.py:57
  14.3 1.3 %collective-permute-start.8 = (bf16[64,640]{1,0:T(8,128)(2,1)S(1)}, bf16[64,640]{1,0:T(8,128)(2,1)S(1)}, u32[]{:S(2)}, u32[]{:S(2)}) collective-permute-start(bf16[64,640]{1,0:T(8,128)(2,1)S(1)} %get-tuple-element.35), channel_id=1, source_target_pairs={{0,24},{16,8},{24,0},{8,16},{1,25},{17,9},{25,1},{9,17},{2,26},{18... | collective-permute-start | bytes 245768 | tf_op jit(solution)/shard_map/ppermute | solution.py:57
  15.7 0.8 collective-permute-start.9
  16.5 0.9 collective-permute-start.4
  17.4 0.6 collective-permute-start.5
  18.0 1.9 %collective-permute-start.6 = (bf16[1,64,640]{2,1,0:T(8,128)(2,1)S(1)}, bf16[1,64,640]{2,1,0:T(8,128)(2,1)S(1)}, u32[]{:S(2)}, u32[]{:S(2)}) collective-permute-start(bf16[1,64,640]{2,1,0:T(8,128)(2,1)S(1)} %bitcast.232), channel_id=1, source_target_pairs={{0,6},{1,7},{2,4},{3,5},{4,2},{5,3},{6,0},{7,1},{8,14},{9,15},{10,... | collective-permute-start | bytes 245768 | tf_op jit(solution)/shard_map/ppermute | solution.py:53
  20.0 0.7 collective-permute-done.8
  20.7 1.3 %collective-permute-done.9 = bf16[64,640]{1,0:T(8,128)(2,1)S(1)} collective-permute-done((bf16[64,640]{1,0:T(8,128)(2,1)S(1)}, bf16[64,640]{1,0:T(8,128)(2,1)S(1)}, u32[]{:S(2)}, u32[]{:S(2)}) %collective-permute-start.9) | collective-permute-done | bytes 81952 | tf_op jit(solution)/shard_map/ppermute | solution.py:57
  22.1 1.1 collective-permute-start.10
  23.1 0.6 collective-permute-start.11
  23.8 1.9 %collective-permute-start.12 = (bf16[3,64,640]{2,1,0:T(8,128)(2,1)S(1)}, bf16[3,64,640]{2,1,0:T(8,128)(2,1)S(1)}, u32[]{:S(2)}, u32[]{:S(2)}) collective-permute-start(bf16[3,64,640]{2,1,0:T(8,128)(2,1)S(1)} %pad_maximum_fusion.4), channel_id=1, source_target_pairs={{0,6},{1,7},{2,4},{3,5},{4,2},{5,3},{6,0},{7,1},{8,14},{9,15},{10,... | collective-permute-start | bytes 737288 | tf_op jit(solution)/shard_map/ppermute | solution.py:53
  25.8 2.3 %all_gather.19 = bf16[1,4,64,2,640]{4,2,1,0,3:T(8,128)(2,1)S(1)} all-gather(bf16[1,4,64,1,640]{4,2,1,0,3:T(8,128)(2,1)S(1)} %bitcast_dynamic-update-slice_fusion.8), channel_id=1, replica_groups={{0,1},{2,3},{4,5},{6,7},{8,9},{10,11},{12,13},{14,15},{16,17},{18,19},{..., dimensions={3}, use_global_device_ids=true | all-gather | bytes 983040 | tf_op jit(solution)/shard_map/all_gather | solution.py:99
  28.0 0.7 copy.47
  30.0 2.5 %collective-permute-start.7 = (bf16[400,256]{1,0:T(8,128)(2,1)S(1)}, bf16[400,256]{1,0:T(8,128)(2,1)S(1)}, u32[]{:S(2)}, u32[]{:S(2)}) collective-permute-start(bf16[400,256]{1,0:T(8,128)(2,1)S(1)} %fusion.17), channel_id=1, source_target_pairs={{0,16},{16,24},{24,8},{8,0},{1,17},{17,25},{25,9},{9,1},{2,18},{18... | collective-permute-start | bytes 614408 | tf_op jit(solution)/shard_map/ppermute | solution.py:57
  32.4 0.9 collective-permute-start.19
  33.3 3.1 %collective-permute-done.11 = bf16[3,64,640]{2,1,0:T(8,128)(2,1)S(1)} collective-permute-done((bf16[3,64,640]{2,1,0:T(8,128)(2,1)S(1)}, bf16[3,64,640]{2,1,0:T(8,128)(2,1)S(1)}, u32[]{:S(2)}, u32[]{:S(2)}) %collective-permute-start.11) | collective-permute-done | bytes 245792 | tf_op jit(solution)/shard_map/ppermute | solution.py:53
  37.3 0.6 collective-permute-done.14
  39.1 0.7 copy.55
  40.4 2.3 %collective-permute-start.17 = (bf16[400,256]{1,0:T(8,128)(2,1)S(1)}, bf16[400,256]{1,0:T(8,128)(2,1)S(1)}, u32[]{:S(2)}, u32[]{:S(2)}) collective-permute-start(bf16[400,256]{1,0:T(8,128)(2,1)S(1)} %add_convert_fusion.3), channel_id=1, source_target_pairs={{0,16},{16,24},{24,8},{8,0},{1,17},{17,25},{25,9},{9,1},{2,18},{18... | collective-permute-start | bytes 614408 | tf_op jit(solution)/shard_map/ppermute | solution.py:57
  42.7 0.7 copy.56
  43.5 0.7 copy.57
  45.8 0.7 collective-permute-start.20
  47.5 0.7 collective-permute-done.17
  48.2 3.4 %collective-permute-start.18 = (bf16[400,256]{1,0:T(8,128)(2,1)S(1)}, bf16[400,256]{1,0:T(8,128)(2,1)S(1)}, u32[]{:S(2)}, u32[]{:S(2)}) collective-permute-start(bf16[400,256]{1,0:T(8,128)(2,1)S(1)} %add_convert_fusion.2), channel_id=1, source_target_pairs={{0,16},{16,24},{24,8},{8,0},{1,17},{17,25},{25,9},{9,1},{2,18},{18... | collective-permute-start | bytes 614408 | tf_op jit(solution)/shard_map/ppermute | solution.py:57
  51.7 2.9 %collective-permute-done.20 = bf16[464,256]{1,0:T(8,128)(2,1)S(1)} collective-permute-done((bf16[464,256]{1,0:T(8,128)(2,1)S(1)}, bf16[464,256]{1,0:T(8,128)(2,1)S(1)}, u32[]{:S(2)}, u32[]{:S(2)}) %collective-permute-start.20) | collective-permute-done | bytes 237600 | tf_op jit(solution)/shard_map/ppermute | solution.py:57
  54.6 2.2 %collective-permute-start.21 = (bf16[464,256]{1,0:T(8,128)(2,1)S(1)}, bf16[464,256]{1,0:T(8,128)(2,1)S(1)}, u32[]{:S(2)}, u32[]{:S(2)}) collective-permute-start(bf16[464,256]{1,0:T(8,128)(2,1)S(1)} %add_convert_fusion), channel_id=1, source_target_pairs={{0,16},{16,24},{24,8},{8,0},{1,17},{17,25},{25,9},{9,1},{2,18},{18... | collective-permute-start | bytes 712712 | tf_op jit(solution)/shard_map/ppermute | solution.py:57
  56.7 2.2 %collective-permute-done.18 = bf16[400,256]{1,0:T(8,128)(2,1)S(1)} collective-permute-done((bf16[400,256]{1,0:T(8,128)(2,1)S(1)}, bf16[400,256]{1,0:T(8,128)(2,1)S(1)}, u32[]{:S(2)}, u32[]{:S(2)}) %collective-permute-start.18) | collective-permute-done | bytes 204832 | tf_op jit(solution)/shard_map/ppermute | solution.py:57
  58.9 1.1 fusion.47
  60.0 1.4 %collective-permute-start.22 = (bf16[400,256]{1,0:T(8,128)(2,1)S(1)}, bf16[400,256]{1,0:T(8,128)(2,1)S(1)}, u32[]{:S(2)}, u32[]{:S(2)}) collective-permute-start(bf16[400,256]{1,0:T(8,128)(2,1)S(1)} %get-tuple-element.26), channel_id=1, source_target_pairs={{0,8},{16,0},{24,16},{8,24},{1,9},{17,1},{25,17},{9,25},{2,10},{18... | collective-permute-start | bytes 614408 | tf_op jit(solution)/shard_map/ppermute | solution.py:57
  61.4 1.7 %collective-permute-done.21 = bf16[464,256]{1,0:T(8,128)(2,1)S(1)} collective-permute-done((bf16[464,256]{1,0:T(8,128)(2,1)S(1)}, bf16[464,256]{1,0:T(8,128)(2,1)S(1)}, u32[]{:S(2)}, u32[]{:S(2)}) %collective-permute-start.21) | collective-permute-done | bytes 237600 | tf_op jit(solution)/shard_map/ppermute | solution.py:57
  63.6 2.6 %collective-permute-start.24 = (bf16[464,256]{1,0:T(8,128)(2,1)S(1)}, bf16[464,256]{1,0:T(8,128)(2,1)S(1)}, u32[]{:S(2)}, u32[]{:S(2)}) collective-permute-start(bf16[464,256]{1,0:T(8,128)(2,1)S(1)} %get-tuple-element.21), channel_id=1, source_target_pairs={{0,8},{16,0},{24,16},{8,24},{1,9},{17,1},{25,17},{9,25},{2,10},{18... | collective-permute-start | bytes 712712 | tf_op jit(solution)/shard_map/ppermute | solution.py:57
  66.2 0.9 convolution_convert_fusion.2
  67.1 2.1 %collective-permute-done.22 = bf16[400,256]{1,0:T(8,128)(2,1)S(1)} collective-permute-done((bf16[400,256]{1,0:T(8,128)(2,1)S(1)}, bf16[400,256]{1,0:T(8,128)(2,1)S(1)}, u32[]{:S(2)}, u32[]{:S(2)}) %collective-permute-start.22) | collective-permute-done | bytes 204832 | tf_op jit(solution)/shard_map/ppermute | solution.py:57
  69.2 0.7 collective-permute-start.23
  69.9 4.4 %collective-permute-done.24 = bf16[464,256]{1,0:T(8,128)(2,1)S(1)} collective-permute-done((bf16[464,256]{1,0:T(8,128)(2,1)S(1)}, bf16[464,256]{1,0:T(8,128)(2,1)S(1)}, u32[]{:S(2)}, u32[]{:S(2)}) %collective-permute-start.24) | collective-permute-done | bytes 237600 | tf_op jit(solution)/shard_map/ppermute | solution.py:57
  74.3 0.7 collective-permute-start.25
  75.0 0.9 convolution_convert_fusion.1
  75.9 2.8 %collective-permute-done.23 = bf16[400,256]{1,0:T(8,128)(2,1)S(1)} collective-permute-done((bf16[400,256]{1,0:T(8,128)(2,1)S(1)}, bf16[400,256]{1,0:T(8,128)(2,1)S(1)}, u32[]{:S(2)}, u32[]{:S(2)}) %collective-permute-start.23) | collective-permute-done | bytes 204832 | tf_op jit(solution)/shard_map/ppermute | solution.py:57
  78.7 4.4 %collective-permute-done.25 = bf16[464,256]{1,0:T(8,128)(2,1)S(1)} collective-permute-done((bf16[464,256]{1,0:T(8,128)(2,1)S(1)}, bf16[464,256]{1,0:T(8,128)(2,1)S(1)}, u32[]{:S(2)}, u32[]{:S(2)}) %collective-permute-start.25) | collective-permute-done | bytes 237600 | tf_op jit(solution)/shard_map/ppermute | solution.py:57
  83.1 0.9 convolution_convert_fusion
  84.5 1.0 fusion.64
  86.0 1.7 %maximum_bitcast_fusion = bf16[256,864]{0,1:T(8,128)(2,1)} fusion(bf16[464,256]{1,0:T(8,128)(2,1)S(1)} %get-tuple-element.22, bf16[400,256]{1,0:T(8,128)(2,1)} %get-tuple-element.27), kind=kLoop, calls=%fused_computation.85 | loop fusion | flops 884736 | bytes 884736 | tf_op jit(solution)/shard_map/transpose | solution.py:130
  88.4 1.4 %convert_add_fusion = f32[3,4,32,1280]{3,2,0,1:T(8,128)S(1)} fusion(bf16[3,2,32,1280]{3,2,0,1:T(8,128)(2,1)} %collective-permute-done.33, bf16[3,2,32,1280]{3,2,0,1:T(8,128)(2,1)} %collective-permute-done.32, bf16[3,4,1,32,1280]{4,3,2,1,0:T(8,128)(2,1)S(1)} %get-tuple-element.12), kind=kLoop, calls=%fused_computation.17 | loop fusion | flops 1966080 | bytes 3932160 | tf_op jit(solution)/shard_map/add | solution.py:148
  90.0 1.5 %collective-permute-start.34 = (bf16[3,32,1280]{2,1,0:T(8,128)(2,1)S(1)}, bf16[3,32,1280]{2,1,0:T(8,128)(2,1)S(1)}, u32[]{:S(2)}, u32[]{:S(2)}) collective-permute-start(bf16[3,32,1280]{2,1,0:T(8,128)(2,1)S(1)} %get-tuple-element.9), channel_id=1, source_target_pairs={{0,2},{1,3},{2,0},{3,1},{4,6},{5,7},{6,4},{7,5},{8,10},{9,11},{10,... | collective-permute-start | bytes 737288 | tf_op jit(solution)/shard_map/ppermute | solution.py:53
  91.4 0.6 collective-permute-start.35
  92.0 1.5 %collective-permute-start.36 = (bf16[3,32,1280]{2,1,0:T(8,128)(2,1)S(1)}, bf16[3,32,1280]{2,1,0:T(8,128)(2,1)S(1)}, u32[]{:S(2)}, u32[]{:S(2)}) collective-permute-start(bf16[3,32,1280]{2,1,0:T(8,128)(2,1)S(1)} %get-tuple-element.10), channel_id=1, source_target_pairs={{0,6},{1,7},{2,4},{3,5},{4,2},{5,3},{6,0},{7,1},{8,14},{9,15},{10,... | collective-permute-start | bytes 737288 | tf_op jit(solution)/shard_map/ppermute | solution.py:53
  93.5 7.4 %collective-permute-done.26 = bf16[864,256]{1,0:T(8,128)(2,1)S(1)} collective-permute-done((bf16[864,256]{1,0:T(8,128)(2,1)}, bf16[864,256]{1,0:T(8,128)(2,1)S(1)}, u32[]{:S(2)}, u32[]{:S(2)}) %collective-permute-start.26) | collective-permute-done | bytes 442400 | tf_op jit(solution)/shard_map/ppermute | solution.py:57
  100.9 0.9 convolution_convert_fusion.3
  102.0 2.4 %collective-permute-done.35 = bf16[3,32,1280]{2,1,0:T(8,128)(2,1)S(1)} collective-permute-done((bf16[3,32,1280]{2,1,0:T(8,128)(2,1)S(1)}, bf16[3,32,1280]{2,1,0:T(8,128)(2,1)S(1)}, u32[]{:S(2)}, u32[]{:S(2)}) %collective-permute-start.35) | collective-permute-done | bytes 245792 | tf_op jit(solution)/shard_map/ppermute | solution.py:53
  104.7 0.7 collective-permute-start.28
  105.4 1.1 collective-permute-start.29
  106.5 1.8 %collective-permute-start.30 = (bf16[1,32,1280]{2,1,0:T(8,128)(2,1)S(1)}, bf16[1,32,1280]{2,1,0:T(8,128)(2,1)S(1)}, u32[]{:S(2)}, u32[]{:S(2)}) collective-permute-start(bf16[1,32,1280]{2,1,0:T(8,128)(2,1)S(1)} %get-tuple-element.24), channel_id=1, source_target_pairs={{0,6},{1,7},{2,4},{3,5},{4,2},{5,3},{6,0},{7,1},{8,14},{9,15},{10,... | collective-permute-start | bytes 245768 | tf_op jit(solution)/shard_map/ppermute | solution.py:53
  108.2 1.9 %collective-permute-start.37 = (bf16[32,1280]{1,0:T(8,128)(2,1)S(1)}, bf16[32,1280]{1,0:T(8,128)(2,1)S(1)}, u32[]{:S(2)}, u32[]{:S(2)}) collective-permute-start(bf16[32,1280]{1,0:T(8,128)(2,1)S(1)} %get-tuple-element.41), channel_id=1, source_target_pairs={{0,24},{16,8},{24,0},{8,16},{1,25},{17,9},{25,1},{9,17},{2,26},{18... | collective-permute-start | bytes 245768 | tf_op jit(solution)/shard_map/ppermute | solution.py:57
  110.2 0.9 collective-permute-start.38
  111.1 0.7 collective-permute-done.30
  111.9 1.4 %collective-permute-start.31 = (bf16[32,1280]{1,0:T(8,128)(2,1)S(1)}, bf16[32,1280]{1,0:T(8,128)(2,1)S(1)}, u32[]{:S(2)}, u32[]{:S(2)}) collective-permute-start(bf16[32,1280]{1,0:T(8,128)(2,1)S(1)} %fusion.61), channel_id=1, source_target_pairs={{0,8},{16,0},{24,16},{8,24},{1,9},{17,1},{25,17},{9,25},{2,10},{18... | collective-permute-start | bytes 245768 | tf_op jit(solution)/shard_map/ppermute | solution.py:57
  113.3 4.5 %convolution_multiply_fusion = f32[1280,864]{0,1:T(8,128)} fusion(bf16[256,1280]{1,0:T(8,128)(2,1)S(1)} %bitcast.219, bf16[256,1280]{1,0:T(8,128)(2,1)S(1)} %bitcast.216, bf16[256,1280]{1,0:T(8,128)(2,1)S(1)} %bitcast.213, bf16[256,1280]{1,0:T(8,128)(2,1)S(1)} %bitcast.210, bf16[464,256]{1,0:T(8,128)(2,1)S(1)} %copy-done.2, ...), kind=kOutput, calls=%fused_computation | convolution fusion | flops 2285363200 | bytes 8814592 | tf_op jit(solution)/shard_map/dot_general | solution.py:31
  117.9 0.7 pad_maximum_fusion.3
  (116 shorter events, 9.6 us)
Async XLA Ops:
  1.7 5.7 %collective-permute-start = (bf16[64,640]{1,0:T(8,128)(2,1)S(1)}, bf16[64,640]{1,0:T(8,128)(2,1)S(1)}, u32[]{:S(2)}, u32[]{:S(2)}) collective-permute-start(bf16[64,640]{1,0:T(8,128)(2,1)S(1)} %get-tuple-element.39), channel_id=1, source_target_pairs={{0,2},{1,3},{2,0},{3,1},{4,6},{5,7},{6,4},{7,5},{8,10},{9,11},{10,... | collective-permute-start | bytes 245768 | tf_op jit(solution)/shard_map/ppermute | solution.py:53
  4.7 5.3 %collective-permute-start.1 = (bf16[64,640]{1,0:T(8,128)(2,1)S(1)}, bf16[64,640]{1,0:T(8,128)(2,1)S(1)}, u32[]{:S(2)}, u32[]{:S(2)}) collective-permute-start(bf16[64,640]{1,0:T(8,128)(2,1)S(1)} %get-tuple-element.38), channel_id=1, source_target_pairs={{0,4},{1,5},{2,6},{3,7},{4,0},{5,1},{6,2},{7,3},{8,12},{9,13},{10,... | collective-permute-start | bytes 245768 | tf_op jit(solution)/shard_map/ppermute | solution.py:53
  6.2 5.3 %collective-permute-start.2 = (bf16[64,640]{1,0:T(8,128)(2,1)S(1)}, bf16[64,640]{1,0:T(8,128)(2,1)S(1)}, u32[]{:S(2)}, u32[]{:S(2)}) collective-permute-start(bf16[64,640]{1,0:T(8,128)(2,1)S(1)} %get-tuple-element.37), channel_id=1, source_target_pairs={{0,6},{1,7},{2,4},{3,5},{4,2},{5,3},{6,0},{7,1},{8,14},{9,15},{10,... | collective-permute-start | bytes 245768 | tf_op jit(solution)/shard_map/ppermute | solution.py:53
  11.7 4.8 %collective-permute-start.3 = (bf16[64,640]{1,0:T(8,128)(2,1)S(1)}, bf16[64,640]{1,0:T(8,128)(2,1)S(1)}, u32[]{:S(2)}, u32[]{:S(2)}) collective-permute-start(bf16[64,640]{1,0:T(8,128)(2,1)S(1)} %get-tuple-element.32), channel_id=1, source_target_pairs={{0,16},{16,24},{24,8},{8,0},{1,17},{17,25},{25,9},{9,1},{2,18},{18... | collective-permute-start | bytes 245768 | tf_op jit(solution)/shard_map/ppermute | solution.py:57
  14.3 6.3 %collective-permute-start.8 = (bf16[64,640]{1,0:T(8,128)(2,1)S(1)}, bf16[64,640]{1,0:T(8,128)(2,1)S(1)}, u32[]{:S(2)}, u32[]{:S(2)}) collective-permute-start(bf16[64,640]{1,0:T(8,128)(2,1)S(1)} %get-tuple-element.35), channel_id=1, source_target_pairs={{0,24},{16,8},{24,0},{8,16},{1,25},{17,9},{25,1},{9,17},{2,26},{18... | collective-permute-start | bytes 245768 | tf_op jit(solution)/shard_map/ppermute | solution.py:57
  15.7 6.3 %collective-permute-start.9 = (bf16[64,640]{1,0:T(8,128)(2,1)S(1)}, bf16[64,640]{1,0:T(8,128)(2,1)S(1)}, u32[]{:S(2)}, u32[]{:S(2)}) collective-permute-start(bf16[64,640]{1,0:T(8,128)(2,1)S(1)} %get-tuple-element.34), channel_id=1, source_target_pairs={{0,8},{16,0},{24,16},{8,24},{1,9},{17,1},{25,17},{9,25},{2,10},{18... | collective-permute-start | bytes 245768 | tf_op jit(solution)/shard_map/ppermute | solution.py:57
  16.5 5.5 %collective-permute-start.4 = (bf16[1,64,640]{2,1,0:T(8,128)(2,1)S(1)}, bf16[1,64,640]{2,1,0:T(8,128)(2,1)S(1)}, u32[]{:S(2)}, u32[]{:S(2)}) collective-permute-start(bf16[1,64,640]{2,1,0:T(8,128)(2,1)S(1)} %bitcast.230), channel_id=1, source_target_pairs={{0,2},{1,3},{2,0},{3,1},{4,6},{5,7},{6,4},{7,5},{8,10},{9,11},{10,... | collective-permute-start | bytes 245768 | tf_op jit(solution)/shard_map/ppermute | solution.py:53
  17.4 6.3 %collective-permute-start.5 = (bf16[1,64,640]{2,1,0:T(8,128)(2,1)S(1)}, bf16[1,64,640]{2,1,0:T(8,128)(2,1)S(1)}, u32[]{:S(2)}, u32[]{:S(2)}) collective-permute-start(bf16[1,64,640]{2,1,0:T(8,128)(2,1)S(1)} %bitcast.231), channel_id=1, source_target_pairs={{0,4},{1,5},{2,6},{3,7},{4,0},{5,1},{6,2},{7,3},{8,12},{9,13},{10,... | collective-permute-start | bytes 245768 | tf_op jit(solution)/shard_map/ppermute | solution.py:53
  18.0 7.7 %collective-permute-start.6 = (bf16[1,64,640]{2,1,0:T(8,128)(2,1)S(1)}, bf16[1,64,640]{2,1,0:T(8,128)(2,1)S(1)}, u32[]{:S(2)}, u32[]{:S(2)}) collective-permute-start(bf16[1,64,640]{2,1,0:T(8,128)(2,1)S(1)} %bitcast.232), channel_id=1, source_target_pairs={{0,6},{1,7},{2,4},{3,5},{4,2},{5,3},{6,0},{7,1},{8,14},{9,15},{10,... | collective-permute-start | bytes 245768 | tf_op jit(solution)/shard_map/ppermute | solution.py:53
  21.9 6.9 %copy-start = (bf16[1280,864]{0,1:T(8,128)(2,1)S(1)}, bf16[1280,864]{0,1:T(8,128)(2,1)}, u32[]{:S(2)}) copy-start(bf16[1280,864]{0,1:T(8,128)(2,1)} %param.4) | copy-start | bytes 6635524
  22.0 15.1 %collective-permute-start.13 = (bf16[3,64,640]{2,1,0:T(8,128)(2,1)S(1)}, bf16[3,64,640]{2,1,0:T(8,128)(2,1)S(1)}, u32[]{:S(2)}, u32[]{:S(2)}) collective-permute-start(bf16[3,64,640]{2,1,0:T(8,128)(2,1)S(1)} %pad_maximum_fusion.4), channel_id=1, source_target_pairs={{0,1},{1,0},{2,3},{3,2},{4,5},{5,4},{6,7},{7,6},{8,9},{9,8},{10,11... | collective-permute-start | bytes 737288 | tf_op jit(solution)/shard_map/ppermute | solution.py:53
  22.1 10.3 %collective-permute-start.10 = (bf16[3,64,640]{2,1,0:T(8,128)(2,1)S(1)}, bf16[3,64,640]{2,1,0:T(8,128)(2,1)S(1)}, u32[]{:S(2)}, u32[]{:S(2)}) collective-permute-start(bf16[3,64,640]{2,1,0:T(8,128)(2,1)S(1)} %pad_maximum_fusion.4), channel_id=1, source_target_pairs={{0,2},{1,3},{2,0},{3,1},{4,6},{5,7},{6,4},{7,5},{8,10},{9,11},{10,... | collective-permute-start | bytes 737288 | tf_op jit(solution)/shard_map/ppermute | solution.py:53
  23.1 13.3 %collective-permute-start.11 = (bf16[3,64,640]{2,1,0:T(8,128)(2,1)S(1)}, bf16[3,64,640]{2,1,0:T(8,128)(2,1)S(1)}, u32[]{:S(2)}, u32[]{:S(2)}) collective-permute-start(bf16[3,64,640]{2,1,0:T(8,128)(2,1)S(1)} %pad_maximum_fusion.4), channel_id=1, source_target_pairs={{0,4},{1,5},{2,6},{3,7},{4,0},{5,1},{6,2},{7,3},{8,12},{9,13},{10,... | collective-permute-start | bytes 737288 | tf_op jit(solution)/shard_map/ppermute | solution.py:53
  23.8 12.7 %collective-permute-start.12 = (bf16[3,64,640]{2,1,0:T(8,128)(2,1)S(1)}, bf16[3,64,640]{2,1,0:T(8,128)(2,1)S(1)}, u32[]{:S(2)}, u32[]{:S(2)}) collective-permute-start(bf16[3,64,640]{2,1,0:T(8,128)(2,1)S(1)} %pad_maximum_fusion.4), channel_id=1, source_target_pairs={{0,6},{1,7},{2,4},{3,5},{4,2},{5,3},{6,0},{7,1},{8,14},{9,15},{10,... | collective-permute-start | bytes 737288 | tf_op jit(solution)/shard_map/ppermute | solution.py:53
  28.8 1.0 copy-start.9
  30.0 9.9 %collective-permute-start.7 = (bf16[400,256]{1,0:T(8,128)(2,1)S(1)}, bf16[400,256]{1,0:T(8,128)(2,1)S(1)}, u32[]{:S(2)}, u32[]{:S(2)}) collective-permute-start(bf16[400,256]{1,0:T(8,128)(2,1)S(1)} %fusion.17), channel_id=1, source_target_pairs={{0,16},{16,24},{24,8},{8,0},{1,17},{17,25},{25,9},{9,1},{2,18},{18... | collective-permute-start | bytes 614408 | tf_op jit(solution)/shard_map/ppermute | solution.py:57
  32.4 12.9 %collective-permute-start.19 = (bf16[464,256]{1,0:T(8,128)(2,1)S(1)}, bf16[464,256]{1,0:T(8,128)(2,1)S(1)}, u32[]{:S(2)}, u32[]{:S(2)}) collective-permute-start(bf16[464,256]{1,0:T(8,128)(2,1)S(1)} %fusion.16), channel_id=1, source_target_pairs={{0,16},{16,24},{24,8},{8,0},{1,17},{17,25},{25,9},{9,1},{2,18},{18... | collective-permute-start | bytes 712712 | tf_op jit(solution)/shard_map/ppermute | solution.py:57
  36.4 1.5 %collective-permute-start.14 = (bf16[3,64,640]{2,1,0:T(8,128)(2,1)S(1)}, bf16[3,64,640]{2,1,0:T(8,128)(2,1)S(1)}, u32[]{:S(2)}, u32[]{:S(2)}) collective-permute-start(bf16[3,64,640]{2,1,0:T(8,128)(2,1)S(1)} %collective-permute-done.10), channel_id=1, source_target_pairs={{0,1},{1,0},{2,3},{3,2},{4,5},{5,4},{6,7},{7,6},{8,9},{9,8},{10,11... | collective-permute-start | bytes 737288 | tf_op jit(solution)/shard_map/ppermute | solution.py:53
  36.5 1.8 %collective-permute-start.15 = (bf16[3,64,640]{2,1,0:T(8,128)(2,1)S(1)}, bf16[3,64,640]{2,1,0:T(8,128)(2,1)S(1)}, u32[]{:S(2)}, u32[]{:S(2)}) collective-permute-start(bf16[3,64,640]{2,1,0:T(8,128)(2,1)S(1)} %collective-permute-done.11), channel_id=1, source_target_pairs={{0,1},{1,0},{2,3},{3,2},{4,5},{5,4},{6,7},{7,6},{8,9},{9,8},{10,11... | collective-permute-start | bytes 737288 | tf_op jit(solution)/shard_map/ppermute | solution.py:53
  37.1 1.6 %collective-permute-start.16 = (bf16[3,64,640]{2,1,0:T(8,128)(2,1)S(1)}, bf16[3,64,640]{2,1,0:T(8,128)(2,1)S(1)}, u32[]{:S(2)}, u32[]{:S(2)}) collective-permute-start(bf16[3,64,640]{2,1,0:T(8,128)(2,1)S(1)} %collective-permute-done.12), channel_id=1, source_target_pairs={{0,1},{1,0},{2,3},{3,2},{4,5},{5,4},{6,7},{7,6},{8,9},{9,8},{10,11... | collective-permute-start | bytes 737288 | tf_op jit(solution)/shard_map/ppermute | solution.py:53
  39.9 5.4 %copy-start.11 = (bf16[32,8,2,640]{3,1,2,0:T(8,128)(2,1)}, bf16[32,8,2,640]{3,1,2,0:T(8,128)(2,1)S(1)}, u32[]{:S(2)}) copy-start(bf16[32,8,2,640]{3,1,2,0:T(8,128)(2,1)S(1)} %copy.67) | copy-start | bytes 1966084
  40.4 7.8 %collective-permute-start.17 = (bf16[400,256]{1,0:T(8,128)(2,1)S(1)}, bf16[400,256]{1,0:T(8,128)(2,1)S(1)}, u32[]{:S(2)}, u32[]{:S(2)}) collective-permute-start(bf16[400,256]{1,0:T(8,128)(2,1)S(1)} %add_convert_fusion.3), channel_id=1, source_target_pairs={{0,16},{16,24},{24,8},{8,0},{1,17},{17,25},{25,9},{9,1},{2,18},{18... | collective-permute-start | bytes 614408 | tf_op jit(solution)/shard_map/ppermute | solution.py:57
  43.5 1.3 %copy-start.13 = (bf16[32,8,2,640]{3,1,2,0:T(8,128)(2,1)}, bf16[32,8,2,640]{3,1,2,0:T(8,128)(2,1)S(1)}, u32[]{:S(2)}) copy-start(bf16[32,8,2,640]{3,1,2,0:T(8,128)(2,1)S(1)} %copy.68) | copy-start | bytes 1966084
  44.3 2.7 %copy-start.15 = (bf16[32,8,2,640]{3,1,2,0:T(8,128)(2,1)}, bf16[32,8,2,640]{3,1,2,0:T(8,128)(2,1)S(1)}, u32[]{:S(2)}) copy-start(bf16[32,8,2,640]{3,1,2,0:T(8,128)(2,1)S(1)} %copy.69) | copy-start | bytes 1966084
  45.8 8.7 %collective-permute-start.20 = (bf16[464,256]{1,0:T(8,128)(2,1)S(1)}, bf16[464,256]{1,0:T(8,128)(2,1)S(1)}, u32[]{:S(2)}, u32[]{:S(2)}) collective-permute-start(bf16[464,256]{1,0:T(8,128)(2,1)S(1)} %add_convert_fusion.1), channel_id=1, source_target_pairs={{0,16},{16,24},{24,8},{8,0},{1,17},{17,25},{25,9},{9,1},{2,18},{18... | collective-permute-start | bytes 712712 | tf_op jit(solution)/shard_map/ppermute | solution.py:57
  47.0 11.9 %copy-start.17 = (bf16[256,864]{0,1:T(8,128)(2,1)S(1)}, bf16[256,864]{0,1:T(8,128)(2,1)}, u32[]{:S(2)}) copy-start(bf16[256,864]{0,1:T(8,128)(2,1)} %param.5) | copy-start | bytes 1327108
  48.2 10.7 %collective-permute-start.18 = (bf16[400,256]{1,0:T(8,128)(2,1)S(1)}, bf16[400,256]{1,0:T(8,128)(2,1)S(1)}, u32[]{:S(2)}, u32[]{:S(2)}) collective-permute-start(bf16[400,256]{1,0:T(8,128)(2,1)S(1)} %add_convert_fusion.2), channel_id=1, source_target_pairs={{0,16},{16,24},{24,8},{8,0},{1,17},{17,25},{25,9},{9,1},{2,18},{18... | collective-permute-start | bytes 614408 | tf_op jit(solution)/shard_map/ppermute | solution.py:57
  54.6 8.5 %collective-permute-start.21 = (bf16[464,256]{1,0:T(8,128)(2,1)S(1)}, bf16[464,256]{1,0:T(8,128)(2,1)S(1)}, u32[]{:S(2)}, u32[]{:S(2)}) collective-permute-start(bf16[464,256]{1,0:T(8,128)(2,1)S(1)} %add_convert_fusion), channel_id=1, source_target_pairs={{0,16},{16,24},{24,8},{8,0},{1,17},{17,25},{25,9},{9,1},{2,18},{18... | collective-permute-start | bytes 712712 | tf_op jit(solution)/shard_map/ppermute | solution.py:57
  60.0 7.1 %copy-start.7 = (bf16[400,256]{1,0:T(8,128)(2,1)}, bf16[400,256]{1,0:T(8,128)(2,1)S(1)}, u32[]{:S(2)}) copy-start(bf16[400,256]{1,0:T(8,128)(2,1)S(1)} %get-tuple-element.26) | copy-start | bytes 614404
  60.0 9.2 %collective-permute-start.22 = (bf16[400,256]{1,0:T(8,128)(2,1)S(1)}, bf16[400,256]{1,0:T(8,128)(2,1)S(1)}, u32[]{:S(2)}, u32[]{:S(2)}) collective-permute-start(bf16[400,256]{1,0:T(8,128)(2,1)S(1)} %get-tuple-element.26), channel_id=1, source_target_pairs={{0,8},{16,0},{24,16},{8,24},{1,9},{17,1},{25,17},{9,25},{2,10},{18... | collective-permute-start | bytes 614408 | tf_op jit(solution)/shard_map/ppermute | solution.py:57
  63.6 12.3 %copy-start.1 = (bf16[464,256]{1,0:T(8,128)(2,1)}, bf16[464,256]{1,0:T(8,128)(2,1)S(1)}, u32[]{:S(2)}) copy-start(bf16[464,256]{1,0:T(8,128)(2,1)S(1)} %get-tuple-element.21) | copy-start | bytes 712708
  63.6 10.7 %collective-permute-start.24 = (bf16[464,256]{1,0:T(8,128)(2,1)S(1)}, bf16[464,256]{1,0:T(8,128)(2,1)S(1)}, u32[]{:S(2)}, u32[]{:S(2)}) collective-permute-start(bf16[464,256]{1,0:T(8,128)(2,1)S(1)} %get-tuple-element.21), channel_id=1, source_target_pairs={{0,8},{16,0},{24,16},{8,24},{1,9},{17,1},{25,17},{9,25},{2,10},{18... | collective-permute-start | bytes 712712 | tf_op jit(solution)/shard_map/ppermute | solution.py:57
  69.2 9.5 %collective-permute-start.23 = (bf16[400,256]{1,0:T(8,128)(2,1)S(1)}, bf16[400,256]{1,0:T(8,128)(2,1)S(1)}, u32[]{:S(2)}, u32[]{:S(2)}) collective-permute-start(bf16[400,256]{1,0:T(8,128)(2,1)S(1)} %collective-permute-done.22), channel_id=1, source_target_pairs={{0,8},{16,0},{24,16},{8,24},{1,9},{17,1},{25,17},{9,25},{2,10},{18... | collective-permute-start | bytes 614408 | tf_op jit(solution)/shard_map/ppermute | solution.py:57
  74.3 8.8 %collective-permute-start.25 = (bf16[464,256]{1,0:T(8,128)(2,1)S(1)}, bf16[464,256]{1,0:T(8,128)(2,1)S(1)}, u32[]{:S(2)}, u32[]{:S(2)}) collective-permute-start(bf16[464,256]{1,0:T(8,128)(2,1)S(1)} %collective-permute-done.24), channel_id=1, source_target_pairs={{0,8},{16,0},{24,16},{8,24},{1,9},{17,1},{25,17},{9,25},{2,10},{18... | collective-permute-start | bytes 712712 | tf_op jit(solution)/shard_map/ppermute | solution.py:57
  75.0 9.0 %copy-start.3 = (bf16[864,256]{1,0:T(8,128)(2,1)}, bf16[864,256]{1,0:T(8,128)(2,1)S(1)}, u32[]{:S(2)}) copy-start(bf16[864,256]{1,0:T(8,128)(2,1)S(1)} %constant_dynamic-update-slice_fusion.2) | copy-start | bytes 1327108
  83.1 0.9 copy-start.5
  85.5 2.6 %collective-permute-start.32 = (bf16[3,2,32,1280]{3,2,0,1:T(8,128)(2,1)}, bf16[3,2,32,1280]{3,2,0,1:T(8,128)(2,1)}, u32[]{:S(2)}, u32[]{:S(2)}) collective-permute-start(bf16[3,2,32,1280]{3,2,0,1:T(8,128)(2,1)} %get-tuple-element.19), channel_id=1, source_target_pairs={{0,1},{1,0},{2,3},{3,2},{4,5},{5,4},{6,7},{7,6},{8,9},{9,8},{10,11... | collective-permute-start | bytes 1474568 | tf_op jit(solution)/shard_map/ppermute | solution.py:53
  85.5 2.9 %collective-permute-start.33 = (bf16[3,2,32,1280]{3,2,0,1:T(8,128)(2,1)}, bf16[3,2,32,1280]{3,2,0,1:T(8,128)(2,1)}, u32[]{:S(2)}, u32[]{:S(2)}) collective-permute-start(bf16[3,2,32,1280]{3,2,0,1:T(8,128)(2,1)} %get-tuple-element.20), channel_id=1, source_target_pairs={{0,1},{1,0},{2,3},{3,2},{4,5},{5,4},{6,7},{7,6},{8,9},{9,8},{10,11... | collective-permute-start | bytes 1474568 | tf_op jit(solution)/shard_map/ppermute | solution.py:53
  87.8 13.2 %collective-permute-start.26 = (bf16[864,256]{1,0:T(8,128)(2,1)}, bf16[864,256]{1,0:T(8,128)(2,1)S(1)}, u32[]{:S(2)}, u32[]{:S(2)}) collective-permute-start(bf16[864,256]{1,0:T(8,128)(2,1)} %copy-done.5), channel_id=1, source_target_pairs={{0,8},{16,0},{24,16},{8,24},{1,9},{17,1},{25,17},{9,25},{2,10},{18... | collective-permute-start | bytes 1327112 | tf_op jit(solution)/shard_map/ppermute | solution.py:57
  90.0 12.1 %collective-permute-start.34 = (bf16[3,32,1280]{2,1,0:T(8,128)(2,1)S(1)}, bf16[3,32,1280]{2,1,0:T(8,128)(2,1)S(1)}, u32[]{:S(2)}, u32[]{:S(2)}) collective-permute-start(bf16[3,32,1280]{2,1,0:T(8,128)(2,1)S(1)} %get-tuple-element.9), channel_id=1, source_target_pairs={{0,2},{1,3},{2,0},{3,1},{4,6},{5,7},{6,4},{7,5},{8,10},{9,11},{10,... | collective-permute-start | bytes 737288 | tf_op jit(solution)/shard_map/ppermute | solution.py:53
  91.4 13.0 %collective-permute-start.35 = (bf16[3,32,1280]{2,1,0:T(8,128)(2,1)S(1)}, bf16[3,32,1280]{2,1,0:T(8,128)(2,1)S(1)}, u32[]{:S(2)}, u32[]{:S(2)}) collective-permute-start(bf16[3,32,1280]{2,1,0:T(8,128)(2,1)S(1)} %get-tuple-element.11), channel_id=1, source_target_pairs={{0,4},{1,5},{2,6},{3,7},{4,0},{5,1},{6,2},{7,3},{8,12},{9,13},{10,... | collective-permute-start | bytes 737288 | tf_op jit(solution)/shard_map/ppermute | solution.py:53
  92.0 12.4 %collective-permute-start.36 = (bf16[3,32,1280]{2,1,0:T(8,128)(2,1)S(1)}, bf16[3,32,1280]{2,1,0:T(8,128)(2,1)S(1)}, u32[]{:S(2)}, u32[]{:S(2)}) collective-permute-start(bf16[3,32,1280]{2,1,0:T(8,128)(2,1)S(1)} %get-tuple-element.10), channel_id=1, source_target_pairs={{0,6},{1,7},{2,4},{3,5},{4,2},{5,3},{6,0},{7,1},{8,14},{9,15},{10,... | collective-permute-start | bytes 737288 | tf_op jit(solution)/shard_map/ppermute | solution.py:53
  101.9 11.4 %copy-start.2 = (bf16[464,256]{1,0:T(8,128)(2,1)S(1)}, bf16[464,256]{1,0:T(8,128)(2,1)}, u32[]{:S(2)}) copy-start(bf16[464,256]{1,0:T(8,128)(2,1)} %copy-done.1) | copy-start | bytes 712708
  101.9 11.4 %copy-start.4 = (bf16[864,256]{1,0:T(8,128)(2,1)S(1)}, bf16[864,256]{1,0:T(8,128)(2,1)}, u32[]{:S(2)}) copy-start(bf16[864,256]{1,0:T(8,128)(2,1)} %copy-done.3) | copy-start | bytes 1327108
  101.9 11.4 %copy-start.6 = (bf16[864,256]{1,0:T(8,128)(2,1)S(1)}, bf16[864,256]{1,0:T(8,128)(2,1)}, u32[]{:S(2)}) copy-start(bf16[864,256]{1,0:T(8,128)(2,1)} %copy-done.5) | copy-start | bytes 1327108
  101.9 11.4 %copy-start.8 = (bf16[400,256]{1,0:T(8,128)(2,1)S(1)}, bf16[400,256]{1,0:T(8,128)(2,1)}, u32[]{:S(2)}) copy-start(bf16[400,256]{1,0:T(8,128)(2,1)} %copy-done.7) | copy-start | bytes 614404
  101.9 11.4 %copy-start.10 = (bf16[32,8,2,640]{3,1,2,0:T(8,128)(2,1)S(1)}, bf16[32,8,2,640]{3,1,2,0:T(8,128)(2,1)}, u32[]{:S(2)}) copy-start(bf16[32,8,2,640]{3,1,2,0:T(8,128)(2,1)} %copy-done.9) | copy-start | bytes 1966084
  101.9 11.4 %copy-start.12 = (bf16[32,8,2,640]{3,1,2,0:T(8,128)(2,1)S(1)}, bf16[32,8,2,640]{3,1,2,0:T(8,128)(2,1)}, u32[]{:S(2)}) copy-start(bf16[32,8,2,640]{3,1,2,0:T(8,128)(2,1)} %copy-done.11) | copy-start | bytes 1966084
  101.9 11.4 %copy-start.14 = (bf16[32,8,2,640]{3,1,2,0:T(8,128)(2,1)S(1)}, bf16[32,8,2,640]{3,1,2,0:T(8,128)(2,1)}, u32[]{:S(2)}) copy-start(bf16[32,8,2,640]{3,1,2,0:T(8,128)(2,1)} %copy-done.13) | copy-start | bytes 1966084
  101.9 11.4 %copy-start.16 = (bf16[32,8,2,640]{3,1,2,0:T(8,128)(2,1)S(1)}, bf16[32,8,2,640]{3,1,2,0:T(8,128)(2,1)}, u32[]{:S(2)}) copy-start(bf16[32,8,2,640]{3,1,2,0:T(8,128)(2,1)} %copy-done.15) | copy-start | bytes 1966084
  101.9 2.6 %collective-permute-start.27 = (bf16[1,4,32,1280]{3,2,1,0:T(8,128)(2,1)S(1)}, bf16[1,4,32,1280]{3,2,1,0:T(8,128)(2,1)S(1)}, u32[]{:S(2)}, u32[]{:S(2)}) collective-permute-start(bf16[1,4,32,1280]{3,2,1,0:T(8,128)(2,1)S(1)} %dynamic-slice_bitcast_fusion), channel_id=1, source_target_pairs={{0,1},{1,0},{2,3},{3,2},{4,5},{5,4},{6,7},{7,6},{8,9},{9,8},{10,11... | collective-permute-start | bytes 983048 | tf_op jit(solution)/shard_map/ppermute | solution.py:53
  104.7 6.5 %collective-permute-start.28 = (bf16[1,32,1280]{2,1,0:T(8,128)(2,1)S(1)}, bf16[1,32,1280]{2,1,0:T(8,128)(2,1)S(1)}, u32[]{:S(2)}, u32[]{:S(2)}) collective-permute-start(bf16[1,32,1280]{2,1,0:T(8,128)(2,1)S(1)} %get-tuple-element.23), channel_id=1, source_target_pairs={{0,2},{1,3},{2,0},{3,1},{4,6},{5,7},{6,4},{7,5},{8,10},{9,11},{10,... | collective-permute-start | bytes 245768 | tf_op jit(solution)/shard_map/ppermute | solution.py:53
  105.4 5.8 %collective-permute-start.29 = (bf16[1,32,1280]{2,1,0:T(8,128)(2,1)S(1)}, bf16[1,32,1280]{2,1,0:T(8,128)(2,1)S(1)}, u32[]{:S(2)}, u32[]{:S(2)}) collective-permute-start(bf16[1,32,1280]{2,1,0:T(8,128)(2,1)S(1)} %get-tuple-element.25), channel_id=1, source_target_pairs={{0,4},{1,5},{2,6},{3,7},{4,0},{5,1},{6,2},{7,3},{8,12},{9,13},{10,... | collective-permute-start | bytes 245768 | tf_op jit(solution)/shard_map/ppermute | solution.py:53
  106.5 5.3 %collective-permute-start.30 = (bf16[1,32,1280]{2,1,0:T(8,128)(2,1)S(1)}, bf16[1,32,1280]{2,1,0:T(8,128)(2,1)S(1)}, u32[]{:S(2)}, u32[]{:S(2)}) collective-permute-start(bf16[1,32,1280]{2,1,0:T(8,128)(2,1)S(1)} %get-tuple-element.24), channel_id=1, source_target_pairs={{0,6},{1,7},{2,4},{3,5},{4,2},{5,3},{6,0},{7,1},{8,14},{9,15},{10,... | collective-permute-start | bytes 245768 | tf_op jit(solution)/shard_map/ppermute | solution.py:53
  108.2 9.6 %collective-permute-start.37 = (bf16[32,1280]{1,0:T(8,128)(2,1)S(1)}, bf16[32,1280]{1,0:T(8,128)(2,1)S(1)}, u32[]{:S(2)}, u32[]{:S(2)}) collective-permute-start(bf16[32,1280]{1,0:T(8,128)(2,1)S(1)} %get-tuple-element.41), channel_id=1, source_target_pairs={{0,24},{16,8},{24,0},{8,16},{1,25},{17,9},{25,1},{9,17},{2,26},{18... | collective-permute-start | bytes 245768 | tf_op jit(solution)/shard_map/ppermute | solution.py:57
  110.2 7.7 %collective-permute-start.38 = (bf16[32,1280]{1,0:T(8,128)(2,1)S(1)}, bf16[32,1280]{1,0:T(8,128)(2,1)S(1)}, u32[]{:S(2)}, u32[]{:S(2)}) collective-permute-start(bf16[32,1280]{1,0:T(8,128)(2,1)S(1)} %get-tuple-element.40), channel_id=1, source_target_pairs={{0,16},{16,24},{24,8},{8,0},{1,17},{17,25},{25,9},{9,1},{2,18},{18... | collective-permute-start | bytes 245768 | tf_op jit(solution)/shard_map/ppermute | solution.py:57
  111.9 6.0 %collective-permute-start.31 = (bf16[32,1280]{1,0:T(8,128)(2,1)S(1)}, bf16[32,1280]{1,0:T(8,128)(2,1)S(1)}, u32[]{:S(2)}, u32[]{:S(2)}) collective-permute-start(bf16[32,1280]{1,0:T(8,128)(2,1)S(1)} %fusion.61), channel_id=1, source_target_pairs={{0,8},{16,0},{24,16},{8,24},{1,9},{17,1},{25,17},{9,25},{2,10},{18... | collective-permute-start | bytes 245768 | tf_op jit(solution)/shard_map/ppermute | solution.py:57

commit v5 on v4

--- a/solution.py
+++ b/solution.py
@@ -158,8 +158,15 @@
         total = narrow(total)
         return [total[i] for i in range(total.shape[0])]
 
-    pieces = [exchange(meet(ring[:-1])), exchange(meet(ring[-1:]))]
-    sums = finish(pieces[0]) + finish(pieces[1])
+    pieces = [exchange(meet(blocks)) for blocks in (ring[:-2], ring[-2:-1], ring[-1:])]
+
+    whole = [jnp.concatenate(s) for s in ring]
+    weight_grad = grad_scale * product(
+        jnp.concatenate(whole[:0:-1] + whole[:1], axis=1), jnp.concatenate(tokens, axis=0), ((1,), (0,))
+    )
+    pieces[-1][1:] = after(pieces[-1][1:], weight_grad)
+
+    sums = [total for batch in pieces for total in finish(batch)]
     placed = [None] * n_row
     for k in range(n_row):
         placed[(n_row - k) % n_row] = along(sums[k], k) if k else sums[k]
@@ -170,11 +177,7 @@
         step *= 2
     input_grad = jnp.concatenate([placed[spot_of[p]] for p in range(n_row)], axis=1)
 
-    whole = [jnp.concatenate(s) for s in ring]
-    weight_grad = product(
-        jnp.concatenate(whole[:0:-1] + whole[:1], axis=1), jnp.concatenate(tokens, axis=0), ((1,), (0,))
-    )
-    return (hidden, input_grad, (weight_grad * grad_scale).T)
+    return (hidden, input_grad, weight_grad.T)
 
 
 def solution(mesh):

time: 119 us -> 116 us (0.975)
  starting transfers between devices: 46.8 us -> 51.2 us
  other arithmetic: 6.6 us -> 3.76 us
  waiting for transfers between devices: 43.5 us -> 41 us
  local copies, waits for them, and re-layouts: 6.17 us -> 4.97 us
    ppermute x17, waiting for transfers between devices: 30.5 us -> 22 us  [along(): return lax.ppermute(array, 'row', pairs)]
    ppermute x22 -> x26, waiting for transfers between devices: 13 us -> 19 us  [across(): return lax.ppermute(array, 'col', [(i, i ^ flip) for i in range(n_col)])]
    ppermute x22 -> x26, starting transfers between devices: 20.1 us -> 22.6 us  [across(): return lax.ppermute(array, 'col', [(i, i ^ flip) for i in range(n_col)])]
    ppermute x17, starting transfers between devices: 26.8 us -> 28.6 us  [along(): return lax.ppermute(array, 'row', pairs)]
    add x2 -> x3, other arithmetic: 1.49 us -> 0.29 us  [meet(): both = wide(at(laid, core, 2)) + wide(got)]
  transfers between devices with their start and end apart: 39 -> 43, of which waited for: 21 -> 24; matrix products, arithmetic and copies ran while one was open for 17% -> 16% of each run, Pallas kernels for 0% -> 0%
where the time goes in v5:
time: 116 us
  starting transfers between devices  51.2 us (44%)
  waiting for transfers between devices  41 us (35%)
  matrix products  11.9 us (10%)
  local copies, waits for them, and re-layouts  4.97 us (4%)
  other arithmetic  3.76 us (3%)
  blocking collectives  2.28 us (2%)
  between operations  1.18 us (1%)
    ppermute x17, starting transfers between devices, along(): return lax.ppermute(array, 'row', pairs)  28.6 us
    ppermute x26, starting transfers between devices, across(): return lax.ppermute(array, 'col', [(i, i ^ flip) for i in range(n_col)])  22.6 us
    ppermute x17, waiting for transfers between devices, along(): return lax.ppermute(array, 'row', pairs)  22 us
    ppermute x26, waiting for transfers between devices, across(): return lax.ppermute(array, 'col', [(i, i ^ flip) for i in range(n_col)])  19 us
    dot_general x13, matrix products, product(): lax.dot_general(left, right, (axes, ((), ())), preferred_element_type=jnp...  11.9 us
  transfers between devices with their start and end apart: 43, of which 24 were waited for; matrix products, arithmetic and copies ran while one was open for 16% of the time, Pallas kernels for 0%

profile of v5, /device:TPU:0, one launch (start us, length us, event | category | flops | bytes accessed | tf_op | source)
XLA Modules:
  0.0 116.3 jit_solution(8214141246503133298)
XLA Ops:
  0.7 1.0 constant_dynamic-slice_fusion
  1.7 3.0 %collective-permute-start = (bf16[64,640]{1,0:T(8,128)(2,1)S(1)}, bf16[64,640]{1,0:T(8,128)(2,1)S(1)}, u32[]{:S(2)}, u32[]{:S(2)}) collective-permute-start(bf16[64,640]{1,0:T(8,128)(2,1)S(1)} %get-tuple-element.48), channel_id=1, source_target_pairs={{0,2},{1,3},{2,0},{3,1},{4,6},{5,7},{6,4},{7,5},{8,10},{9,11},{10,... | collective-permute-start | bytes 245768 | tf_op jit(solution)/shard_map/ppermute | solution.py:53
  4.7 1.5 %collective-permute-start.1 = (bf16[64,640]{1,0:T(8,128)(2,1)S(1)}, bf16[64,640]{1,0:T(8,128)(2,1)S(1)}, u32[]{:S(2)}, u32[]{:S(2)}) collective-permute-start(bf16[64,640]{1,0:T(8,128)(2,1)S(1)} %get-tuple-element.47), channel_id=1, source_target_pairs={{0,4},{1,5},{2,6},{3,7},{4,0},{5,1},{6,2},{7,3},{8,12},{9,13},{10,... | collective-permute-start | bytes 245768 | tf_op jit(solution)/shard_map/ppermute | solution.py:53
  6.3 1.2 %collective-permute-done = bf16[64,640]{1,0:T(8,128)(2,1)S(1)} collective-permute-done((bf16[64,640]{1,0:T(8,128)(2,1)S(1)}, bf16[64,640]{1,0:T(8,128)(2,1)S(1)}, u32[]{:S(2)}, u32[]{:S(2)}) %collective-permute-start) | collective-permute-done | bytes 81952 | tf_op jit(solution)/shard_map/ppermute | solution.py:53
  7.4 2.6 %collective-permute-done.1 = bf16[64,640]{1,0:T(8,128)(2,1)S(1)} collective-permute-done((bf16[64,640]{1,0:T(8,128)(2,1)S(1)}, bf16[64,640]{1,0:T(8,128)(2,1)S(1)}, u32[]{:S(2)}, u32[]{:S(2)}) %collective-permute-start.1) | collective-permute-done | bytes 81952 | tf_op jit(solution)/shard_map/ppermute | solution.py:53
  10.0 1.5 %collective-permute-done.2 = bf16[64,640]{1,0:T(8,128)(2,1)S(1)} collective-permute-done((bf16[64,640]{1,0:T(8,128)(2,1)S(1)}, bf16[64,640]{1,0:T(8,128)(2,1)S(1)}, u32[]{:S(2)}, u32[]{:S(2)}) %collective-permute-start.2) | collective-permute-done | bytes 81952 | tf_op jit(solution)/shard_map/ppermute | solution.py:53
  11.7 2.6 %collective-permute-start.3 = (bf16[64,640]{1,0:T(8,128)(2,1)S(1)}, bf16[64,640]{1,0:T(8,128)(2,1)S(1)}, u32[]{:S(2)}, u32[]{:S(2)}) collective-permute-start(bf16[64,640]{1,0:T(8,128)(2,1)S(1)} %get-tuple-element.41), channel_id=1, source_target_pairs={{0,16},{16,24},{24,8},{8,0},{1,17},{17,25},{25,9},{9,1},{2,18},{18... | collective-permute-start | bytes 245768 | tf_op jit(solution)/shard_map/ppermute | solution.py:57
  14.3 1.3 %collective-permute-start.8 = (bf16[64,640]{1,0:T(8,128)(2,1)S(1)}, bf16[64,640]{1,0:T(8,128)(2,1)S(1)}, u32[]{:S(2)}, u32[]{:S(2)}) collective-permute-start(bf16[64,640]{1,0:T(8,128)(2,1)S(1)} %get-tuple-element.44), channel_id=1, source_target_pairs={{0,24},{16,8},{24,0},{8,16},{1,25},{17,9},{25,1},{9,17},{2,26},{18... | collective-permute-start | bytes 245768 | tf_op jit(solution)/shard_map/ppermute | solution.py:57
  15.7 0.8 collective-permute-start.9
  16.5 1.0 collective-permute-start.4
  17.4 0.6 collective-permute-start.5
  18.0 1.9 %collective-permute-start.6 = (bf16[1,64,640]{2,1,0:T(8,128)(2,1)S(1)}, bf16[1,64,640]{2,1,0:T(8,128)(2,1)S(1)}, u32[]{:S(2)}, u32[]{:S(2)}) collective-permute-start(bf16[1,64,640]{2,1,0:T(8,128)(2,1)S(1)} %bitcast.256), channel_id=1, source_target_pairs={{0,6},{1,7},{2,4},{3,5},{4,2},{5,3},{6,0},{7,1},{8,14},{9,15},{10,... | collective-permute-start | bytes 245768 | tf_op jit(solution)/shard_map/ppermute | solution.py:53
  20.0 0.7 collective-permute-done.8
  20.7 1.3 %collective-permute-done.9 = bf16[64,640]{1,0:T(8,128)(2,1)S(1)} collective-permute-done((bf16[64,640]{1,0:T(8,128)(2,1)S(1)}, bf16[64,640]{1,0:T(8,128)(2,1)S(1)}, u32[]{:S(2)}, u32[]{:S(2)}) %collective-permute-start.9) | collective-permute-done | bytes 81952 | tf_op jit(solution)/shard_map/ppermute | solution.py:57
  22.1 1.1 collective-permute-start.10
  23.1 0.6 collective-permute-start.11
  23.8 1.9 %collective-permute-start.12 = (bf16[3,64,640]{2,1,0:T(8,128)(2,1)S(1)}, bf16[3,64,640]{2,1,0:T(8,128)(2,1)S(1)}, u32[]{:S(2)}, u32[]{:S(2)}) collective-permute-start(bf16[3,64,640]{2,1,0:T(8,128)(2,1)S(1)} %pad_maximum_fusion.3), channel_id=1, source_target_pairs={{0,6},{1,7},{2,4},{3,5},{4,2},{5,3},{6,0},{7,1},{8,14},{9,15},{10,... | collective-permute-start | bytes 737288 | tf_op jit(solution)/shard_map/ppermute | solution.py:53
  25.8 2.3 %all_gather.19 = bf16[1,4,64,2,640]{4,2,1,0,3:T(8,128)(2,1)S(1)} all-gather(bf16[1,4,64,1,640]{4,2,1,0,3:T(8,128)(2,1)S(1)} %bitcast_dynamic-update-slice_fusion.8), channel_id=1, replica_groups={{0,1},{2,3},{4,5},{6,7},{8,9},{10,11},{12,13},{14,15},{16,17},{18,19},{..., dimensions={3}, use_global_device_ids=true | all-gather | bytes 983040 | tf_op jit(solution)/shard_map/all_gather | solution.py:99
  28.0 0.7 copy.47
  29.9 2.4 %collective-permute-start.7 = (bf16[400,256]{1,0:T(8,128)(2,1)S(1)}, bf16[400,256]{1,0:T(8,128)(2,1)S(1)}, u32[]{:S(2)}, u32[]{:S(2)}) collective-permute-start(bf16[400,256]{1,0:T(8,128)(2,1)S(1)} %fusion.17), channel_id=1, source_target_pairs={{0,16},{16,24},{24,8},{8,0},{1,17},{17,25},{25,9},{9,1},{2,18},{18... | collective-permute-start | bytes 614408 | tf_op jit(solution)/shard_map/ppermute | solution.py:57
  32.4 0.9 collective-permute-start.19
  33.3 3.1 %collective-permute-done.11 = bf16[3,64,640]{2,1,0:T(8,128)(2,1)S(1)} collective-permute-done((bf16[3,64,640]{2,1,0:T(8,128)(2,1)S(1)}, bf16[3,64,640]{2,1,0:T(8,128)(2,1)S(1)}, u32[]{:S(2)}, u32[]{:S(2)}) %collective-permute-start.11) | collective-permute-done | bytes 245792 | tf_op jit(solution)/shard_map/ppermute | solution.py:53
  36.5 0.6 collective-permute-start.15
  37.3 0.6 collective-permute-done.14
  39.1 0.7 copy.55
  40.4 2.4 %collective-permute-start.17 = (bf16[400,256]{1,0:T(8,128)(2,1)S(1)}, bf16[400,256]{1,0:T(8,128)(2,1)S(1)}, u32[]{:S(2)}, u32[]{:S(2)}) collective-permute-start(bf16[400,256]{1,0:T(8,128)(2,1)S(1)} %add_convert_fusion.3), channel_id=1, source_target_pairs={{0,16},{16,24},{24,8},{8,0},{1,17},{17,25},{25,9},{9,1},{2,18},{18... | collective-permute-start | bytes 614408 | tf_op jit(solution)/shard_map/ppermute | solution.py:57
  42.7 0.7 copy.56
  43.5 0.7 copy.57
  45.8 0.7 collective-permute-start.20
  47.4 0.7 collective-permute-done.17
  48.2 3.4 %collective-permute-start.18 = (bf16[400,256]{1,0:T(8,128)(2,1)S(1)}, bf16[400,256]{1,0:T(8,128)(2,1)S(1)}, u32[]{:S(2)}, u32[]{:S(2)}) collective-permute-start(bf16[400,256]{1,0:T(8,128)(2,1)S(1)} %add_convert_fusion.2), channel_id=1, source_target_pairs={{0,16},{16,24},{24,8},{8,0},{1,17},{17,25},{25,9},{9,1},{2,18},{18... | collective-permute-start | bytes 614408 | tf_op jit(solution)/shard_map/ppermute | solution.py:57
  51.7 2.8 %collective-permute-done.20 = bf16[464,256]{1,0:T(8,128)(2,1)S(1)} collective-permute-done((bf16[464,256]{1,0:T(8,128)(2,1)S(1)}, bf16[464,256]{1,0:T(8,128)(2,1)S(1)}, u32[]{:S(2)}, u32[]{:S(2)}) %collective-permute-start.20) | collective-permute-done | bytes 237600 | tf_op jit(solution)/shard_map/ppermute | solution.py:57
  54.6 2.2 %collective-permute-start.21 = (bf16[464,256]{1,0:T(8,128)(2,1)S(1)}, bf16[464,256]{1,0:T(8,128)(2,1)S(1)}, u32[]{:S(2)}, u32[]{:S(2)}) collective-permute-start(bf16[464,256]{1,0:T(8,128)(2,1)S(1)} %add_convert_fusion), channel_id=1, source_target_pairs={{0,16},{16,24},{24,8},{8,0},{1,17},{17,25},{25,9},{9,1},{2,18},{18... | collective-permute-start | bytes 712712 | tf_op jit(solution)/shard_map/ppermute | solution.py:57
  56.8 2.1 %collective-permute-done.18 = bf16[400,256]{1,0:T(8,128)(2,1)S(1)} collective-permute-done((bf16[400,256]{1,0:T(8,128)(2,1)S(1)}, bf16[400,256]{1,0:T(8,128)(2,1)S(1)}, u32[]{:S(2)}, u32[]{:S(2)}) %collective-permute-start.18) | collective-permute-done | bytes 204832 | tf_op jit(solution)/shard_map/ppermute | solution.py:57
  59.3 1.5 %collective-permute-start.22 = (bf16[400,256]{1,0:T(8,128)(2,1)S(1)}, bf16[400,256]{1,0:T(8,128)(2,1)S(1)}, u32[]{:S(2)}, u32[]{:S(2)}) collective-permute-start(bf16[400,256]{1,0:T(8,128)(2,1)S(1)} %get-tuple-element.35), channel_id=1, source_target_pairs={{0,8},{16,0},{24,16},{8,24},{1,9},{17,1},{25,17},{9,25},{2,10},{18... | collective-permute-start | bytes 614408 | tf_op jit(solution)/shard_map/ppermute | solution.py:57
  60.8 2.2 %collective-permute-done.21 = bf16[464,256]{1,0:T(8,128)(2,1)S(1)} collective-permute-done((bf16[464,256]{1,0:T(8,128)(2,1)S(1)}, bf16[464,256]{1,0:T(8,128)(2,1)S(1)}, u32[]{:S(2)}, u32[]{:S(2)}) %collective-permute-start.21) | collective-permute-done | bytes 237600 | tf_op jit(solution)/shard_map/ppermute | solution.py:57
  63.6 2.7 %collective-permute-start.24 = (bf16[464,256]{1,0:T(8,128)(2,1)S(1)}, bf16[464,256]{1,0:T(8,128)(2,1)S(1)}, u32[]{:S(2)}, u32[]{:S(2)}) collective-permute-start(bf16[464,256]{1,0:T(8,128)(2,1)S(1)} %get-tuple-element.25), channel_id=1, source_target_pairs={{0,8},{16,0},{24,16},{8,24},{1,9},{17,1},{25,17},{9,25},{2,10},{18... | collective-permute-start | bytes 712712 | tf_op jit(solution)/shard_map/ppermute | solution.py:57
  66.3 0.9 convolution_convert_fusion.1
  67.2 0.8 maximum_bitcast_fusion
  67.9 1.0 collective-permute-done.22
  68.9 1.0 collective-permute-start.23
  69.9 4.1 %collective-permute-done.24 = bf16[464,256]{1,0:T(8,128)(2,1)S(1)} collective-permute-done((bf16[464,256]{1,0:T(8,128)(2,1)S(1)}, bf16[464,256]{1,0:T(8,128)(2,1)S(1)}, u32[]{:S(2)}, u32[]{:S(2)}) %collective-permute-start.24) | collective-permute-done | bytes 237600 | tf_op jit(solution)/shard_map/ppermute | solution.py:57
  74.1 0.9 convolution_convert_fusion
  75.1 1.2 %collective-permute-start.25 = (bf16[464,256]{1,0:T(8,128)(2,1)S(1)}, bf16[464,256]{1,0:T(8,128)(2,1)S(1)}, u32[]{:S(2)}, u32[]{:S(2)}) collective-permute-start(bf16[464,256]{1,0:T(8,128)(2,1)S(1)} %collective-permute-done.24), channel_id=1, source_target_pairs={{0,8},{16,0},{24,16},{8,24},{1,9},{17,1},{25,17},{9,25},{2,10},{18... | collective-permute-start | bytes 712712 | tf_op jit(solution)/shard_map/ppermute | solution.py:57
  76.9 1.1 collective-permute-done.23
  78.0 5.2 %collective-permute-done.25 = bf16[464,256]{1,0:T(8,128)(2,1)S(1)} collective-permute-done((bf16[464,256]{1,0:T(8,128)(2,1)S(1)}, bf16[464,256]{1,0:T(8,128)(2,1)S(1)}, u32[]{:S(2)}, u32[]{:S(2)}) %collective-permute-start.25) | collective-permute-done | bytes 237600 | tf_op jit(solution)/shard_map/ppermute | solution.py:57
  83.6 0.9 convolution_convert_fusion.2
  84.7 1.4 %collective-permute-start.39 = (bf16[2,32,1280]{2,1,0:T(8,128)(2,1)S(1)}, bf16[2,32,1280]{2,1,0:T(8,128)(2,1)S(1)}, u32[]{:S(2)}, u32[]{:S(2)}) collective-permute-start(bf16[2,32,1280]{2,1,0:T(8,128)(2,1)S(1)} %get-tuple-element.20), channel_id=1, source_target_pairs={{0,2},{1,3},{2,0},{3,1},{4,6},{5,7},{6,4},{7,5},{8,10},{9,11},{10,... | collective-permute-start | bytes 491528 | tf_op jit(solution)/shard_map/ppermute | solution.py:53
  86.1 0.7 collective-permute-start.40
  86.8 1.5 %collective-permute-start.41 = (bf16[2,32,1280]{2,1,0:T(8,128)(2,1)S(1)}, bf16[2,32,1280]{2,1,0:T(8,128)(2,1)S(1)}, u32[]{:S(2)}, u32[]{:S(2)}) collective-permute-start(bf16[2,32,1280]{2,1,0:T(8,128)(2,1)S(1)} %get-tuple-element.21), channel_id=1, source_target_pairs={{0,6},{1,7},{2,4},{3,5},{4,2},{5,3},{6,0},{7,1},{8,14},{9,15},{10,... | collective-permute-start | bytes 491528 | tf_op jit(solution)/shard_map/ppermute | solution.py:53
  88.4 3.4 %collective-permute-done.39 = bf16[2,32,1280]{2,1,0:T(8,128)(2,1)S(1)} collective-permute-done((bf16[2,32,1280]{2,1,0:T(8,128)(2,1)S(1)}, bf16[2,32,1280]{2,1,0:T(8,128)(2,1)S(1)}, u32[]{:S(2)}, u32[]{:S(2)}) %collective-permute-start.39) | collective-permute-done | bytes 163872 | tf_op jit(solution)/shard_map/ppermute | solution.py:53
  91.8 2.7 %collective-permute-done.40 = bf16[2,32,1280]{2,1,0:T(8,128)(2,1)S(1)} collective-permute-done((bf16[2,32,1280]{2,1,0:T(8,128)(2,1)S(1)}, bf16[2,32,1280]{2,1,0:T(8,128)(2,1)S(1)}, u32[]{:S(2)}, u32[]{:S(2)}) %collective-permute-start.40) | collective-permute-done | bytes 163872 | tf_op jit(solution)/shard_map/ppermute | solution.py:53
  94.6 2.8 %collective-permute-start.42 = (bf16[32,1280]{1,0:T(8,128)(2,1)S(1)}, bf16[32,1280]{1,0:T(8,128)(2,1)S(1)}, u32[]{:S(2)}, u32[]{:S(2)}) collective-permute-start(bf16[32,1280]{1,0:T(8,128)(2,1)S(1)} %slice_bitcast_fusion.1), channel_id=1, source_target_pairs={{0,16},{16,24},{24,8},{8,0},{1,17},{17,25},{25,9},{9,1},{2,18},{18... | collective-permute-start | bytes 245768 | tf_op jit(solution)/shard_map/ppermute | solution.py:57
  97.4 0.9 convolution_convert_fusion.3
  99.0 1.0 collective-permute-start.34
  100.0 2.1 %collective-permute-start.35 = (bf16[1,32,1280]{2,1,0:T(8,128)(2,1)S(1)}, bf16[1,32,1280]{2,1,0:T(8,128)(2,1)S(1)}, u32[]{:S(2)}, u32[]{:S(2)}) collective-permute-start(bf16[1,32,1280]{2,1,0:T(8,128)(2,1)S(1)} %get-tuple-element.30), channel_id=1, source_target_pairs={{0,6},{1,7},{2,4},{3,5},{4,2},{5,3},{6,0},{7,1},{8,14},{9,15},{10,... | collective-permute-start | bytes 245768 | tf_op jit(solution)/shard_map/ppermute | solution.py:53
  102.7 1.2 %collective-permute-done.33 = bf16[1,32,1280]{2,1,0:T(8,128)(2,1)S(1)} collective-permute-done((bf16[1,32,1280]{2,1,0:T(8,128)(2,1)S(1)}, bf16[1,32,1280]{2,1,0:T(8,128)(2,1)S(1)}, u32[]{:S(2)}, u32[]{:S(2)}) %collective-permute-start.33) | collective-permute-done | bytes 81952 | tf_op jit(solution)/shard_map/ppermute | solution.py:53
  103.8 0.9 collective-permute-start.29
  104.7 1.1 collective-permute-start.30
  106.2 2.2 %collective-permute-start.36 = (bf16[32,1280]{1,0:T(8,128)(2,1)S(1)}, bf16[32,1280]{1,0:T(8,128)(2,1)S(1)}, u32[]{:S(2)}, u32[]{:S(2)}) collective-permute-start(bf16[32,1280]{1,0:T(8,128)(2,1)S(1)} %fusion.70), channel_id=1, source_target_pairs={{0,24},{16,8},{24,0},{8,16},{1,25},{17,9},{25,1},{9,17},{2,26},{18... | collective-permute-start | bytes 245768 | tf_op jit(solution)/shard_map/ppermute | solution.py:57
  109.0 1.0 collective-permute-done.30
  110.2 4.6 %convolution_multiply_fusion = f32[1280,864]{0,1:T(8,128)} fusion(bf16[256,1280]{1,0:T(8,128)(2,1)S(1)} %bitcast.243, bf16[256,1280]{1,0:T(8,128)(2,1)S(1)} %bitcast.240, bf16[256,1280]{1,0:T(8,128)(2,1)S(1)} %bitcast.237, bf16[256,1280]{1,0:T(8,128)(2,1)S(1)} %bitcast.234, bf16[464,256]{1,0:T(8,128)(2,1)S(1)} %get-tuple-element.25, ...), kind=kOutput, calls=%fused_computation | convolution fusion | flops 2285363200 | bytes 8814592 | tf_op jit(solution)/shard_map/dot_general | solution.py:31
  114.7 0.8 collective-permute-done.31
  115.5 0.7 pad_maximum_fusion.2
  (95 shorter events, 11.2 us)
Async XLA Ops:
  1.7 5.7 %collective-permute-start = (bf16[64,640]{1,0:T(8,128)(2,1)S(1)}, bf16[64,640]{1,0:T(8,128)(2,1)S(1)}, u32[]{:S(2)}, u32[]{:S(2)}) collective-permute-start(bf16[64,640]{1,0:T(8,128)(2,1)S(1)} %get-tuple-element.48), channel_id=1, source_target_pairs={{0,2},{1,3},{2,0},{3,1},{4,6},{5,7},{6,4},{7,5},{8,10},{9,11},{10,... | collective-permute-start | bytes 245768 | tf_op jit(solution)/shard_map/ppermute | solution.py:53
  4.7 5.3 %collective-permute-start.1 = (bf16[64,640]{1,0:T(8,128)(2,1)S(1)}, bf16[64,640]{1,0:T(8,128)(2,1)S(1)}, u32[]{:S(2)}, u32[]{:S(2)}) collective-permute-start(bf16[64,640]{1,0:T(8,128)(2,1)S(1)} %get-tuple-element.47), channel_id=1, source_target_pairs={{0,4},{1,5},{2,6},{3,7},{4,0},{5,1},{6,2},{7,3},{8,12},{9,13},{10,... | collective-permute-start | bytes 245768 | tf_op jit(solution)/shard_map/ppermute | solution.py:53
  6.2 5.3 %collective-permute-start.2 = (bf16[64,640]{1,0:T(8,128)(2,1)S(1)}, bf16[64,640]{1,0:T(8,128)(2,1)S(1)}, u32[]{:S(2)}, u32[]{:S(2)}) collective-permute-start(bf16[64,640]{1,0:T(8,128)(2,1)S(1)} %get-tuple-element.46), channel_id=1, source_target_pairs={{0,6},{1,7},{2,4},{3,5},{4,2},{5,3},{6,0},{7,1},{8,14},{9,15},{10,... | collective-permute-start | bytes 245768 | tf_op jit(solution)/shard_map/ppermute | solution.py:53
  11.7 4.8 %collective-permute-start.3 = (bf16[64,640]{1,0:T(8,128)(2,1)S(1)}, bf16[64,640]{1,0:T(8,128)(2,1)S(1)}, u32[]{:S(2)}, u32[]{:S(2)}) collective-permute-start(bf16[64,640]{1,0:T(8,128)(2,1)S(1)} %get-tuple-element.41), channel_id=1, source_target_pairs={{0,16},{16,24},{24,8},{8,0},{1,17},{17,25},{25,9},{9,1},{2,18},{18... | collective-permute-start | bytes 245768 | tf_op jit(solution)/shard_map/ppermute | solution.py:57
  14.3 6.3 %collective-permute-start.8 = (bf16[64,640]{1,0:T(8,128)(2,1)S(1)}, bf16[64,640]{1,0:T(8,128)(2,1)S(1)}, u32[]{:S(2)}, u32[]{:S(2)}) collective-permute-start(bf16[64,640]{1,0:T(8,128)(2,1)S(1)} %get-tuple-element.44), channel_id=1, source_target_pairs={{0,24},{16,8},{24,0},{8,16},{1,25},{17,9},{25,1},{9,17},{2,26},{18... | collective-permute-start | bytes 245768 | tf_op jit(solution)/shard_map/ppermute | solution.py:57
  15.7 6.3 %collective-permute-start.9 = (bf16[64,640]{1,0:T(8,128)(2,1)S(1)}, bf16[64,640]{1,0:T(8,128)(2,1)S(1)}, u32[]{:S(2)}, u32[]{:S(2)}) collective-permute-start(bf16[64,640]{1,0:T(8,128)(2,1)S(1)} %get-tuple-element.43), channel_id=1, source_target_pairs={{0,8},{16,0},{24,16},{8,24},{1,9},{17,1},{25,17},{9,25},{2,10},{18... | collective-permute-start | bytes 245768 | tf_op jit(solution)/shard_map/ppermute | solution.py:57
  16.5 5.5 %collective-permute-start.4 = (bf16[1,64,640]{2,1,0:T(8,128)(2,1)S(1)}, bf16[1,64,640]{2,1,0:T(8,128)(2,1)S(1)}, u32[]{:S(2)}, u32[]{:S(2)}) collective-permute-start(bf16[1,64,640]{2,1,0:T(8,128)(2,1)S(1)} %bitcast.254), channel_id=1, source_target_pairs={{0,2},{1,3},{2,0},{3,1},{4,6},{5,7},{6,4},{7,5},{8,10},{9,11},{10,... | collective-permute-start | bytes 245768 | tf_op jit(solution)/shard_map/ppermute | solution.py:53
  17.4 6.3 %collective-permute-start.5 = (bf16[1,64,640]{2,1,0:T(8,128)(2,1)S(1)}, bf16[1,64,640]{2,1,0:T(8,128)(2,1)S(1)}, u32[]{:S(2)}, u32[]{:S(2)}) collective-permute-start(bf16[1,64,640]{2,1,0:T(8,128)(2,1)S(1)} %bitcast.255), channel_id=1, source_target_pairs={{0,4},{1,5},{2,6},{3,7},{4,0},{5,1},{6,2},{7,3},{8,12},{9,13},{10,... | collective-permute-start | bytes 245768 | tf_op jit(solution)/shard_map/ppermute | solution.py:53
  18.0 7.7 %collective-permute-start.6 = (bf16[1,64,640]{2,1,0:T(8,128)(2,1)S(1)}, bf16[1,64,640]{2,1,0:T(8,128)(2,1)S(1)}, u32[]{:S(2)}, u32[]{:S(2)}) collective-permute-start(bf16[1,64,640]{2,1,0:T(8,128)(2,1)S(1)} %bitcast.256), channel_id=1, source_target_pairs={{0,6},{1,7},{2,4},{3,5},{4,2},{5,3},{6,0},{7,1},{8,14},{9,15},{10,... | collective-permute-start | bytes 245768 | tf_op jit(solution)/shard_map/ppermute | solution.py:53
  21.9 6.9 %copy-start = (bf16[1280,864]{0,1:T(8,128)(2,1)S(1)}, bf16[1280,864]{0,1:T(8,128)(2,1)}, u32[]{:S(2)}) copy-start(bf16[1280,864]{0,1:T(8,128)(2,1)} %param.4) | copy-start | bytes 6635524
  22.0 15.1 %collective-permute-start.13 = (bf16[3,64,640]{2,1,0:T(8,128)(2,1)S(1)}, bf16[3,64,640]{2,1,0:T(8,128)(2,1)S(1)}, u32[]{:S(2)}, u32[]{:S(2)}) collective-permute-start(bf16[3,64,640]{2,1,0:T(8,128)(2,1)S(1)} %pad_maximum_fusion.3), channel_id=1, source_target_pairs={{0,1},{1,0},{2,3},{3,2},{4,5},{5,4},{6,7},{7,6},{8,9},{9,8},{10,11... | collective-permute-start | bytes 737288 | tf_op jit(solution)/shard_map/ppermute | solution.py:53
  22.1 10.3 %collective-permute-start.10 = (bf16[3,64,640]{2,1,0:T(8,128)(2,1)S(1)}, bf16[3,64,640]{2,1,0:T(8,128)(2,1)S(1)}, u32[]{:S(2)}, u32[]{:S(2)}) collective-permute-start(bf16[3,64,640]{2,1,0:T(8,128)(2,1)S(1)} %pad_maximum_fusion.3), channel_id=1, source_target_pairs={{0,2},{1,3},{2,0},{3,1},{4,6},{5,7},{6,4},{7,5},{8,10},{9,11},{10,... | collective-permute-start | bytes 737288 | tf_op jit(solution)/shard_map/ppermute | solution.py:53
  23.1 13.3 %collective-permute-start.11 = (bf16[3,64,640]{2,1,0:T(8,128)(2,1)S(1)}, bf16[3,64,640]{2,1,0:T(8,128)(2,1)S(1)}, u32[]{:S(2)}, u32[]{:S(2)}) collective-permute-start(bf16[3,64,640]{2,1,0:T(8,128)(2,1)S(1)} %pad_maximum_fusion.3), channel_id=1, source_target_pairs={{0,4},{1,5},{2,6},{3,7},{4,0},{5,1},{6,2},{7,3},{8,12},{9,13},{10,... | collective-permute-start | bytes 737288 | tf_op jit(solution)/shard_map/ppermute | solution.py:53
  23.8 12.7 %collective-permute-start.12 = (bf16[3,64,640]{2,1,0:T(8,128)(2,1)S(1)}, bf16[3,64,640]{2,1,0:T(8,128)(2,1)S(1)}, u32[]{:S(2)}, u32[]{:S(2)}) collective-permute-start(bf16[3,64,640]{2,1,0:T(8,128)(2,1)S(1)} %pad_maximum_fusion.3), channel_id=1, source_target_pairs={{0,6},{1,7},{2,4},{3,5},{4,2},{5,3},{6,0},{7,1},{8,14},{9,15},{10,... | collective-permute-start | bytes 737288 | tf_op jit(solution)/shard_map/ppermute | solution.py:53
  29.9 10.0 %collective-permute-start.7 = (bf16[400,256]{1,0:T(8,128)(2,1)S(1)}, bf16[400,256]{1,0:T(8,128)(2,1)S(1)}, u32[]{:S(2)}, u32[]{:S(2)}) collective-permute-start(bf16[400,256]{1,0:T(8,128)(2,1)S(1)} %fusion.17), channel_id=1, source_target_pairs={{0,16},{16,24},{24,8},{8,0},{1,17},{17,25},{25,9},{9,1},{2,18},{18... | collective-permute-start | bytes 614408 | tf_op jit(solution)/shard_map/ppermute | solution.py:57
  32.4 12.9 %collective-permute-start.19 = (bf16[464,256]{1,0:T(8,128)(2,1)S(1)}, bf16[464,256]{1,0:T(8,128)(2,1)S(1)}, u32[]{:S(2)}, u32[]{:S(2)}) collective-permute-start(bf16[464,256]{1,0:T(8,128)(2,1)S(1)} %fusion.16), channel_id=1, source_target_pairs={{0,16},{16,24},{24,8},{8,0},{1,17},{17,25},{25,9},{9,1},{2,18},{18... | collective-permute-start | bytes 712712 | tf_op jit(solution)/shard_map/ppermute | solution.py:57
  36.4 1.5 %collective-permute-start.14 = (bf16[3,64,640]{2,1,0:T(8,128)(2,1)S(1)}, bf16[3,64,640]{2,1,0:T(8,128)(2,1)S(1)}, u32[]{:S(2)}, u32[]{:S(2)}) collective-permute-start(bf16[3,64,640]{2,1,0:T(8,128)(2,1)S(1)} %collective-permute-done.10), channel_id=1, source_target_pairs={{0,1},{1,0},{2,3},{3,2},{4,5},{5,4},{6,7},{7,6},{8,9},{9,8},{10,11... | collective-permute-start | bytes 737288 | tf_op jit(solution)/shard_map/ppermute | solution.py:53
  36.5 1.8 %collective-permute-start.15 = (bf16[3,64,640]{2,1,0:T(8,128)(2,1)S(1)}, bf16[3,64,640]{2,1,0:T(8,128)(2,1)S(1)}, u32[]{:S(2)}, u32[]{:S(2)}) collective-permute-start(bf16[3,64,640]{2,1,0:T(8,128)(2,1)S(1)} %collective-permute-done.11), channel_id=1, source_target_pairs={{0,1},{1,0},{2,3},{3,2},{4,5},{5,4},{6,7},{7,6},{8,9},{9,8},{10,11... | collective-permute-start | bytes 737288 | tf_op jit(solution)/shard_map/ppermute | solution.py:53
  37.1 1.6 %collective-permute-start.16 = (bf16[3,64,640]{2,1,0:T(8,128)(2,1)S(1)}, bf16[3,64,640]{2,1,0:T(8,128)(2,1)S(1)}, u32[]{:S(2)}, u32[]{:S(2)}) collective-permute-start(bf16[3,64,640]{2,1,0:T(8,128)(2,1)S(1)} %collective-permute-done.12), channel_id=1, source_target_pairs={{0,1},{1,0},{2,3},{3,2},{4,5},{5,4},{6,7},{7,6},{8,9},{9,8},{10,11... | collective-permute-start | bytes 737288 | tf_op jit(solution)/shard_map/ppermute | solution.py:53
  40.4 7.8 %collective-permute-start.17 = (bf16[400,256]{1,0:T(8,128)(2,1)S(1)}, bf16[400,256]{1,0:T(8,128)(2,1)S(1)}, u32[]{:S(2)}, u32[]{:S(2)}) collective-permute-start(bf16[400,256]{1,0:T(8,128)(2,1)S(1)} %add_convert_fusion.3), channel_id=1, source_target_pairs={{0,16},{16,24},{24,8},{8,0},{1,17},{17,25},{25,9},{9,1},{2,18},{18... | collective-permute-start | bytes 614408 | tf_op jit(solution)/shard_map/ppermute | solution.py:57
  45.8 8.7 %collective-permute-start.20 = (bf16[464,256]{1,0:T(8,128)(2,1)S(1)}, bf16[464,256]{1,0:T(8,128)(2,1)S(1)}, u32[]{:S(2)}, u32[]{:S(2)}) collective-permute-start(bf16[464,256]{1,0:T(8,128)(2,1)S(1)} %add_convert_fusion.1), channel_id=1, source_target_pairs={{0,16},{16,24},{24,8},{8,0},{1,17},{17,25},{25,9},{9,1},{2,18},{18... | collective-permute-start | bytes 712712 | tf_op jit(solution)/shard_map/ppermute | solution.py:57
  47.0 11.9 %copy-start.1 = (bf16[256,864]{0,1:T(8,128)(2,1)S(1)}, bf16[256,864]{0,1:T(8,128)(2,1)}, u32[]{:S(2)}) copy-start(bf16[256,864]{0,1:T(8,128)(2,1)} %param.5) | copy-start | bytes 1327108
  48.2 10.6 %collective-permute-start.18 = (bf16[400,256]{1,0:T(8,128)(2,1)S(1)}, bf16[400,256]{1,0:T(8,128)(2,1)S(1)}, u32[]{:S(2)}, u32[]{:S(2)}) collective-permute-start(bf16[400,256]{1,0:T(8,128)(2,1)S(1)} %add_convert_fusion.2), channel_id=1, source_target_pairs={{0,16},{16,24},{24,8},{8,0},{1,17},{17,25},{25,9},{9,1},{2,18},{18... | collective-permute-start | bytes 614408 | tf_op jit(solution)/shard_map/ppermute | solution.py:57
  54.6 8.5 %collective-permute-start.21 = (bf16[464,256]{1,0:T(8,128)(2,1)S(1)}, bf16[464,256]{1,0:T(8,128)(2,1)S(1)}, u32[]{:S(2)}, u32[]{:S(2)}) collective-permute-start(bf16[464,256]{1,0:T(8,128)(2,1)S(1)} %add_convert_fusion), channel_id=1, source_target_pairs={{0,16},{16,24},{24,8},{8,0},{1,17},{17,25},{25,9},{9,1},{2,18},{18... | collective-permute-start | bytes 712712 | tf_op jit(solution)/shard_map/ppermute | solution.py:57
  59.3 9.6 %collective-permute-start.22 = (bf16[400,256]{1,0:T(8,128)(2,1)S(1)}, bf16[400,256]{1,0:T(8,128)(2,1)S(1)}, u32[]{:S(2)}, u32[]{:S(2)}) collective-permute-start(bf16[400,256]{1,0:T(8,128)(2,1)S(1)} %get-tuple-element.35), channel_id=1, source_target_pairs={{0,8},{16,0},{24,16},{8,24},{1,9},{17,1},{25,17},{9,25},{2,10},{18... | collective-permute-start | bytes 614408 | tf_op jit(solution)/shard_map/ppermute | solution.py:57
  63.6 10.5 %collective-permute-start.24 = (bf16[464,256]{1,0:T(8,128)(2,1)S(1)}, bf16[464,256]{1,0:T(8,128)(2,1)S(1)}, u32[]{:S(2)}, u32[]{:S(2)}) collective-permute-start(bf16[464,256]{1,0:T(8,128)(2,1)S(1)} %get-tuple-element.25), channel_id=1, source_target_pairs={{0,8},{16,0},{24,16},{8,24},{1,9},{17,1},{25,17},{9,25},{2,10},{18... | collective-permute-start | bytes 712712 | tf_op jit(solution)/shard_map/ppermute | solution.py:57
  68.9 9.1 %collective-permute-start.23 = (bf16[400,256]{1,0:T(8,128)(2,1)S(1)}, bf16[400,256]{1,0:T(8,128)(2,1)S(1)}, u32[]{:S(2)}, u32[]{:S(2)}) collective-permute-start(bf16[400,256]{1,0:T(8,128)(2,1)S(1)} %collective-permute-done.22), channel_id=1, source_target_pairs={{0,8},{16,0},{24,16},{8,24},{1,9},{17,1},{25,17},{9,25},{2,10},{18... | collective-permute-start | bytes 614408 | tf_op jit(solution)/shard_map/ppermute | solution.py:57
  75.1 8.1 %collective-permute-start.25 = (bf16[464,256]{1,0:T(8,128)(2,1)S(1)}, bf16[464,256]{1,0:T(8,128)(2,1)S(1)}, u32[]{:S(2)}, u32[]{:S(2)}) collective-permute-start(bf16[464,256]{1,0:T(8,128)(2,1)S(1)} %collective-permute-done.24), channel_id=1, source_target_pairs={{0,8},{16,0},{24,16},{8,24},{1,9},{17,1},{25,17},{9,25},{2,10},{18... | collective-permute-start | bytes 712712 | tf_op jit(solution)/shard_map/ppermute | solution.py:57
  76.4 8.1 %collective-permute-start.37 = (bf16[2,2,32,1280]{3,2,0,1:T(8,128)(2,1)S(1)}, bf16[2,2,32,1280]{3,2,0,1:T(8,128)(2,1)S(1)}, u32[]{:S(2)}, u32[]{:S(2)}) collective-permute-start(bf16[2,2,32,1280]{3,2,0,1:T(8,128)(2,1)S(1)} %get-tuple-element.27), channel_id=1, source_target_pairs={{0,1},{1,0},{2,3},{3,2},{4,5},{5,4},{6,7},{7,6},{8,9},{9,8},{10,11... | collective-permute-start | bytes 983048 | tf_op jit(solution)/shard_map/ppermute | solution.py:53
  76.4 8.1 %collective-permute-start.38 = (bf16[2,2,32,1280]{3,2,0,1:T(8,128)(2,1)S(1)}, bf16[2,2,32,1280]{3,2,0,1:T(8,128)(2,1)S(1)}, u32[]{:S(2)}, u32[]{:S(2)}) collective-permute-start(bf16[2,2,32,1280]{3,2,0,1:T(8,128)(2,1)S(1)} %get-tuple-element.28), channel_id=1, source_target_pairs={{0,1},{1,0},{2,3},{3,2},{4,5},{5,4},{6,7},{7,6},{8,9},{9,8},{10,11... | collective-permute-start | bytes 983048 | tf_op jit(solution)/shard_map/ppermute | solution.py:53
  83.2 14.2 %collective-permute-start.26 = (bf16[864,256]{1,0:T(8,128)(2,1)S(1)}, bf16[864,256]{1,0:T(8,128)(2,1)S(1)}, u32[]{:S(2)}, u32[]{:S(2)}) collective-permute-start(bf16[864,256]{1,0:T(8,128)(2,1)S(1)} %constant_dynamic-update-slice_fusion), channel_id=1, source_target_pairs={{0,8},{16,0},{24,16},{8,24},{1,9},{17,1},{25,17},{9,25},{2,10},{18... | collective-permute-start | bytes 1327112 | tf_op jit(solution)/shard_map/ppermute | solution.py:57
  84.7 7.1 %collective-permute-start.39 = (bf16[2,32,1280]{2,1,0:T(8,128)(2,1)S(1)}, bf16[2,32,1280]{2,1,0:T(8,128)(2,1)S(1)}, u32[]{:S(2)}, u32[]{:S(2)}) collective-permute-start(bf16[2,32,1280]{2,1,0:T(8,128)(2,1)S(1)} %get-tuple-element.20), channel_id=1, source_target_pairs={{0,2},{1,3},{2,0},{3,1},{4,6},{5,7},{6,4},{7,5},{8,10},{9,11},{10,... | collective-permute-start | bytes 491528 | tf_op jit(solution)/shard_map/ppermute | solution.py:53
  86.1 8.4 %collective-permute-start.40 = (bf16[2,32,1280]{2,1,0:T(8,128)(2,1)S(1)}, bf16[2,32,1280]{2,1,0:T(8,128)(2,1)S(1)}, u32[]{:S(2)}, u32[]{:S(2)}) collective-permute-start(bf16[2,32,1280]{2,1,0:T(8,128)(2,1)S(1)} %get-tuple-element.22), channel_id=1, source_target_pairs={{0,4},{1,5},{2,6},{3,7},{4,0},{5,1},{6,2},{7,3},{8,12},{9,13},{10,... | collective-permute-start | bytes 491528 | tf_op jit(solution)/shard_map/ppermute | solution.py:53
  86.8 7.7 %collective-permute-start.41 = (bf16[2,32,1280]{2,1,0:T(8,128)(2,1)S(1)}, bf16[2,32,1280]{2,1,0:T(8,128)(2,1)S(1)}, u32[]{:S(2)}, u32[]{:S(2)}) collective-permute-start(bf16[2,32,1280]{2,1,0:T(8,128)(2,1)S(1)} %get-tuple-element.21), channel_id=1, source_target_pairs={{0,6},{1,7},{2,4},{3,5},{4,2},{5,3},{6,0},{7,1},{8,14},{9,15},{10,... | collective-permute-start | bytes 491528 | tf_op jit(solution)/shard_map/ppermute | solution.py:53
  88.3 10.1 %collective-permute-start.32 = (bf16[1,4,32,1280]{3,2,1,0:T(8,128)(2,1)S(1)}, bf16[1,4,32,1280]{3,2,1,0:T(8,128)(2,1)S(1)}, u32[]{:S(2)}, u32[]{:S(2)}) collective-permute-start(bf16[1,4,32,1280]{3,2,1,0:T(8,128)(2,1)S(1)} %dynamic-slice_bitcast_fusion), channel_id=1, source_target_pairs={{0,1},{1,0},{2,3},{3,2},{4,5},{5,4},{6,7},{7,6},{8,9},{9,8},{10,11... | collective-permute-start | bytes 983048 | tf_op jit(solution)/shard_map/ppermute | solution.py:53
  94.6 20.1 %collective-permute-start.42 = (bf16[32,1280]{1,0:T(8,128)(2,1)S(1)}, bf16[32,1280]{1,0:T(8,128)(2,1)S(1)}, u32[]{:S(2)}, u32[]{:S(2)}) collective-permute-start(bf16[32,1280]{1,0:T(8,128)(2,1)S(1)} %slice_bitcast_fusion.1), channel_id=1, source_target_pairs={{0,16},{16,24},{24,8},{8,0},{1,17},{17,25},{25,9},{9,1},{2,18},{18... | collective-permute-start | bytes 245768 | tf_op jit(solution)/shard_map/ppermute | solution.py:57
  98.3 3.8 %collective-permute-start.27 = (bf16[1,4,32,1280]{3,2,1,0:T(8,128)(2,1)S(1)}, bf16[1,4,32,1280]{3,2,1,0:T(8,128)(2,1)S(1)}, u32[]{:S(2)}, u32[]{:S(2)}) collective-permute-start(bf16[1,4,32,1280]{3,2,1,0:T(8,128)(2,1)S(1)} %dynamic-slice_bitcast_fusion.1), channel_id=1, source_target_pairs={{0,1},{1,0},{2,3},{3,2},{4,5},{5,4},{6,7},{7,6},{8,9},{9,8},{10,11... | collective-permute-start | bytes 983048 | tf_op jit(solution)/shard_map/ppermute | solution.py:53
  98.5 5.3 %collective-permute-start.33 = (bf16[1,32,1280]{2,1,0:T(8,128)(2,1)S(1)}, bf16[1,32,1280]{2,1,0:T(8,128)(2,1)S(1)}, u32[]{:S(2)}, u32[]{:S(2)}) collective-permute-start(bf16[1,32,1280]{2,1,0:T(8,128)(2,1)S(1)} %get-tuple-element.29), channel_id=1, source_target_pairs={{0,2},{1,3},{2,0},{3,1},{4,6},{5,7},{6,4},{7,5},{8,10},{9,11},{10,... | collective-permute-start | bytes 245768 | tf_op jit(solution)/shard_map/ppermute | solution.py:53
  99.0 5.7 %collective-permute-start.34 = (bf16[1,32,1280]{2,1,0:T(8,128)(2,1)S(1)}, bf16[1,32,1280]{2,1,0:T(8,128)(2,1)S(1)}, u32[]{:S(2)}, u32[]{:S(2)}) collective-permute-start(bf16[1,32,1280]{2,1,0:T(8,128)(2,1)S(1)} %get-tuple-element.31), channel_id=1, source_target_pairs={{0,4},{1,5},{2,6},{3,7},{4,0},{5,1},{6,2},{7,3},{8,12},{9,13},{10,... | collective-permute-start | bytes 245768 | tf_op jit(solution)/shard_map/ppermute | solution.py:53
  100.0 6.2 %collective-permute-start.35 = (bf16[1,32,1280]{2,1,0:T(8,128)(2,1)S(1)}, bf16[1,32,1280]{2,1,0:T(8,128)(2,1)S(1)}, u32[]{:S(2)}, u32[]{:S(2)}) collective-permute-start(bf16[1,32,1280]{2,1,0:T(8,128)(2,1)S(1)} %get-tuple-element.30), channel_id=1, source_target_pairs={{0,6},{1,7},{2,4},{3,5},{4,2},{5,3},{6,0},{7,1},{8,14},{9,15},{10,... | collective-permute-start | bytes 245768 | tf_op jit(solution)/shard_map/ppermute | solution.py:53
  102.2 6.2 %collective-permute-start.28 = (bf16[1,32,1280]{2,1,0:T(8,128)(2,1)S(1)}, bf16[1,32,1280]{2,1,0:T(8,128)(2,1)S(1)}, u32[]{:S(2)}, u32[]{:S(2)}) collective-permute-start(bf16[1,32,1280]{2,1,0:T(8,128)(2,1)S(1)} %get-tuple-element.34), channel_id=1, source_target_pairs={{0,2},{1,3},{2,0},{3,1},{4,6},{5,7},{6,4},{7,5},{8,10},{9,11},{10,... | collective-permute-start | bytes 245768 | tf_op jit(solution)/shard_map/ppermute | solution.py:53
  103.8 5.2 %collective-permute-start.29 = (bf16[1,32,1280]{2,1,0:T(8,128)(2,1)S(1)}, bf16[1,32,1280]{2,1,0:T(8,128)(2,1)S(1)}, u32[]{:S(2)}, u32[]{:S(2)}) collective-permute-start(bf16[1,32,1280]{2,1,0:T(8,128)(2,1)S(1)} %get-tuple-element.33), channel_id=1, source_target_pairs={{0,4},{1,5},{2,6},{3,7},{4,0},{5,1},{6,2},{7,3},{8,12},{9,13},{10,... | collective-permute-start | bytes 245768 | tf_op jit(solution)/shard_map/ppermute | solution.py:53
  104.7 5.3 %collective-permute-start.30 = (bf16[1,32,1280]{2,1,0:T(8,128)(2,1)S(1)}, bf16[1,32,1280]{2,1,0:T(8,128)(2,1)S(1)}, u32[]{:S(2)}, u32[]{:S(2)}) collective-permute-start(bf16[1,32,1280]{2,1,0:T(8,128)(2,1)S(1)} %get-tuple-element.32), channel_id=1, source_target_pairs={{0,6},{1,7},{2,4},{3,5},{4,2},{5,3},{6,0},{7,1},{8,14},{9,15},{10,... | collective-permute-start | bytes 245768 | tf_op jit(solution)/shard_map/ppermute | solution.py:53
  106.2 8.5 %collective-permute-start.36 = (bf16[32,1280]{1,0:T(8,128)(2,1)S(1)}, bf16[32,1280]{1,0:T(8,128)(2,1)S(1)}, u32[]{:S(2)}, u32[]{:S(2)}) collective-permute-start(bf16[32,1280]{1,0:T(8,128)(2,1)S(1)} %fusion.70), channel_id=1, source_target_pairs={{0,24},{16,8},{24,0},{8,16},{1,25},{17,9},{25,1},{9,17},{2,26},{18... | collective-permute-start | bytes 245768 | tf_op jit(solution)/shard_map/ppermute | solution.py:57
  110.1 5.4 %collective-permute-start.31 = (bf16[32,1280]{1,0:T(8,128)(2,1)S(1)}, bf16[32,1280]{1,0:T(8,128)(2,1)S(1)}, u32[]{:S(2)}, u32[]{:S(2)}) collective-permute-start(bf16[32,1280]{1,0:T(8,128)(2,1)S(1)} %fusion.69), channel_id=1, source_target_pairs={{0,8},{16,0},{24,16},{8,24},{1,9},{17,1},{25,17},{9,25},{2,10},{18... | collective-permute-start | bytes 245768 | tf_op jit(solution)/shard_map/ppermute | solution.py:57

commit v6 on v5

--- a/solution.py
+++ b/solution.py
@@ -38,7 +38,7 @@
     tok, width = activations.shape
     sub = tok // n_col
     depth, units = up_weight.shape
-    cuts = [0, (units // 2 - 32) // 16 * 16, units]
+    cuts = [0, (units // 2 - 16) // 16 * 16, units]
     flipped = up_weight.T
 
     plane_at = list(range(0, n_row, 2)) + list(range(1, n_row, 2))[::-1]
@@ -81,7 +81,7 @@
 
     def fetch(blocks):
         held = jnp.stack(blocks)
-        return [held] + [across(held, cores * e) for e in range(1, chips)]
+        return [held] + [across(held, cores * e) for e in range(chips - 1, 0, -1)][::-1]
 
     def lay(pieces):
         count, part, breadth = pieces[0].shape
@@ -96,7 +96,15 @@
 
     def gather_one(pieces):
         pairs = [list(range(i, i + cores)) for i in range(0, n_col, cores)]
-        return blocks_of(lax.all_gather(lay(pieces), "col", axis=3 if halved else 2, axis_index_groups=pairs))
+        whole = lax.all_gather(lay(pieces), "col", axis=3 if halved else 2, axis_index_groups=pairs)
+        tokens = blocks_of(whole)
+        if not halved:
+            return tokens, terms_of(tokens[0])
+        sides = [whole[0, :, :, k].reshape(tok, width) for k in range(cores)]
+        return tokens, [
+            sum(product(part[:, k * width:(k + 1) * width], sides[k], ((1,), (1,))) for k in range(cores))
+            for part in split(flipped)
+        ]
 
     def gather(pieces):
         others = [across(piece, 1) for piece in pieces]
@@ -110,9 +118,9 @@
     order = list(range(1, n_row)) + [0]
     early = fetch([arrived[order[0]]])
     late = fetch(after([arrived[k] for k in order[1:]], early[1]))
-    tokens = gather_one(early)
+    tokens, first_terms = gather_one(early)
 
-    flow = [narrow(t) for t in terms_of(tokens[0])]
+    flow = [narrow(t) for t in first_terms]
     for j in range(1, n_row):
         flow = [along(f, 1) for f in flow]
         if j == 1:

time: 116 us -> 116 us (level)
  waiting for transfers between devices: 41 us -> 39.2 us
    ppermute x26, waiting for transfers between devices: 19 us -> 17.5 us  [across(): return lax.ppermute(array, 'col', [(i, i ^ flip) for i in range(n_col)])]
    dot_general x13 -> x15, matrix products: 11.9 us -> 12.4 us  [product(): lax.dot_general(left, right, (axes, ((), ())), preferred_element_type=jnp...]
  transfers between devices with their start and end apart: 43 -> 43, of which waited for: 24 -> 23; matrix products, arithmetic and copies ran while one was open for 16% -> 17% of each run, Pallas kernels for 0% -> 0%
where the time goes in v6:
time: 116 us
  starting transfers between devices  52 us (45%)
  waiting for transfers between devices  39.2 us (34%)
  matrix products  12.4 us (11%)
  local copies, waits for them, and re-layouts  5.03 us (4%)
  other arithmetic  3.73 us (3%)
  blocking collectives  2.28 us (2%)
  between operations  1.23 us (1%)
    ppermute x17, starting transfers between devices, along(): return lax.ppermute(array, 'row', pairs)  28.6 us
    ppermute x26, starting transfers between devices, across(): return lax.ppermute(array, 'col', [(i, i ^ flip) for i in range(n_col)])  23.5 us
    ppermute x17, waiting for transfers between devices, along(): return lax.ppermute(array, 'row', pairs)  21.8 us
    ppermute x26, waiting for transfers between devices, across(): return lax.ppermute(array, 'col', [(i, i ^ flip) for i in range(n_col)])  17.5 us
    dot_general x15, matrix products, product(): lax.dot_general(left, right, (axes, ((), ())), preferred_element_type=jnp...  12.4 us
  transfers between devices with their start and end apart: 43, of which 23 were waited for; matrix products, arithmetic and copies ran while one was open for 17% of the time, Pallas kernels for 0%

profile of v6, /device:TPU:0, one launch (start us, length us, event | category | flops | bytes accessed | tf_op | source)
XLA Modules:
  0.0 116.0 jit_solution(14917715506091435699)
XLA Ops:
  0.7 1.0 constant_dynamic-slice_fusion
  1.7 3.0 %collective-permute-start = (bf16[64,640]{1,0:T(8,128)(2,1)S(1)}, bf16[64,640]{1,0:T(8,128)(2,1)S(1)}, u32[]{:S(2)}, u32[]{:S(2)}) collective-permute-start(bf16[64,640]{1,0:T(8,128)(2,1)S(1)} %get-tuple-element.50), channel_id=1, source_target_pairs={{0,2},{1,3},{2,0},{3,1},{4,6},{5,7},{6,4},{7,5},{8,10},{9,11},{10,... | collective-permute-start | bytes 245768 | tf_op jit(solution)/shard_map/ppermute | solution.py:53
  4.7 1.5 %collective-permute-start.1 = (bf16[64,640]{1,0:T(8,128)(2,1)S(1)}, bf16[64,640]{1,0:T(8,128)(2,1)S(1)}, u32[]{:S(2)}, u32[]{:S(2)}) collective-permute-start(bf16[64,640]{1,0:T(8,128)(2,1)S(1)} %get-tuple-element.49), channel_id=1, source_target_pairs={{0,4},{1,5},{2,6},{3,7},{4,0},{5,1},{6,2},{7,3},{8,12},{9,13},{10,... | collective-permute-start | bytes 245768 | tf_op jit(solution)/shard_map/ppermute | solution.py:53
  6.3 1.2 %collective-permute-done = bf16[64,640]{1,0:T(8,128)(2,1)S(1)} collective-permute-done((bf16[64,640]{1,0:T(8,128)(2,1)S(1)}, bf16[64,640]{1,0:T(8,128)(2,1)S(1)}, u32[]{:S(2)}, u32[]{:S(2)}) %collective-permute-start) | collective-permute-done | bytes 81952 | tf_op jit(solution)/shard_map/ppermute | solution.py:53
  7.4 2.6 %collective-permute-done.1 = bf16[64,640]{1,0:T(8,128)(2,1)S(1)} collective-permute-done((bf16[64,640]{1,0:T(8,128)(2,1)S(1)}, bf16[64,640]{1,0:T(8,128)(2,1)S(1)}, u32[]{:S(2)}, u32[]{:S(2)}) %collective-permute-start.1) | collective-permute-done | bytes 81952 | tf_op jit(solution)/shard_map/ppermute | solution.py:53
  10.0 1.5 %collective-permute-done.2 = bf16[64,640]{1,0:T(8,128)(2,1)S(1)} collective-permute-done((bf16[64,640]{1,0:T(8,128)(2,1)S(1)}, bf16[64,640]{1,0:T(8,128)(2,1)S(1)}, u32[]{:S(2)}, u32[]{:S(2)}) %collective-permute-start.2) | collective-permute-done | bytes 81952 | tf_op jit(solution)/shard_map/ppermute | solution.py:53
  11.7 2.6 %collective-permute-start.3 = (bf16[64,640]{1,0:T(8,128)(2,1)S(1)}, bf16[64,640]{1,0:T(8,128)(2,1)S(1)}, u32[]{:S(2)}, u32[]{:S(2)}) collective-permute-start(bf16[64,640]{1,0:T(8,128)(2,1)S(1)} %get-tuple-element.43), channel_id=1, source_target_pairs={{0,16},{16,24},{24,8},{8,0},{1,17},{17,25},{25,9},{9,1},{2,18},{18... | collective-permute-start | bytes 245768 | tf_op jit(solution)/shard_map/ppermute | solution.py:57
  14.3 1.3 %collective-permute-start.8 = (bf16[64,640]{1,0:T(8,128)(2,1)S(1)}, bf16[64,640]{1,0:T(8,128)(2,1)S(1)}, u32[]{:S(2)}, u32[]{:S(2)}) collective-permute-start(bf16[64,640]{1,0:T(8,128)(2,1)S(1)} %get-tuple-element.46), channel_id=1, source_target_pairs={{0,24},{16,8},{24,0},{8,16},{1,25},{17,9},{25,1},{9,17},{2,26},{18... | collective-permute-start | bytes 245768 | tf_op jit(solution)/shard_map/ppermute | solution.py:57
  15.7 0.8 collective-permute-start.9
  16.5 1.0 collective-permute-start.4
  17.4 0.6 collective-permute-start.5
  18.1 1.9 %collective-permute-start.6 = (bf16[1,64,640]{2,1,0:T(8,128)(2,1)S(1)}, bf16[1,64,640]{2,1,0:T(8,128)(2,1)S(1)}, u32[]{:S(2)}, u32[]{:S(2)}) collective-permute-start(bf16[1,64,640]{2,1,0:T(8,128)(2,1)S(1)} %bitcast.267), channel_id=1, source_target_pairs={{0,6},{1,7},{2,4},{3,5},{4,2},{5,3},{6,0},{7,1},{8,14},{9,15},{10,... | collective-permute-start | bytes 245768 | tf_op jit(solution)/shard_map/ppermute | solution.py:53
  20.0 0.7 collective-permute-done.8
  20.7 1.3 %collective-permute-done.9 = bf16[64,640]{1,0:T(8,128)(2,1)S(1)} collective-permute-done((bf16[64,640]{1,0:T(8,128)(2,1)S(1)}, bf16[64,640]{1,0:T(8,128)(2,1)S(1)}, u32[]{:S(2)}, u32[]{:S(2)}) %collective-permute-start.9) | collective-permute-done | bytes 81952 | tf_op jit(solution)/shard_map/ppermute | solution.py:57
  22.1 1.1 collective-permute-start.10
  23.1 0.6 collective-permute-start.11
  23.8 1.9 %collective-permute-start.12 = (bf16[3,64,640]{2,1,0:T(8,128)(2,1)S(1)}, bf16[3,64,640]{2,1,0:T(8,128)(2,1)S(1)}, u32[]{:S(2)}, u32[]{:S(2)}) collective-permute-start(bf16[3,64,640]{2,1,0:T(8,128)(2,1)S(1)} %pad_maximum_fusion.3), channel_id=1, source_target_pairs={{0,6},{1,7},{2,4},{3,5},{4,2},{5,3},{6,0},{7,1},{8,14},{9,15},{10,... | collective-permute-start | bytes 737288 | tf_op jit(solution)/shard_map/ppermute | solution.py:53
  25.8 2.3 %all_gather.19 = bf16[1,4,64,2,640]{4,2,1,0,3:T(8,128)(2,1)S(1)} all-gather(bf16[1,4,64,1,640]{4,2,1,0,3:T(8,128)(2,1)S(1)} %bitcast_dynamic-update-slice_fusion.8), channel_id=1, replica_groups={{0,1},{2,3},{4,5},{6,7},{8,9},{10,11},{12,13},{14,15},{16,17},{18,19},{..., dimensions={3}, use_global_device_ids=true | all-gather | bytes 983040 | tf_op jit(solution)/shard_map/all_gather | solution.py:99
  29.2 2.4 %collective-permute-start.7 = (bf16[416,256]{1,0:T(8,128)(2,1)S(1)}, bf16[416,256]{1,0:T(8,128)(2,1)S(1)}, u32[]{:S(2)}, u32[]{:S(2)}) collective-permute-start(bf16[416,256]{1,0:T(8,128)(2,1)S(1)} %fusion.19), channel_id=1, source_target_pairs={{0,16},{16,24},{24,8},{8,0},{1,17},{17,25},{25,9},{9,1},{2,18},{18... | collective-permute-start | bytes 638984 | tf_op jit(solution)/shard_map/ppermute | solution.py:57
  32.2 0.7 copy.64
  33.0 0.9 collective-permute-start.19
  34.0 2.5 %collective-permute-done.11 = bf16[3,64,640]{2,1,0:T(8,128)(2,1)S(1)} collective-permute-done((bf16[3,64,640]{2,1,0:T(8,128)(2,1)S(1)}, bf16[3,64,640]{2,1,0:T(8,128)(2,1)S(1)}, u32[]{:S(2)}, u32[]{:S(2)}) %collective-permute-start.11) | collective-permute-done | bytes 245792 | tf_op jit(solution)/shard_map/ppermute | solution.py:53
  36.5 0.6 collective-permute-start.15
  37.3 0.6 collective-permute-done.14
  39.1 0.7 copy.57
  40.4 2.4 %collective-permute-start.17 = (bf16[416,256]{1,0:T(8,128)(2,1)S(1)}, bf16[416,256]{1,0:T(8,128)(2,1)S(1)}, u32[]{:S(2)}, u32[]{:S(2)}) collective-permute-start(bf16[416,256]{1,0:T(8,128)(2,1)S(1)} %add_convert_fusion.3), channel_id=1, source_target_pairs={{0,16},{16,24},{24,8},{8,0},{1,17},{17,25},{25,9},{9,1},{2,18},{18... | collective-permute-start | bytes 638984 | tf_op jit(solution)/shard_map/ppermute | solution.py:57
  42.8 0.7 copy.58
  43.5 0.7 copy.59
  45.8 0.7 collective-permute-start.20
  47.5 0.9 collective-permute-done.17
  48.4 3.4 %collective-permute-start.18 = (bf16[416,256]{1,0:T(8,128)(2,1)S(1)}, bf16[416,256]{1,0:T(8,128)(2,1)S(1)}, u32[]{:S(2)}, u32[]{:S(2)}) collective-permute-start(bf16[416,256]{1,0:T(8,128)(2,1)S(1)} %add_convert_fusion.2), channel_id=1, source_target_pairs={{0,16},{16,24},{24,8},{8,0},{1,17},{17,25},{25,9},{9,1},{2,18},{18... | collective-permute-start | bytes 638984 | tf_op jit(solution)/shard_map/ppermute | solution.py:57
  51.9 2.5 %collective-permute-done.20 = bf16[448,256]{1,0:T(8,128)(2,1)S(1)} collective-permute-done((bf16[448,256]{1,0:T(8,128)(2,1)S(1)}, bf16[448,256]{1,0:T(8,128)(2,1)S(1)}, u32[]{:S(2)}, u32[]{:S(2)}) %collective-permute-start.20) | collective-permute-done | bytes 229408 | tf_op jit(solution)/shard_map/ppermute | solution.py:57
  54.4 2.4 %collective-permute-start.21 = (bf16[448,256]{1,0:T(8,128)(2,1)S(1)}, bf16[448,256]{1,0:T(8,128)(2,1)S(1)}, u32[]{:S(2)}, u32[]{:S(2)}) collective-permute-start(bf16[448,256]{1,0:T(8,128)(2,1)S(1)} %add_convert_fusion), channel_id=1, source_target_pairs={{0,16},{16,24},{24,8},{8,0},{1,17},{17,25},{25,9},{9,1},{2,18},{18... | collective-permute-start | bytes 688136 | tf_op jit(solution)/shard_map/ppermute | solution.py:57
  56.8 2.1 %collective-permute-done.18 = bf16[416,256]{1,0:T(8,128)(2,1)S(1)} collective-permute-done((bf16[416,256]{1,0:T(8,128)(2,1)S(1)}, bf16[416,256]{1,0:T(8,128)(2,1)S(1)}, u32[]{:S(2)}, u32[]{:S(2)}) %collective-permute-start.18) | collective-permute-done | bytes 213024 | tf_op jit(solution)/shard_map/ppermute | solution.py:57
  59.3 1.7 %collective-permute-start.22 = (bf16[416,256]{1,0:T(8,128)(2,1)S(1)}, bf16[416,256]{1,0:T(8,128)(2,1)S(1)}, u32[]{:S(2)}, u32[]{:S(2)}) collective-permute-start(bf16[416,256]{1,0:T(8,128)(2,1)S(1)} %get-tuple-element.37), channel_id=1, source_target_pairs={{0,8},{16,0},{24,16},{8,24},{1,9},{17,1},{25,17},{9,25},{2,10},{18... | collective-permute-start | bytes 638984 | tf_op jit(solution)/shard_map/ppermute | solution.py:57
  61.0 1.9 %collective-permute-done.21 = bf16[448,256]{1,0:T(8,128)(2,1)S(1)} collective-permute-done((bf16[448,256]{1,0:T(8,128)(2,1)S(1)}, bf16[448,256]{1,0:T(8,128)(2,1)S(1)}, u32[]{:S(2)}, u32[]{:S(2)}) %collective-permute-start.21) | collective-permute-done | bytes 229408 | tf_op jit(solution)/shard_map/ppermute | solution.py:57
  63.4 2.7 %collective-permute-start.24 = (bf16[448,256]{1,0:T(8,128)(2,1)S(1)}, bf16[448,256]{1,0:T(8,128)(2,1)S(1)}, u32[]{:S(2)}, u32[]{:S(2)}) collective-permute-start(bf16[448,256]{1,0:T(8,128)(2,1)S(1)} %get-tuple-element.25), channel_id=1, source_target_pairs={{0,8},{16,0},{24,16},{8,24},{1,9},{17,1},{25,17},{9,25},{2,10},{18... | collective-permute-start | bytes 688136 | tf_op jit(solution)/shard_map/ppermute | solution.py:57
  66.1 0.9 convolution_convert_fusion.1
  67.0 0.8 maximum_bitcast_fusion
  67.7 1.2 %collective-permute-done.22 = bf16[416,256]{1,0:T(8,128)(2,1)S(1)} collective-permute-done((bf16[416,256]{1,0:T(8,128)(2,1)S(1)}, bf16[416,256]{1,0:T(8,128)(2,1)S(1)}, u32[]{:S(2)}, u32[]{:S(2)}) %collective-permute-start.22) | collective-permute-done | bytes 213024 | tf_op jit(solution)/shard_map/ppermute | solution.py:57
  69.0 0.9 collective-permute-start.23
  69.9 4.0 %collective-permute-done.24 = bf16[448,256]{1,0:T(8,128)(2,1)S(1)} collective-permute-done((bf16[448,256]{1,0:T(8,128)(2,1)S(1)}, bf16[448,256]{1,0:T(8,128)(2,1)S(1)}, u32[]{:S(2)}, u32[]{:S(2)}) %collective-permute-start.24) | collective-permute-done | bytes 229408 | tf_op jit(solution)/shard_map/ppermute | solution.py:57
  73.9 0.9 convolution_convert_fusion
  75.0 1.0 collective-permute-start.25
  76.6 1.6 %collective-permute-done.23 = bf16[416,256]{1,0:T(8,128)(2,1)S(1)} collective-permute-done((bf16[416,256]{1,0:T(8,128)(2,1)S(1)}, bf16[416,256]{1,0:T(8,128)(2,1)S(1)}, u32[]{:S(2)}, u32[]{:S(2)}) %collective-permute-start.23) | collective-permute-done | bytes 213024 | tf_op jit(solution)/shard_map/ppermute | solution.py:57
  78.2 4.9 %collective-permute-done.25 = bf16[448,256]{1,0:T(8,128)(2,1)S(1)} collective-permute-done((bf16[448,256]{1,0:T(8,128)(2,1)S(1)}, bf16[448,256]{1,0:T(8,128)(2,1)S(1)}, u32[]{:S(2)}, u32[]{:S(2)}) %collective-permute-start.25) | collective-permute-done | bytes 229408 | tf_op jit(solution)/shard_map/ppermute | solution.py:57
  83.6 0.9 convolution_convert_fusion.2
  84.7 1.2 %collective-permute-start.39 = (bf16[2,32,1280]{2,1,0:T(8,128)(2,1)S(1)}, bf16[2,32,1280]{2,1,0:T(8,128)(2,1)S(1)}, u32[]{:S(2)}, u32[]{:S(2)}) collective-permute-start(bf16[2,32,1280]{2,1,0:T(8,128)(2,1)S(1)} %get-tuple-element.20), channel_id=1, source_target_pairs={{0,2},{1,3},{2,0},{3,1},{4,6},{5,7},{6,4},{7,5},{8,10},{9,11},{10,... | collective-permute-start | bytes 491528 | tf_op jit(solution)/shard_map/ppermute | solution.py:53
  86.5 1.8 %collective-permute-start.41 = (bf16[2,32,1280]{2,1,0:T(8,128)(2,1)S(1)}, bf16[2,32,1280]{2,1,0:T(8,128)(2,1)S(1)}, u32[]{:S(2)}, u32[]{:S(2)}) collective-permute-start(bf16[2,32,1280]{2,1,0:T(8,128)(2,1)S(1)} %get-tuple-element.21), channel_id=1, source_target_pairs={{0,6},{1,7},{2,4},{3,5},{4,2},{5,3},{6,0},{7,1},{8,14},{9,15},{10,... | collective-permute-start | bytes 491528 | tf_op jit(solution)/shard_map/ppermute | solution.py:53
  88.4 3.5 %collective-permute-done.39 = bf16[2,32,1280]{2,1,0:T(8,128)(2,1)S(1)} collective-permute-done((bf16[2,32,1280]{2,1,0:T(8,128)(2,1)S(1)}, bf16[2,32,1280]{2,1,0:T(8,128)(2,1)S(1)}, u32[]{:S(2)}, u32[]{:S(2)}) %collective-permute-start.39) | collective-permute-done | bytes 163872 | tf_op jit(solution)/shard_map/ppermute | solution.py:53
  91.9 2.4 %collective-permute-done.40 = bf16[2,32,1280]{2,1,0:T(8,128)(2,1)S(1)} collective-permute-done((bf16[2,32,1280]{2,1,0:T(8,128)(2,1)S(1)}, bf16[2,32,1280]{2,1,0:T(8,128)(2,1)S(1)}, u32[]{:S(2)}, u32[]{:S(2)}) %collective-permute-start.40) | collective-permute-done | bytes 163872 | tf_op jit(solution)/shard_map/ppermute | solution.py:53
  94.3 2.8 %collective-permute-start.42 = (bf16[32,1280]{1,0:T(8,128)(2,1)S(1)}, bf16[32,1280]{1,0:T(8,128)(2,1)S(1)}, u32[]{:S(2)}, u32[]{:S(2)}) collective-permute-start(bf16[32,1280]{1,0:T(8,128)(2,1)S(1)} %slice_bitcast_fusion.1), channel_id=1, source_target_pairs={{0,16},{16,24},{24,8},{8,0},{1,17},{17,25},{25,9},{9,1},{2,18},{18... | collective-permute-start | bytes 245768 | tf_op jit(solution)/shard_map/ppermute | solution.py:57
  97.1 0.9 convolution_convert_fusion.3
  98.8 1.2 collective-permute-start.34
  99.9 1.8 %collective-permute-start.35 = (bf16[1,32,1280]{2,1,0:T(8,128)(2,1)S(1)}, bf16[1,32,1280]{2,1,0:T(8,128)(2,1)S(1)}, u32[]{:S(2)}, u32[]{:S(2)}) collective-permute-start(bf16[1,32,1280]{2,1,0:T(8,128)(2,1)S(1)} %get-tuple-element.30), channel_id=1, source_target_pairs={{0,6},{1,7},{2,4},{3,5},{4,2},{5,3},{6,0},{7,1},{8,14},{9,15},{10,... | collective-permute-start | bytes 245768 | tf_op jit(solution)/shard_map/ppermute | solution.py:53
  102.5 1.0 collective-permute-done.33
  103.5 0.9 collective-permute-start.29
  104.4 1.8 %collective-permute-start.30 = (bf16[1,32,1280]{2,1,0:T(8,128)(2,1)S(1)}, bf16[1,32,1280]{2,1,0:T(8,128)(2,1)S(1)}, u32[]{:S(2)}, u32[]{:S(2)}) collective-permute-start(bf16[1,32,1280]{2,1,0:T(8,128)(2,1)S(1)} %get-tuple-element.32), channel_id=1, source_target_pairs={{0,6},{1,7},{2,4},{3,5},{4,2},{5,3},{6,0},{7,1},{8,14},{9,15},{10,... | collective-permute-start | bytes 245768 | tf_op jit(solution)/shard_map/ppermute | solution.py:53
  106.3 1.9 %collective-permute-start.36 = (bf16[32,1280]{1,0:T(8,128)(2,1)S(1)}, bf16[32,1280]{1,0:T(8,128)(2,1)S(1)}, u32[]{:S(2)}, u32[]{:S(2)}) collective-permute-start(bf16[32,1280]{1,0:T(8,128)(2,1)S(1)} %fusion.76), channel_id=1, source_target_pairs={{0,24},{16,8},{24,0},{8,16},{1,25},{17,9},{25,1},{9,17},{2,26},{18... | collective-permute-start | bytes 245768 | tf_op jit(solution)/shard_map/ppermute | solution.py:57
  108.2 0.6 collective-permute-done.29
  108.8 0.9 collective-permute-done.30
  109.8 4.5 %convolution_multiply_fusion = f32[1280,864]{0,1:T(8,128)} fusion(bf16[256,1280]{1,0:T(8,128)(2,1)S(1)} %bitcast.254, bf16[256,1280]{1,0:T(8,128)(2,1)S(1)} %bitcast.251, bf16[256,1280]{1,0:T(8,128)(2,1)S(1)} %bitcast.248, bf16[256,1280]{1,0:T(8,128)(2,1)S(1)} %bitcast.245, bf16[448,256]{1,0:T(8,128)(2,1)S(1)} %get-tuple-element.25, ...), kind=kOutput, calls=%fused_computation | convolution fusion | flops 2285363200 | bytes 8814592 | tf_op jit(solution)/shard_map/dot_general | solution.py:31
  114.4 0.8 collective-permute-done.31
  115.2 0.7 pad_maximum_fusion.2
  (98 shorter events, 11.7 us)
Async XLA Ops:
  1.7 5.7 %collective-permute-start = (bf16[64,640]{1,0:T(8,128)(2,1)S(1)}, bf16[64,640]{1,0:T(8,128)(2,1)S(1)}, u32[]{:S(2)}, u32[]{:S(2)}) collective-permute-start(bf16[64,640]{1,0:T(8,128)(2,1)S(1)} %get-tuple-element.50), channel_id=1, source_target_pairs={{0,2},{1,3},{2,0},{3,1},{4,6},{5,7},{6,4},{7,5},{8,10},{9,11},{10,... | collective-permute-start | bytes 245768 | tf_op jit(solution)/shard_map/ppermute | solution.py:53
  4.7 5.3 %collective-permute-start.1 = (bf16[64,640]{1,0:T(8,128)(2,1)S(1)}, bf16[64,640]{1,0:T(8,128)(2,1)S(1)}, u32[]{:S(2)}, u32[]{:S(2)}) collective-permute-start(bf16[64,640]{1,0:T(8,128)(2,1)S(1)} %get-tuple-element.49), channel_id=1, source_target_pairs={{0,4},{1,5},{2,6},{3,7},{4,0},{5,1},{6,2},{7,3},{8,12},{9,13},{10,... | collective-permute-start | bytes 245768 | tf_op jit(solution)/shard_map/ppermute | solution.py:53
  6.2 5.3 %collective-permute-start.2 = (bf16[64,640]{1,0:T(8,128)(2,1)S(1)}, bf16[64,640]{1,0:T(8,128)(2,1)S(1)}, u32[]{:S(2)}, u32[]{:S(2)}) collective-permute-start(bf16[64,640]{1,0:T(8,128)(2,1)S(1)} %get-tuple-element.48), channel_id=1, source_target_pairs={{0,6},{1,7},{2,4},{3,5},{4,2},{5,3},{6,0},{7,1},{8,14},{9,15},{10,... | collective-permute-start | bytes 245768 | tf_op jit(solution)/shard_map/ppermute | solution.py:53
  11.6 16.5 %copy-start = (bf16[1280,864]{0,1:T(8,128)(2,1)S(1)}, bf16[1280,864]{0,1:T(8,128)(2,1)}, u32[]{:S(2)}) copy-start(bf16[1280,864]{0,1:T(8,128)(2,1)} %param.4) | copy-start | bytes 6635524
  11.7 4.8 %collective-permute-start.3 = (bf16[64,640]{1,0:T(8,128)(2,1)S(1)}, bf16[64,640]{1,0:T(8,128)(2,1)S(1)}, u32[]{:S(2)}, u32[]{:S(2)}) collective-permute-start(bf16[64,640]{1,0:T(8,128)(2,1)S(1)} %get-tuple-element.43), channel_id=1, source_target_pairs={{0,16},{16,24},{24,8},{8,0},{1,17},{17,25},{25,9},{9,1},{2,18},{18... | collective-permute-start | bytes 245768 | tf_op jit(solution)/shard_map/ppermute | solution.py:57
  14.3 6.3 %collective-permute-start.8 = (bf16[64,640]{1,0:T(8,128)(2,1)S(1)}, bf16[64,640]{1,0:T(8,128)(2,1)S(1)}, u32[]{:S(2)}, u32[]{:S(2)}) collective-permute-start(bf16[64,640]{1,0:T(8,128)(2,1)S(1)} %get-tuple-element.46), channel_id=1, source_target_pairs={{0,24},{16,8},{24,0},{8,16},{1,25},{17,9},{25,1},{9,17},{2,26},{18... | collective-permute-start | bytes 245768 | tf_op jit(solution)/shard_map/ppermute | solution.py:57
  15.7 6.3 %collective-permute-start.9 = (bf16[64,640]{1,0:T(8,128)(2,1)S(1)}, bf16[64,640]{1,0:T(8,128)(2,1)S(1)}, u32[]{:S(2)}, u32[]{:S(2)}) collective-permute-start(bf16[64,640]{1,0:T(8,128)(2,1)S(1)} %get-tuple-element.45), channel_id=1, source_target_pairs={{0,8},{16,0},{24,16},{8,24},{1,9},{17,1},{25,17},{9,25},{2,10},{18... | collective-permute-start | bytes 245768 | tf_op jit(solution)/shard_map/ppermute | solution.py:57
  16.5 5.5 %collective-permute-start.4 = (bf16[1,64,640]{2,1,0:T(8,128)(2,1)S(1)}, bf16[1,64,640]{2,1,0:T(8,128)(2,1)S(1)}, u32[]{:S(2)}, u32[]{:S(2)}) collective-permute-start(bf16[1,64,640]{2,1,0:T(8,128)(2,1)S(1)} %bitcast.265), channel_id=1, source_target_pairs={{0,2},{1,3},{2,0},{3,1},{4,6},{5,7},{6,4},{7,5},{8,10},{9,11},{10,... | collective-permute-start | bytes 245768 | tf_op jit(solution)/shard_map/ppermute | solution.py:53
  17.4 6.3 %collective-permute-start.5 = (bf16[1,64,640]{2,1,0:T(8,128)(2,1)S(1)}, bf16[1,64,640]{2,1,0:T(8,128)(2,1)S(1)}, u32[]{:S(2)}, u32[]{:S(2)}) collective-permute-start(bf16[1,64,640]{2,1,0:T(8,128)(2,1)S(1)} %bitcast.266), channel_id=1, source_target_pairs={{0,4},{1,5},{2,6},{3,7},{4,0},{5,1},{6,2},{7,3},{8,12},{9,13},{10,... | collective-permute-start | bytes 245768 | tf_op jit(solution)/shard_map/ppermute | solution.py:53
  18.1 7.7 %collective-permute-start.6 = (bf16[1,64,640]{2,1,0:T(8,128)(2,1)S(1)}, bf16[1,64,640]{2,1,0:T(8,128)(2,1)S(1)}, u32[]{:S(2)}, u32[]{:S(2)}) collective-permute-start(bf16[1,64,640]{2,1,0:T(8,128)(2,1)S(1)} %bitcast.267), channel_id=1, source_target_pairs={{0,6},{1,7},{2,4},{3,5},{4,2},{5,3},{6,0},{7,1},{8,14},{9,15},{10,... | collective-permute-start | bytes 245768 | tf_op jit(solution)/shard_map/ppermute | solution.py:53
  22.0 15.1 %collective-permute-start.13 = (bf16[3,64,640]{2,1,0:T(8,128)(2,1)S(1)}, bf16[3,64,640]{2,1,0:T(8,128)(2,1)S(1)}, u32[]{:S(2)}, u32[]{:S(2)}) collective-permute-start(bf16[3,64,640]{2,1,0:T(8,128)(2,1)S(1)} %pad_maximum_fusion.3), channel_id=1, source_target_pairs={{0,1},{1,0},{2,3},{3,2},{4,5},{5,4},{6,7},{7,6},{8,9},{9,8},{10,11... | collective-permute-start | bytes 737288 | tf_op jit(solution)/shard_map/ppermute | solution.py:53
  22.1 10.9 %collective-permute-start.10 = (bf16[3,64,640]{2,1,0:T(8,128)(2,1)S(1)}, bf16[3,64,640]{2,1,0:T(8,128)(2,1)S(1)}, u32[]{:S(2)}, u32[]{:S(2)}) collective-permute-start(bf16[3,64,640]{2,1,0:T(8,128)(2,1)S(1)} %pad_maximum_fusion.3), channel_id=1, source_target_pairs={{0,2},{1,3},{2,0},{3,1},{4,6},{5,7},{6,4},{7,5},{8,10},{9,11},{10,... | collective-permute-start | bytes 737288 | tf_op jit(solution)/shard_map/ppermute | solution.py:53
  23.1 13.3 %collective-permute-start.11 = (bf16[3,64,640]{2,1,0:T(8,128)(2,1)S(1)}, bf16[3,64,640]{2,1,0:T(8,128)(2,1)S(1)}, u32[]{:S(2)}, u32[]{:S(2)}) collective-permute-start(bf16[3,64,640]{2,1,0:T(8,128)(2,1)S(1)} %pad_maximum_fusion.3), channel_id=1, source_target_pairs={{0,4},{1,5},{2,6},{3,7},{4,0},{5,1},{6,2},{7,3},{8,12},{9,13},{10,... | collective-permute-start | bytes 737288 | tf_op jit(solution)/shard_map/ppermute | solution.py:53
  23.8 12.7 %collective-permute-start.12 = (bf16[3,64,640]{2,1,0:T(8,128)(2,1)S(1)}, bf16[3,64,640]{2,1,0:T(8,128)(2,1)S(1)}, u32[]{:S(2)}, u32[]{:S(2)}) collective-permute-start(bf16[3,64,640]{2,1,0:T(8,128)(2,1)S(1)} %pad_maximum_fusion.3), channel_id=1, source_target_pairs={{0,6},{1,7},{2,4},{3,5},{4,2},{5,3},{6,0},{7,1},{8,14},{9,15},{10,... | collective-permute-start | bytes 737288 | tf_op jit(solution)/shard_map/ppermute | solution.py:53
  29.2 10.7 %collective-permute-start.7 = (bf16[416,256]{1,0:T(8,128)(2,1)S(1)}, bf16[416,256]{1,0:T(8,128)(2,1)S(1)}, u32[]{:S(2)}, u32[]{:S(2)}) collective-permute-start(bf16[416,256]{1,0:T(8,128)(2,1)S(1)} %fusion.19), channel_id=1, source_target_pairs={{0,16},{16,24},{24,8},{8,0},{1,17},{17,25},{25,9},{9,1},{2,18},{18... | collective-permute-start | bytes 638984 | tf_op jit(solution)/shard_map/ppermute | solution.py:57
  33.0 12.3 %collective-permute-start.19 = (bf16[448,256]{1,0:T(8,128)(2,1)S(1)}, bf16[448,256]{1,0:T(8,128)(2,1)S(1)}, u32[]{:S(2)}, u32[]{:S(2)}) collective-permute-start(bf16[448,256]{1,0:T(8,128)(2,1)S(1)} %fusion.18), channel_id=1, source_target_pairs={{0,16},{16,24},{24,8},{8,0},{1,17},{17,25},{25,9},{9,1},{2,18},{18... | collective-permute-start | bytes 688136 | tf_op jit(solution)/shard_map/ppermute | solution.py:57
  36.4 1.5 %collective-permute-start.14 = (bf16[3,64,640]{2,1,0:T(8,128)(2,1)S(1)}, bf16[3,64,640]{2,1,0:T(8,128)(2,1)S(1)}, u32[]{:S(2)}, u32[]{:S(2)}) collective-permute-start(bf16[3,64,640]{2,1,0:T(8,128)(2,1)S(1)} %collective-permute-done.10), channel_id=1, source_target_pairs={{0,1},{1,0},{2,3},{3,2},{4,5},{5,4},{6,7},{7,6},{8,9},{9,8},{10,11... | collective-permute-start | bytes 737288 | tf_op jit(solution)/shard_map/ppermute | solution.py:53
  36.5 1.8 %collective-permute-start.15 = (bf16[3,64,640]{2,1,0:T(8,128)(2,1)S(1)}, bf16[3,64,640]{2,1,0:T(8,128)(2,1)S(1)}, u32[]{:S(2)}, u32[]{:S(2)}) collective-permute-start(bf16[3,64,640]{2,1,0:T(8,128)(2,1)S(1)} %collective-permute-done.11), channel_id=1, source_target_pairs={{0,1},{1,0},{2,3},{3,2},{4,5},{5,4},{6,7},{7,6},{8,9},{9,8},{10,11... | collective-permute-start | bytes 737288 | tf_op jit(solution)/shard_map/ppermute | solution.py:53
  37.1 1.6 %collective-permute-start.16 = (bf16[3,64,640]{2,1,0:T(8,128)(2,1)S(1)}, bf16[3,64,640]{2,1,0:T(8,128)(2,1)S(1)}, u32[]{:S(2)}, u32[]{:S(2)}) collective-permute-start(bf16[3,64,640]{2,1,0:T(8,128)(2,1)S(1)} %collective-permute-done.12), channel_id=1, source_target_pairs={{0,1},{1,0},{2,3},{3,2},{4,5},{5,4},{6,7},{7,6},{8,9},{9,8},{10,11... | collective-permute-start | bytes 737288 | tf_op jit(solution)/shard_map/ppermute | solution.py:53
  40.4 7.9 %collective-permute-start.17 = (bf16[416,256]{1,0:T(8,128)(2,1)S(1)}, bf16[416,256]{1,0:T(8,128)(2,1)S(1)}, u32[]{:S(2)}, u32[]{:S(2)}) collective-permute-start(bf16[416,256]{1,0:T(8,128)(2,1)S(1)} %add_convert_fusion.3), channel_id=1, source_target_pairs={{0,16},{16,24},{24,8},{8,0},{1,17},{17,25},{25,9},{9,1},{2,18},{18... | collective-permute-start | bytes 638984 | tf_op jit(solution)/shard_map/ppermute | solution.py:57
  45.8 8.5 %collective-permute-start.20 = (bf16[448,256]{1,0:T(8,128)(2,1)S(1)}, bf16[448,256]{1,0:T(8,128)(2,1)S(1)}, u32[]{:S(2)}, u32[]{:S(2)}) collective-permute-start(bf16[448,256]{1,0:T(8,128)(2,1)S(1)} %add_convert_fusion.1), channel_id=1, source_target_pairs={{0,16},{16,24},{24,8},{8,0},{1,17},{17,25},{25,9},{9,1},{2,18},{18... | collective-permute-start | bytes 688136 | tf_op jit(solution)/shard_map/ppermute | solution.py:57
  47.0 11.9 %copy-start.1 = (bf16[256,864]{0,1:T(8,128)(2,1)S(1)}, bf16[256,864]{0,1:T(8,128)(2,1)}, u32[]{:S(2)}) copy-start(bf16[256,864]{0,1:T(8,128)(2,1)} %param.5) | copy-start | bytes 1327108
  48.4 10.5 %collective-permute-start.18 = (bf16[416,256]{1,0:T(8,128)(2,1)S(1)}, bf16[416,256]{1,0:T(8,128)(2,1)S(1)}, u32[]{:S(2)}, u32[]{:S(2)}) collective-permute-start(bf16[416,256]{1,0:T(8,128)(2,1)S(1)} %add_convert_fusion.2), channel_id=1, source_target_pairs={{0,16},{16,24},{24,8},{8,0},{1,17},{17,25},{25,9},{9,1},{2,18},{18... | collective-permute-start | bytes 638984 | tf_op jit(solution)/shard_map/ppermute | solution.py:57
  54.4 8.5 %collective-permute-start.21 = (bf16[448,256]{1,0:T(8,128)(2,1)S(1)}, bf16[448,256]{1,0:T(8,128)(2,1)S(1)}, u32[]{:S(2)}, u32[]{:S(2)}) collective-permute-start(bf16[448,256]{1,0:T(8,128)(2,1)S(1)} %add_convert_fusion), channel_id=1, source_target_pairs={{0,16},{16,24},{24,8},{8,0},{1,17},{17,25},{25,9},{9,1},{2,18},{18... | collective-permute-start | bytes 688136 | tf_op jit(solution)/shard_map/ppermute | solution.py:57
  59.3 9.6 %collective-permute-start.22 = (bf16[416,256]{1,0:T(8,128)(2,1)S(1)}, bf16[416,256]{1,0:T(8,128)(2,1)S(1)}, u32[]{:S(2)}, u32[]{:S(2)}) collective-permute-start(bf16[416,256]{1,0:T(8,128)(2,1)S(1)} %get-tuple-element.37), channel_id=1, source_target_pairs={{0,8},{16,0},{24,16},{8,24},{1,9},{17,1},{25,17},{9,25},{2,10},{18... | collective-permute-start | bytes 638984 | tf_op jit(solution)/shard_map/ppermute | solution.py:57
  63.4 10.5 %collective-permute-start.24 = (bf16[448,256]{1,0:T(8,128)(2,1)S(1)}, bf16[448,256]{1,0:T(8,128)(2,1)S(1)}, u32[]{:S(2)}, u32[]{:S(2)}) collective-permute-start(bf16[448,256]{1,0:T(8,128)(2,1)S(1)} %get-tuple-element.25), channel_id=1, source_target_pairs={{0,8},{16,0},{24,16},{8,24},{1,9},{17,1},{25,17},{9,25},{2,10},{18... | collective-permute-start | bytes 688136 | tf_op jit(solution)/shard_map/ppermute | solution.py:57
  69.0 9.2 %collective-permute-start.23 = (bf16[416,256]{1,0:T(8,128)(2,1)S(1)}, bf16[416,256]{1,0:T(8,128)(2,1)S(1)}, u32[]{:S(2)}, u32[]{:S(2)}) collective-permute-start(bf16[416,256]{1,0:T(8,128)(2,1)S(1)} %collective-permute-done.22), channel_id=1, source_target_pairs={{0,8},{16,0},{24,16},{8,24},{1,9},{17,1},{25,17},{9,25},{2,10},{18... | collective-permute-start | bytes 638984 | tf_op jit(solution)/shard_map/ppermute | solution.py:57
  75.0 8.2 %collective-permute-start.25 = (bf16[448,256]{1,0:T(8,128)(2,1)S(1)}, bf16[448,256]{1,0:T(8,128)(2,1)S(1)}, u32[]{:S(2)}, u32[]{:S(2)}) collective-permute-start(bf16[448,256]{1,0:T(8,128)(2,1)S(1)} %collective-permute-done.24), channel_id=1, source_target_pairs={{0,8},{16,0},{24,16},{8,24},{1,9},{17,1},{25,17},{9,25},{2,10},{18... | collective-permute-start | bytes 688136 | tf_op jit(solution)/shard_map/ppermute | solution.py:57
  76.0 8.5 %collective-permute-start.37 = (bf16[2,2,32,1280]{3,2,0,1:T(8,128)(2,1)S(1)}, bf16[2,2,32,1280]{3,2,0,1:T(8,128)(2,1)S(1)}, u32[]{:S(2)}, u32[]{:S(2)}) collective-permute-start(bf16[2,2,32,1280]{3,2,0,1:T(8,128)(2,1)S(1)} %get-tuple-element.27), channel_id=1, source_target_pairs={{0,1},{1,0},{2,3},{3,2},{4,5},{5,4},{6,7},{7,6},{8,9},{9,8},{10,11... | collective-permute-start | bytes 983048 | tf_op jit(solution)/shard_map/ppermute | solution.py:53
  76.1 8.4 %collective-permute-start.38 = (bf16[2,2,32,1280]{3,2,0,1:T(8,128)(2,1)S(1)}, bf16[2,2,32,1280]{3,2,0,1:T(8,128)(2,1)S(1)}, u32[]{:S(2)}, u32[]{:S(2)}) collective-permute-start(bf16[2,2,32,1280]{3,2,0,1:T(8,128)(2,1)S(1)} %get-tuple-element.28), channel_id=1, source_target_pairs={{0,1},{1,0},{2,3},{3,2},{4,5},{5,4},{6,7},{7,6},{8,9},{9,8},{10,11... | collective-permute-start | bytes 983048 | tf_op jit(solution)/shard_map/ppermute | solution.py:53
  83.1 14.0 %collective-permute-start.26 = (bf16[864,256]{1,0:T(8,128)(2,1)S(1)}, bf16[864,256]{1,0:T(8,128)(2,1)S(1)}, u32[]{:S(2)}, u32[]{:S(2)}) collective-permute-start(bf16[864,256]{1,0:T(8,128)(2,1)S(1)} %constant_dynamic-update-slice_fusion), channel_id=1, source_target_pairs={{0,8},{16,0},{24,16},{8,24},{1,9},{17,1},{25,17},{9,25},{2,10},{18... | collective-permute-start | bytes 1327112 | tf_op jit(solution)/shard_map/ppermute | solution.py:57
  84.7 7.1 %collective-permute-start.39 = (bf16[2,32,1280]{2,1,0:T(8,128)(2,1)S(1)}, bf16[2,32,1280]{2,1,0:T(8,128)(2,1)S(1)}, u32[]{:S(2)}, u32[]{:S(2)}) collective-permute-start(bf16[2,32,1280]{2,1,0:T(8,128)(2,1)S(1)} %get-tuple-element.20), channel_id=1, source_target_pairs={{0,2},{1,3},{2,0},{3,1},{4,6},{5,7},{6,4},{7,5},{8,10},{9,11},{10,... | collective-permute-start | bytes 491528 | tf_op jit(solution)/shard_map/ppermute | solution.py:53
  85.9 8.3 %collective-permute-start.40 = (bf16[2,32,1280]{2,1,0:T(8,128)(2,1)S(1)}, bf16[2,32,1280]{2,1,0:T(8,128)(2,1)S(1)}, u32[]{:S(2)}, u32[]{:S(2)}) collective-permute-start(bf16[2,32,1280]{2,1,0:T(8,128)(2,1)S(1)} %get-tuple-element.22), channel_id=1, source_target_pairs={{0,4},{1,5},{2,6},{3,7},{4,0},{5,1},{6,2},{7,3},{8,12},{9,13},{10,... | collective-permute-start | bytes 491528 | tf_op jit(solution)/shard_map/ppermute | solution.py:53
  86.5 7.8 %collective-permute-start.41 = (bf16[2,32,1280]{2,1,0:T(8,128)(2,1)S(1)}, bf16[2,32,1280]{2,1,0:T(8,128)(2,1)S(1)}, u32[]{:S(2)}, u32[]{:S(2)}) collective-permute-start(bf16[2,32,1280]{2,1,0:T(8,128)(2,1)S(1)} %get-tuple-element.21), channel_id=1, source_target_pairs={{0,6},{1,7},{2,4},{3,5},{4,2},{5,3},{6,0},{7,1},{8,14},{9,15},{10,... | collective-permute-start | bytes 491528 | tf_op jit(solution)/shard_map/ppermute | solution.py:53
  88.3 9.8 %collective-permute-start.32 = (bf16[1,4,32,1280]{3,2,1,0:T(8,128)(2,1)S(1)}, bf16[1,4,32,1280]{3,2,1,0:T(8,128)(2,1)S(1)}, u32[]{:S(2)}, u32[]{:S(2)}) collective-permute-start(bf16[1,4,32,1280]{3,2,1,0:T(8,128)(2,1)S(1)} %dynamic-slice_bitcast_fusion), channel_id=1, source_target_pairs={{0,1},{1,0},{2,3},{3,2},{4,5},{5,4},{6,7},{7,6},{8,9},{9,8},{10,11... | collective-permute-start | bytes 983048 | tf_op jit(solution)/shard_map/ppermute | solution.py:53
  94.3 20.0 %collective-permute-start.42 = (bf16[32,1280]{1,0:T(8,128)(2,1)S(1)}, bf16[32,1280]{1,0:T(8,128)(2,1)S(1)}, u32[]{:S(2)}, u32[]{:S(2)}) collective-permute-start(bf16[32,1280]{1,0:T(8,128)(2,1)S(1)} %slice_bitcast_fusion.1), channel_id=1, source_target_pairs={{0,16},{16,24},{24,8},{8,0},{1,17},{17,25},{25,9},{9,1},{2,18},{18... | collective-permute-start | bytes 245768 | tf_op jit(solution)/shard_map/ppermute | solution.py:57
  98.0 3.8 %collective-permute-start.27 = (bf16[1,4,32,1280]{3,2,1,0:T(8,128)(2,1)S(1)}, bf16[1,4,32,1280]{3,2,1,0:T(8,128)(2,1)S(1)}, u32[]{:S(2)}, u32[]{:S(2)}) collective-permute-start(bf16[1,4,32,1280]{3,2,1,0:T(8,128)(2,1)S(1)} %dynamic-slice_bitcast_fusion.1), channel_id=1, source_target_pairs={{0,1},{1,0},{2,3},{3,2},{4,5},{5,4},{6,7},{7,6},{8,9},{9,8},{10,11... | collective-permute-start | bytes 983048 | tf_op jit(solution)/shard_map/ppermute | solution.py:53
  98.2 5.3 %collective-permute-start.33 = (bf16[1,32,1280]{2,1,0:T(8,128)(2,1)S(1)}, bf16[1,32,1280]{2,1,0:T(8,128)(2,1)S(1)}, u32[]{:S(2)}, u32[]{:S(2)}) collective-permute-start(bf16[1,32,1280]{2,1,0:T(8,128)(2,1)S(1)} %get-tuple-element.29), channel_id=1, source_target_pairs={{0,2},{1,3},{2,0},{3,1},{4,6},{5,7},{6,4},{7,5},{8,10},{9,11},{10,... | collective-permute-start | bytes 245768 | tf_op jit(solution)/shard_map/ppermute | solution.py:53
  98.8 5.6 %collective-permute-start.34 = (bf16[1,32,1280]{2,1,0:T(8,128)(2,1)S(1)}, bf16[1,32,1280]{2,1,0:T(8,128)(2,1)S(1)}, u32[]{:S(2)}, u32[]{:S(2)}) collective-permute-start(bf16[1,32,1280]{2,1,0:T(8,128)(2,1)S(1)} %get-tuple-element.31), channel_id=1, source_target_pairs={{0,4},{1,5},{2,6},{3,7},{4,0},{5,1},{6,2},{7,3},{8,12},{9,13},{10,... | collective-permute-start | bytes 245768 | tf_op jit(solution)/shard_map/ppermute | solution.py:53
  99.9 6.3 %collective-permute-start.35 = (bf16[1,32,1280]{2,1,0:T(8,128)(2,1)S(1)}, bf16[1,32,1280]{2,1,0:T(8,128)(2,1)S(1)}, u32[]{:S(2)}, u32[]{:S(2)}) collective-permute-start(bf16[1,32,1280]{2,1,0:T(8,128)(2,1)S(1)} %get-tuple-element.30), channel_id=1, source_target_pairs={{0,6},{1,7},{2,4},{3,5},{4,2},{5,3},{6,0},{7,1},{8,14},{9,15},{10,... | collective-permute-start | bytes 245768 | tf_op jit(solution)/shard_map/ppermute | solution.py:53
  101.9 6.3 %collective-permute-start.28 = (bf16[1,32,1280]{2,1,0:T(8,128)(2,1)S(1)}, bf16[1,32,1280]{2,1,0:T(8,128)(2,1)S(1)}, u32[]{:S(2)}, u32[]{:S(2)}) collective-permute-start(bf16[1,32,1280]{2,1,0:T(8,128)(2,1)S(1)} %get-tuple-element.34), channel_id=1, source_target_pairs={{0,2},{1,3},{2,0},{3,1},{4,6},{5,7},{6,4},{7,5},{8,10},{9,11},{10,... | collective-permute-start | bytes 245768 | tf_op jit(solution)/shard_map/ppermute | solution.py:53
  103.5 5.3 %collective-permute-start.29 = (bf16[1,32,1280]{2,1,0:T(8,128)(2,1)S(1)}, bf16[1,32,1280]{2,1,0:T(8,128)(2,1)S(1)}, u32[]{:S(2)}, u32[]{:S(2)}) collective-permute-start(bf16[1,32,1280]{2,1,0:T(8,128)(2,1)S(1)} %get-tuple-element.33), channel_id=1, source_target_pairs={{0,4},{1,5},{2,6},{3,7},{4,0},{5,1},{6,2},{7,3},{8,12},{9,13},{10,... | collective-permute-start | bytes 245768 | tf_op jit(solution)/shard_map/ppermute | solution.py:53
  104.4 5.3 %collective-permute-start.30 = (bf16[1,32,1280]{2,1,0:T(8,128)(2,1)S(1)}, bf16[1,32,1280]{2,1,0:T(8,128)(2,1)S(1)}, u32[]{:S(2)}, u32[]{:S(2)}) collective-permute-start(bf16[1,32,1280]{2,1,0:T(8,128)(2,1)S(1)} %get-tuple-element.32), channel_id=1, source_target_pairs={{0,6},{1,7},{2,4},{3,5},{4,2},{5,3},{6,0},{7,1},{8,14},{9,15},{10,... | collective-permute-start | bytes 245768 | tf_op jit(solution)/shard_map/ppermute | solution.py:53
  106.3 8.1 %collective-permute-start.36 = (bf16[32,1280]{1,0:T(8,128)(2,1)S(1)}, bf16[32,1280]{1,0:T(8,128)(2,1)S(1)}, u32[]{:S(2)}, u32[]{:S(2)}) collective-permute-start(bf16[32,1280]{1,0:T(8,128)(2,1)S(1)} %fusion.76), channel_id=1, source_target_pairs={{0,24},{16,8},{24,0},{8,16},{1,25},{17,9},{25,1},{9,17},{2,26},{18... | collective-permute-start | bytes 245768 | tf_op jit(solution)/shard_map/ppermute | solution.py:57
  109.8 5.4 %collective-permute-start.31 = (bf16[32,1280]{1,0:T(8,128)(2,1)S(1)}, bf16[32,1280]{1,0:T(8,128)(2,1)S(1)}, u32[]{:S(2)}, u32[]{:S(2)}) collective-permute-start(bf16[32,1280]{1,0:T(8,128)(2,1)S(1)} %fusion.75), channel_id=1, source_target_pairs={{0,8},{16,0},{24,16},{8,24},{1,9},{17,1},{25,17},{9,25},{2,10},{18... | collective-permute-start | bytes 245768 | tf_op jit(solution)/shard_map/ppermute | solution.py:57
